TPU v7x, 32 devices: a whole 2x2x4 slice. The times are simulated.
32 devices in a mesh: grp: 8 (over y, x, core), dp: 4 (over z).
Axes of the slice: x: 2, y: 2, z: 4, core: 2. Of those that a mesh axis runs over, the one named last changes fastest.
Arguments:
- tokens: bfloat16 [192, 197, 384], P(('grp', 'dp')), may hold values from -6 to 6
- kinds: int32 [192], P(('grp', 'dp')), may hold values from 0 to 2
- interp: float32 [3, 197, 197], replicated, may hold values from -0.4375 to 0.4375
- pos_base: bfloat16 [197, 384], replicated, may hold values from -5 to 5
- ln_gain: bfloat16 [2, 2, 384], replicated, may hold values from 0.5 to 1.5
- ln_bias: bfloat16 [2, 2, 384], replicated, may hold values from -2 to 2
- w_qkv: bfloat16 [2, 384, 1152], replicated, may hold values from -0.3125 to 0.3125
- qv_bias: bfloat16 [2, 2, 384], replicated, may hold values from -2 to 2
- w_out: bfloat16 [2, 384, 384], replicated, may hold values from -1.25 to 1.25
- out_bias: bfloat16 [2, 384], replicated, may hold values from -2 to 2
- w_fc1: bfloat16 [2, 384, 1536], replicated, may hold values from -0.3125 to 0.3125
- fc1_bias: bfloat16 [2, 1536], replicated, may hold values from -2 to 2
- w_fc2: bfloat16 [2, 1536, 384], replicated, may hold values from -0.15625 to 0.15625
- fc2_bias: bfloat16 [2, 384], replicated, may hold values from -2 to 2
- cotangent: bfloat16 [192, 197, 384], P(('grp', 'dp')), may hold values from -6 to 6
Outputs:
- mixed: bfloat16 [192, 197, 384], P(('grp', 'dp'))
- grad_tokens: float32 [192, 197, 384], P(('grp', 'dp'))
- grad_pos: float32 [197, 384], replicated
- grad_ln_gain: float32 [2, 2, 384], replicated
- grad_ln_bias: float32 [2, 2, 384], replicated
- grad_w_qkv: float32 [2, 384, 1152], replicated
- grad_qv_bias: float32 [2, 2, 384], replicated
- grad_w_out: float32 [2, 384, 384], replicated
- grad_out_bias: float32 [2, 384], replicated
- grad_w_fc1: float32 [2, 384, 1536], replicated
- grad_fc1_bias: float32 [2, 1536], replicated
- grad_w_fc2: float32 [2, 1536, 384], replicated
- grad_fc2_bias: float32 [2, 384], replicated
All inputs are finite; a program needn't handle non-finite values.
Results may differ from a plain program's by a relative error of at most 0.0085.
Values sent between devices are 32-bit elements; how exact they have to be, the bound alone decides.
No kernel may reach another device: no remote copies, remote signals or barrier semaphores. Data moves between devices by JAX's collectives and lax.ppermute only.
A program may use at most 192 MiB of HBM per device.

v0:
```python
from functools import partial

import jax
import jax.numpy as jnp
from jax import lax
from jax.experimental import pallas as pl
from jax.experimental.pallas import tpu as pltpu
from jax.sharding import PartitionSpec as P

HEADS = 6
HEAD = 64
BASE = 197
CROP_B = 181
CROP_C = 193
EPS = 1e-06
F32 = jnp.float32
BF16 = jnp.bfloat16
VMEM_LIMIT = 60 * 1024 * 1024

ERF_P = 0.39
ERF_C = (0.11766263, 0.04569411, 0.32477995, -0.31770045, 0.44333237, -0.11376861)


def dot(a, b):
    return lax.dot_general(a, b, (((1,), (0,)), ((), ())), preferred_element_type=F32)


def dot_bt(a, b):
    return lax.dot_general(a, b, (((1,), (1,)), ((), ())), preferred_element_type=F32)


def dot_at(a, b):
    return lax.dot_general(a, b, (((0,), (0,)), ((), ())), preferred_element_type=F32)


def split3(x):
    hi = x.astype(BF16)
    rest = x - hi.astype(F32)
    mid = rest.astype(BF16)
    low = (rest - mid.astype(F32)).astype(BF16)
    return hi, mid, low


def length_of(kind):
    return jnp.where(kind == 0, BASE, jnp.where(kind == 1, CROP_B, CROP_C)).astype(jnp.int32)


def pick(ref, layer):
    row = ref[0:1].astype(F32)
    for index in range(1, ref.shape[0]):
        row = jnp.where(layer == index, ref[index : index + 1].astype(F32), row)
    return row


def norm(x):
    width = x.shape[-1]
    mean = jnp.sum(x, -1, keepdims=True) * (1.0 / width)
    centered = x - mean
    var = jnp.sum(centered * centered, -1, keepdims=True) * (1.0 / width)
    rstd = lax.rsqrt(var + EPS)
    return centered * rstd, rstd


def norm_back(dc, xhat, rstd, gain):
    width = dc.shape[-1]
    dxh = dc * gain
    m1 = jnp.sum(dxh, -1, keepdims=True) * (1.0 / width)
    m2 = jnp.sum(dxh * xhat, -1, keepdims=True) * (1.0 / width)
    return rstd * (dxh - m1 - xhat * m2)


def gelu_parts(x):
    phi = 0.5 + 0.5 * lax.erf(x * 0.5**0.5)
    return x * phi, phi + x * (jnp.exp2(x * x * (-0.5 * 1.4426950408889634)) * 0.3989422804014327)


def head_masks():
    first = lax.broadcasted_iota(jnp.int32, (1, 2 * HEAD), 1) < HEAD
    plain = [jnp.where(first, 1.0, 0.0), jnp.where(first, 0.0, 1.0)]
    return [x.astype(BF16) for x in plain], [(x * HEAD**-0.5).astype(BF16) for x in plain]


def fwd_kernel(
    kinds, tok, interp, pos, gain, bias, w_qkv, qvb, w_out, outb, w1, b1, w2, b2,
    mixed, a_o, qkv_o, lse_o, o_o, c_o, gp_o, gh_o, xh1_o, r1_o, xh2_o, r2_o,
    x_all, table_s, mid_s, o_s,
):
    layer, block = pl.program_id(0), pl.program_id(1)
    x_s = x_all.at[block]
    images, rows, width = tok.shape
    padded = x_all.shape[2]
    flat = images * padded
    heads_pair = 2 * HEAD

    @pl.when((block == 0) & (layer == 0))
    def _():
        for kind in range(interp.shape[0]):
            total = jnp.zeros((rows, width), F32)
            for part in split3(interp[kind])[::-1]:
                total += dot(part, pos[...])
            table_s[kind, 0:rows, :] = total

    @pl.when(layer == 0)
    def _():
        for i in range(images):
            kind = kinds[block * images + i]
            here = lax.broadcasted_iota(jnp.int32, (rows, 1), 0) < length_of(kind)
            h0 = tok[i].astype(F32) + table_s[kind, 0:rows, :]
            x_s[i] = jnp.zeros((padded, width), F32)
            x_s[i, 0:rows, :] = jnp.where(here, h0, 0.0)

    x = x_s[...].reshape(flat, width)
    xhat, rstd = norm(x)
    a = (xhat * gain[0, 0:1].astype(F32) + bias[0, 0:1].astype(F32)).astype(BF16)
    a_o[0] = a
    xh1_o[0] = xhat.astype(BF16)
    r1_o[0] = rstd
    bias_row = qvb[0].astype(F32)
    bias_row = jnp.concatenate([bias_row[0:1], jnp.zeros((1, width), F32), bias_row[1:2]], 1)
    qkv_o[0] = (dot(a, w_qkv[0]) + bias_row).astype(BF16)
    plain, scaled = head_masks()
    for i in range(images):
        r0 = i * padded
        length = length_of(kinds[block * images + i])
        key_ok = lax.broadcasted_iota(jnp.int32, (1, padded, 1), 1) < length
        for pair in range(HEADS // 2):
            c0 = pair * heads_pair
            q2 = qkv_o[0, r0 : r0 + padded, c0 : c0 + heads_pair]
            k2 = qkv_o[0, r0 : r0 + padded, width + c0 : width + c0 + heads_pair]
            v2 = qkv_o[0, r0 : r0 + padded, 2 * width + c0 : 2 * width + c0 + heads_pair]
            ks = jnp.concatenate([k2 * keep for keep in scaled], 0)
            vs = jnp.concatenate([v2 * keep for keep in plain], 0)
            s = jnp.where(key_ok, dot_bt(ks, q2).reshape(2, padded, padded), -1e9)
            top = jnp.max(s, 1, keepdims=True)
            e = jnp.exp(s - top)
            total = jnp.sum(e, 1, keepdims=True)
            lse_o[0, i, 2 * pair : 2 * pair + 2, :] = (top + jnp.log(total)).reshape(2, padded)
            p = (e * (1.0 / total)).astype(BF16).reshape(2 * padded, padded)
            o_s[r0 : r0 + padded, c0 : c0 + heads_pair] = dot_at(p, vs).astype(BF16)
    o = o_s[...]
    o_o[0] = o
    mid = x_s[...].reshape(flat, width) + dot(o, w_out[0]) + pick(outb, layer)
    mid_s[...] = mid
    xhat, rstd = norm(mid)
    c = (xhat * gain[0, 1:2].astype(F32) + bias[0, 1:2].astype(F32)).astype(BF16)
    c_o[0] = c
    xh2_o[0] = xhat.astype(BF16)
    r2_o[0] = rstd
    hidden = w1.shape[2]
    bias1 = pick(b1, layer)
    step = 256
    total = mid_s[...] + pick(b2, layer)
    for f in range(0, hidden, step):
        pre = dot(c, w1[0, :, f : f + step]) + bias1[:, f : f + step]
        gh, gp = gelu_parts(pre)
        gh = gh.astype(BF16)
        gh_o[0, :, f : f + step] = gh
        gp_o[0, :, f : f + step] = gp.astype(BF16)
        total += dot(gh, w2[0, f : f + step, :])
    x_s[...] = total.reshape(images, padded, width)

    @pl.when(layer == pl.num_programs(0) - 1)
    def _():
        for i in range(images):
            kind = kinds[block * images + i]
            here = lax.broadcasted_iota(jnp.int32, (rows, 1), 0) < length_of(kind)
            mixed[i] = jnp.where(here, x_s[i, 0:rows, :], 0.0).astype(BF16)


def forward(kinds, tokens, interp, pos_base, ln_gain, ln_bias, w_qkv, qv_bias, w_out, out_bias, w_fc1, fc1_bias, w_fc2, fc2_bias, padded, per):
    count, rows, width = tokens.shape
    layers, _, hidden = w_fc1.shape
    blocks = count // per
    flat = per * padded
    whole = lambda shape: pl.BlockSpec(shape, lambda l, b, k: (0,) * len(shape))
    by_layer = lambda shape: pl.BlockSpec((1,) + shape, lambda l, b, k: (l,) + (0,) * len(shape))
    read_image = pl.BlockSpec((per, rows, width), lambda l, b, k: (jnp.where(l == 0, b, blocks - 1), 0, 0))
    write_image = pl.BlockSpec((per, rows, width), lambda l, b, k: (jnp.where(l == layers - 1, b, 0), 0, 0))
    saved = lambda feat: pl.BlockSpec((1, flat, feat), lambda l, b, k: (l, b, 0))
    shape = lambda feat, dtype: jax.ShapeDtypeStruct((layers, count * padded, feat), dtype)
    return pl.pallas_call(
        fwd_kernel,
        grid_spec=pltpu.PrefetchScalarGridSpec(
            num_scalar_prefetch=1,
            grid=(layers, blocks),
            in_specs=[
                read_image,
                whole(interp.shape),
                whole(pos_base.shape),
                by_layer((2, width)),
                by_layer((2, width)),
                by_layer((width, 3 * width)),
                by_layer((2, width)),
                by_layer((width, width)),
                whole(out_bias.shape),
                by_layer((width, hidden)),
                whole(fc1_bias.shape),
                by_layer((hidden, width)),
                whole(fc2_bias.shape),
            ],
            out_specs=[
                write_image,
                saved(width),
                saved(3 * width),
                pl.BlockSpec((1, per, 8, padded), lambda l, b, k: (l, b, 0, 0)),
                saved(width),
                saved(width),
                saved(hidden),
                saved(hidden),
                saved(width),
                saved(1),
                saved(width),
                saved(1),
            ],
            scratch_shapes=[
                pltpu.VMEM((blocks, per, padded, width), F32),
                pltpu.VMEM((3, padded, width), F32),
                pltpu.VMEM((flat, width), F32),
                pltpu.VMEM((flat, width), BF16),
            ],
        ),
        out_shape=[
            jax.ShapeDtypeStruct(tokens.shape, BF16),
            shape(width, BF16),
            shape(3 * width, BF16),
            jax.ShapeDtypeStruct((layers, count, 8, padded), F32),
            shape(width, BF16),
            shape(width, BF16),
            shape(hidden, BF16),
            shape(hidden, BF16),
            shape(width, BF16),
            shape(1, F32),
            shape(width, BF16),
            shape(1, F32),
        ],
        compiler_params=pltpu.CompilerParams(vmem_limit_bytes=VMEM_LIMIT),
        name="encoder_forward",
    )(kinds, tokens, interp, pos_base, ln_gain, ln_bias, w_qkv, qv_bias, w_out, out_bias, w_fc1, fc1_bias, w_fc2, fc2_bias)


PIECES = 32
GROUP = 8


def xor(value, index):
    return lax.bitwise_xor(value, jnp.int32(index))


def copy_all(copies):
    for item in copies:
        item.start()
    for item in copies:
        item.wait()


def mlp_back_kernel(
    top, kinds, me, dx_ref, c, gh, gp, xh, rstd, gain, w1, w2,
    dmid, keep1, send1, keep2, send2, sums, dx_s, gw1, gw2, sems,
):
    block = pl.program_id(0)

    @pl.when(block == 0)
    def _():
        gw1[...] = jnp.zeros_like(gw1)
        gw2[...] = jnp.zeros_like(gw2)
        sums[...] = jnp.zeros_like(sums)

    if top:
        images, rows, width = dx_ref.shape
        padded = dx_s.shape[1]
        for i in range(images):
            kind = kinds[block * images + i]
            here = lax.broadcasted_iota(jnp.int32, (rows, 1), 0) < length_of(kind)
            dx_s[i] = jnp.zeros((padded, width), F32)
            dx_s[i, 0:rows, :] = jnp.where(here, dx_ref[i].astype(F32), 0.0)
        dx = dx_s[...].reshape(images * padded, width)
    else:
        dx = dx_ref[...]
    flat, width = dx.shape
    hidden = w1.shape[2]
    dz = dx.astype(BF16)
    sums[11:12, :] += jnp.sum(dz.astype(F32), 0, keepdims=True)
    dc = jnp.zeros((flat, width), F32)
    together = 4
    for index in range(0, hidden // width, together):
        cols = slice(index * width, (index + together) * width)
        dgh = dot_bt(dz, w2[0, cols, :])
        dpre = (dgh * gp[0, :, cols].astype(F32)).astype(BF16)
        column = jnp.sum(dpre.astype(F32), 0, keepdims=True)
        grad = dot_at(c[0], dpre)
        for k in range(together):
            here = slice(k * width, (k + 1) * width)
            sums[7 + index + k : 8 + index + k, :] += column[:, here]
            gw1[index + k] += grad[:, here]
        gw2[cols, :] += dot_at(gh[0, :, cols], dz)
        dc += dot_bt(dpre, w1[0, :, cols])
    xhat = xh[0].astype(F32)
    sums[1:2, :] += jnp.sum(dc * xhat, 0, keepdims=True)
    sums[3:4, :] += jnp.sum(dc, 0, keepdims=True)
    dmid[...] = dx + norm_back(dc, xhat, rstd[0], gain[0, 1:2].astype(F32))

    @pl.when(block == pl.num_programs(0) - 1)
    def _():
        piece = hidden // PIECES
        half = PIECES // 2
        copies = []
        for r in range(PIECES):
            first, second = xor(me[0], r), xor(me[1], r)
            out1, out2 = (keep1, keep2) if r < half else (send1, send2)
            row = pl.multiple_of(lax.bitwise_and(first, GROUP - 1) * piece, 8)
            col = lax.shift_right_logical(first, 3)
            copies.append(pltpu.make_async_copy(gw1.at[col, pl.ds(row, piece)], out1.at[r % half], sems.at[2 * r]))
            row = pl.multiple_of(second * piece, 8)
            copies.append(pltpu.make_async_copy(gw2.at[pl.ds(row, piece)], out2.at[r % half], sems.at[2 * r + 1]))
        copy_all(copies)


def halves(piece, width):
    return [jax.ShapeDtypeStruct((PIECES // 2, piece, width), F32)] * 2


def drop(kernel, fixed, first, count):
    def body(*refs):
        return kernel(*fixed, *refs[:first], *refs[first + count :])

    return body


def mlp_back(layer, top, kinds, me, dx, c, gh, gp, xh, rstd, gain, w1, w2, padded, per, after):
    layers, width, hidden = w1.shape
    total = c.shape[1]
    flat = per * padded
    blocks = total // flat
    saved = lambda feat: pl.BlockSpec((1, flat, feat), lambda b, k, m: (layer, b, 0))
    param = lambda *shape: pl.BlockSpec((1,) + shape, lambda b, k, m: (layer, 0, 0))
    if top:
        dx_spec = pl.BlockSpec((per,) + dx.shape[1:], lambda b, k, m: (b, 0, 0))
    else:
        dx_spec = pl.BlockSpec((flat, width), lambda b, k, m: (b, 0))
    anywhere = pl.BlockSpec(memory_space=pl.ANY)
    return pl.pallas_call(
        drop(mlp_back_kernel, (top,), 11, len(after)),
        grid_spec=pltpu.PrefetchScalarGridSpec(
            num_scalar_prefetch=2,
            grid=(blocks,),
            in_specs=[
                dx_spec,
                saved(width),
                saved(hidden),
                saved(hidden),
                saved(width),
                saved(1),
                param(2, width),
                param(width, hidden),
                param(hidden, width),
            ]
            + [anywhere] * len(after),
            out_specs=[
                pl.BlockSpec((flat, width), lambda b, k, m: (b, 0)),
                anywhere,
                anywhere,
                anywhere,
                anywhere,
                pl.BlockSpec((16, width), lambda b, k, m: (0, 0)),
            ],
            scratch_shapes=[
                pltpu.VMEM((per, padded, width), F32),
                pltpu.VMEM((hidden // width, width, width), F32),
                pltpu.VMEM((hidden, width), F32),
                pltpu.SemaphoreType.DMA((2 * PIECES,)),
            ],
        ),
        out_shape=[jax.ShapeDtypeStruct((total, width), F32)]
        + halves(hidden // PIECES, width)
        + halves(hidden // PIECES, width)
        + [jax.ShapeDtypeStruct((16, width), F32)],
        compiler_params=pltpu.CompilerParams(vmem_limit_bytes=VMEM_LIMIT),
        cost_estimate=pl.CostEstimate(flops=8 * total * width * hidden, bytes_accessed=30 * total * width, transcendentals=0),
        name="mlp_backward",
    )(kinds, me, dx, c, gh, gp, xh, rstd, gain, w1, w2, *after)


def attn_back_kernel(bottom, layers, kinds, me, dmid, o, qkv, lse, a, xh, rstd, gain, w_qkv, w_out, *rest):
    if bottom:
        interp, dx_ref, keep1, send1, keep2, send2, dqkv_s, do_s, gw, sems, sums, kind_s, misc = rest[:1] + rest[2 * layers :]
        others = rest[1 : 2 * layers]
    else:
        dx_ref, keep1, send1, keep2, send2, sums, dqkv_s, do_s, gw, sems = rest
    block = pl.program_id(0)
    images = lse.shape[1]
    flat, width = dmid.shape
    padded = flat // images

    @pl.when(block == 0)
    def _():
        gw[...] = jnp.zeros_like(gw)
        sums[...] = jnp.zeros_like(sums)
        if bottom:
            kind_s[...] = jnp.zeros_like(kind_s)

    dy = dmid[...].astype(BF16)
    sums[6:7, :] += jnp.sum(dy.astype(F32), 0, keepdims=True)
    do_s[...] = dot_bt(dy, w_out[0]).astype(BF16)
    gw[3] += dot_at(o[0], dy)
    pair_width = 2 * HEAD
    plain, scaled = head_masks()
    first = lax.broadcasted_iota(jnp.int32, (1, pair_width), 1) < HEAD
    for i in range(images):
        rows = slice(i * padded, (i + 1) * padded)
        length = length_of(kinds[block * images + i])
        key_ok = lax.broadcasted_iota(jnp.int32, (1, padded, 1), 1) < length
        for pair in range(HEADS // 2):
            c0 = pair * pair_width
            part = lambda base: slice(base + c0, base + c0 + pair_width)
            q2, k2, v2 = qkv[0, rows, part(0)], qkv[0, rows, part(width)], qkv[0, rows, part(2 * width)]
            do2 = do_s[rows, part(0)]
            ks = jnp.concatenate([k2 * keep for keep in scaled], 0)
            vs = jnp.concatenate([v2 * keep for keep in plain], 0)
            s = jnp.where(key_ok, dot_bt(ks, q2).reshape(2, padded, padded), -1e9)
            p = jnp.exp(s - lse[0, i, 2 * pair : 2 * pair + 2, :].reshape(2, 1, padded))
            dp = dot_bt(vs, do2).reshape(2, padded, padded)
            delta = jnp.sum(dp * p, 1, keepdims=True)
            ds = (p * (dp - delta)).astype(BF16).reshape(2 * padded, padded)
            dv = dot(p.astype(BF16).reshape(2 * padded, padded), do2)
            dk = dot(ds, q2)
            dqkv_s[rows, part(0)] = dot_at(ds, ks).astype(BF16)
            dqkv_s[rows, part(width)] = (jnp.where(first, dk[:padded], dk[padded:]) * HEAD**-0.5).astype(BF16)
            dqkv_s[rows, part(2 * width)] = jnp.where(first, dv[:padded], dv[padded:]).astype(BF16)
    d = dqkv_s[...]
    for index in (0, 2):
        row = 4 + index // 2
        sums[row : row + 1, :] += jnp.sum(d[:, index * width : (index + 1) * width].astype(F32), 0, keepdims=True)
    grad = dot_at(a[0], d)
    for index in range(3):
        gw[index] += grad[:, index * width : (index + 1) * width]
    da = dot_bt(d, w_qkv[0])
    xhat = xh[0].astype(F32)
    sums[0:1, :] += jnp.sum(da * xhat, 0, keepdims=True)
    sums[2:3, :] += jnp.sum(da, 0, keepdims=True)
    dx = dmid[...] + norm_back(da, xhat, rstd[0], gain[0, 0:1].astype(F32))
    if bottom:
        real = dx_ref.shape[1]
        for i in range(images):
            kind = kinds[block * images + i]
            here = lax.broadcasted_iota(jnp.int32, (padded, 1), 0) < length_of(kind)
            mine = jnp.where(here, dx[i * padded : (i + 1) * padded], 0.0)
            dx_ref[i] = mine[0:real]
            kind_s[kind] += mine
    else:
        dx_ref[...] = dx

    @pl.when(block == pl.num_programs(0) - 1)
    def _():
        half = PIECES // 2
        piece = gw.shape[0] * width // PIECES
        part = piece // 2
        copies = []
        for r in range(PIECES):
            for which, out in ((0, keep1 if r < half else send1), (1, keep2 if r < half else send2)):
                j = xor(me[which], r)
                row = pl.multiple_of(lax.bitwise_and(j, GROUP - 1) * piece + which * part, 8)
                col = lax.shift_right_logical(j, 3)
                copies.append(
                    pltpu.make_async_copy(
                        gw.at[col, pl.ds(row, part)], out.at[r % half, pl.ds(0, part)], sems.at[2 * r + which]
                    )
                )
        for item in copies:
            item.start()
        if bottom:
            total = jnp.zeros((real, width), F32)
            for kind in range(interp.shape[0]):
                hi, mid, _ = split3(interp[kind])
                ghi, gmid, _ = split3(kind_s[kind, 0:real, :])
                total += dot_at(mid, ghi) + dot_at(hi, gmid) + dot_at(hi, ghi)
            misc[...] = jnp.zeros_like(misc)
            misc[0:real, :] = total
            misc[200:216, :] = sums[...] + others[0][...]
            for layer in range(1, layers):
                misc[200 + 16 * layer : 216 + 16 * layer, :] = others[2 * layer - 1][...] + others[2 * layer][...]
            tail = misc.shape[0] // PIECES
            more = []
            for r in range(PIECES):
                j = xor(me[1], r)
                more.append(
                    pltpu.make_async_copy(
                        misc.at[pl.ds(pl.multiple_of(j * tail, 8), tail)],
                        (keep2 if r < half else send2).at[r % half, pl.ds(part, tail)],
                        sems.at[2 * PIECES + r],
                    )
                )
            copy_all(more)
        for item in copies:
            item.wait()


MISC_ROWS = 256


def attn_back(layer, bottom, kinds, me, dmid, o, qkv, lse, a, xh, rstd, gain, w_qkv, w_out, interp, like, others, padded, per, after):
    width = dmid.shape[1]
    total = dmid.shape[0]
    layers = w_qkv.shape[0]
    flat = per * padded
    blocks = total // flat
    saved = lambda feat: pl.BlockSpec((1, flat, feat), lambda b, k, m: (layer, b, 0))
    param = lambda *shape: pl.BlockSpec((1,) + shape, lambda b, k, m: (layer, 0, 0))
    fixed = lambda *shape: pl.BlockSpec(shape, lambda b, k, m: (0,) * len(shape))
    anywhere = pl.BlockSpec(memory_space=pl.ANY)
    in_specs = [
        pl.BlockSpec((flat, width), lambda b, k, m: (b, 0)),
        saved(width),
        saved(3 * width),
        pl.BlockSpec((1, per, 8, padded), lambda b, k, m: (layer, b, 0, 0)),
        saved(width),
        saved(width),
        saved(1),
        param(2, width),
        param(width, 3 * width),
        param(width, width),
    ]
    part = 4 * width // PIECES // 2
    tail = MISC_ROWS // PIECES if bottom else 0
    grads = halves(part, width) + halves(part + tail, width)
    grads_specs = [anywhere] * 4
    scratch = [
        pltpu.VMEM((flat, 3 * width), BF16),
        pltpu.VMEM((flat, width), BF16),
        pltpu.VMEM((4, width, width), F32),
        pltpu.SemaphoreType.DMA(((3 if bottom else 2) * PIECES,)),
    ]
    args = [kinds, me, dmid, o, qkv, lse, a, xh, rstd, gain, w_qkv, w_out]
    if bottom:
        rows = like.shape[1]
        in_specs += [fixed(*interp.shape)] + [fixed(16, width)] * len(others)
        args += [interp] + others
        out_specs = [pl.BlockSpec((per, rows, width), lambda b, k, m: (b, 0, 0))] + grads_specs
        out_shape = [jax.ShapeDtypeStruct(like.shape, F32)] + grads
        scratch += [pltpu.VMEM((16, width), F32), pltpu.VMEM((3, padded, width), F32), pltpu.VMEM((MISC_ROWS, width), F32)]
    else:
        out_specs = [pl.BlockSpec((flat, width), lambda b, k, m: (b, 0))] + grads_specs + [fixed(16, width)]
        out_shape = [jax.ShapeDtypeStruct((total, width), F32)] + grads + [jax.ShapeDtypeStruct((16, width), F32)]
    first = len(args)
    in_specs += [anywhere] * len(after)
    args += after
    return pl.pallas_call(
        drop(attn_back_kernel, (bottom, layers), first, len(after)),
        grid_spec=pltpu.PrefetchScalarGridSpec(
            num_scalar_prefetch=2,
            grid=(blocks,),
            in_specs=in_specs,
            out_specs=out_specs,
            scratch_shapes=scratch,
        ),
        out_shape=out_shape,
        compiler_params=pltpu.CompilerParams(vmem_limit_bytes=VMEM_LIMIT),
        cost_estimate=pl.CostEstimate(flops=32 * total * width * width, bytes_accessed=30 * total * width, transcendentals=0),
        name="attention_backward",
    )(*args)


def exchange(x, axis, bits, size):
    return lax.ppermute(x, axis, [(i, i ^ bits) for i in range(size)])


class Round:
    def __init__(self, streams, sizes):
        self.streams, self.sizes, self.stage = streams, sizes, 0

    def swap(self, x, axis, bits):
        return exchange(x, axis, bits, self.sizes[axis])

    def advance(self):
        stage = self.stage
        self.stage += 1
        if stage == 0:
            self.keep = [stream[0] for stream in self.streams]
            sent = [stream[1] for stream in self.streams]
            self.got = [self.swap(x, "grp", 1) for x in sent]
        elif stage <= 2:
            half = self.keep[0].shape[0] // 2
            sent = [keep[half:] + got[half:] for keep, got in zip(self.keep, self.got)]
            self.keep = [keep[:half] + got[:half] for keep, got in zip(self.keep, self.got)]
            self.got = [self.swap(x, "grp", stream[1 + stage]) for x, stream in zip(sent, self.streams)]
        elif stage == 3:
            joined = jnp.concatenate([keep + got for keep, got in zip(self.keep, self.got)], 1)
            self.keep = joined[0]
            sent = [joined[k] for k in range(1, 4)]
            self.got = [self.swap(x, "dp", k + 1) for k, x in enumerate(sent)]
        elif stage == 4:
            total = self.keep + self.got[0] + self.got[1] + self.got[2]
            for axis, bit in (("grp", 8), ("dp", 4)):
                while bit < self.sizes[axis]:
                    total = total + self.swap(total, axis, bit)
                    bit *= 2
            sent = [total]
            self.keep = total
            self.got = [self.swap(total, "dp", k) for k in range(1, 4)]
        elif stage == 5:
            every = jnp.stack([self.keep] + self.got)
            start, sent = 0, []
            for stream in self.streams:
                rows = stream[0].shape[1]
                sent.append(every[:, start : start + rows])
                start += rows
            self.keep = sent
            self.got = [self.swap(x, "grp", stream[3]) for x, stream in zip(sent, self.streams)]
        elif stage == 6:
            sent = [jnp.concatenate([keep, got]) for keep, got in zip(self.keep, self.got)]
            self.keep = sent
            self.got = [self.swap(x, "grp", stream[2]) for x, stream in zip(sent, self.streams)]
        else:
            self.keep = [[keep, got] for keep, got in zip(self.keep, self.got)]
            sent = sum(self.keep, [])
            self.got = [[self.swap(x, "grp", 1) for x in pair] for pair in self.keep]
        return sent

    def finish(self):
        while self.stage < 8:
            self.advance()
        return [keep + got for keep, got in zip(self.keep, self.got)]


def place_mlp_kernel(layer, me, *refs):
    alphas, betas = refs[0:4], refs[4:8]
    out1, out2, sems = refs[-3:]
    piece = alphas[0].shape[1]
    width = alphas[0].shape[2]
    copies = []
    for r in range(PIECES):
        j = xor(me[0], r)
        row = pl.multiple_of(lax.bitwise_and(j, GROUP - 1) * piece, 8)
        col = pl.multiple_of(lax.shift_right_logical(j, 3) * width, 128)
        copies.append(
            pltpu.make_async_copy(
                alphas[r // GROUP].at[r % GROUP], out1.at[layer, pl.ds(row, piece), pl.ds(col, width)], sems.at[2 * r]
            )
        )
        j = xor(me[1], r)
        row = pl.multiple_of(j * piece, 8)
        copies.append(
            pltpu.make_async_copy(betas[r // GROUP].at[r % GROUP], out2.at[layer, pl.ds(row, piece)], sems.at[2 * r + 1])
        )
    copy_all(copies)


def place_mlp(layer, me, pieces, before, shapes):
    anywhere = pl.BlockSpec(memory_space=pl.ANY)
    args = [me] + pieces[0] + pieces[1] + list(before)
    return pl.pallas_call(
        partial(place_mlp_kernel, layer),
        grid_spec=pltpu.PrefetchScalarGridSpec(
            num_scalar_prefetch=1,
            grid=(1,),
            in_specs=[pl.BlockSpec(x.shape, lambda b, m: (0, 0, 0)) for x in args[1:9]] + [anywhere] * len(before),
            out_specs=[anywhere] * 2,
            scratch_shapes=[pltpu.SemaphoreType.DMA((2 * PIECES,))],
        ),
        out_shape=[jax.ShapeDtypeStruct(shape, F32) for shape in shapes],
        input_output_aliases={9: 0, 10: 1} if before else {},
        compiler_params=pltpu.CompilerParams(vmem_limit_bytes=VMEM_LIMIT),
        name="place_mlp",
    )(*args)


def place_attn_kernel(layer, layers, last, me, *refs):
    alphas, betas = refs[0:4], refs[4:8]
    if last:
        gqkv, gout, gpos, ggain, gbias, gqvb, goutb, gb1, gb2, sems, misc, tail_sems = refs[-12:]
    else:
        gqkv, gout, sems = refs[-3:]
    part = alphas[0].shape[1]
    width = alphas[0].shape[2]
    waits = []
    tails = []
    for r in range(PIECES):
        for which, group in ((0, alphas), (1, betas)):
            j = xor(me[which], r)
            row = pl.multiple_of(lax.bitwise_and(j, GROUP - 1) * 2 * part + which * part, 8)
            col = lax.shift_right_logical(j, 3)
            source = group[r // GROUP].at[r % GROUP, pl.ds(0, part)]
            sem = sems.at[2 * r + which]

            @pl.when(col < 3)
            def _():
                wide = pl.multiple_of(col * width, 128)
                pltpu.make_async_copy(source, gqkv.at[layer, pl.ds(row, part), pl.ds(wide, width)], sem).start()

            @pl.when(col == 3)
            def _():
                pltpu.make_async_copy(source, gout.at[layer, pl.ds(row, part)], sem).start()

            waits.append(pltpu.make_async_copy(source, gout.at[layer, pl.ds(row, part)], sem))
        if last:
            tail = misc.shape[0] // PIECES
            j = xor(me[1], r)
            item = pltpu.make_async_copy(
                betas[r // GROUP].at[r % GROUP, pl.ds(part, tail)],
                misc.at[pl.ds(pl.multiple_of(j * tail, 8), tail)],
                tail_sems.at[r],
            )
            item.start()
            tails.append(item)
    if last:
        for item in tails:
            item.wait()
        gpos[...] = misc[0 : gpos.shape[0], :]
        for index in range(layers):
            base = 200 + 16 * index
            ggain[index] = misc[base : base + 2, :]
            gbias[index] = misc[base + 2 : base + 4, :]
            gqvb[index] = misc[base + 4 : base + 6, :]
            goutb[index : index + 1, :] = misc[base + 6 : base + 7, :]
            for k in range(gb1.shape[1] // width):
                gb1[index : index + 1, k * width : (k + 1) * width] = misc[base + 7 + k : base + 8 + k, :]
            gb2[index : index + 1, :] = misc[base + 11 : base + 12, :]
    for item in waits:
        item.wait()


def place_attn(layer, layers, me, pieces, before, shapes, small):
    anywhere = pl.BlockSpec(memory_space=pl.ANY)
    args = [me] + pieces[0] + pieces[1] + list(before)
    last = bool(small)
    scratch = [pltpu.SemaphoreType.DMA((2 * PIECES,))]
    if last:
        scratch += [pltpu.VMEM((MISC_ROWS, shapes[1][-1]), F32), pltpu.SemaphoreType.DMA((PIECES,))]
    return pl.pallas_call(
        partial(place_attn_kernel, layer, layers, last),
        grid_spec=pltpu.PrefetchScalarGridSpec(
            num_scalar_prefetch=1,
            grid=(1,),
            in_specs=[pl.BlockSpec(x.shape, lambda b, m: (0, 0, 0)) for x in args[1:9]] + [anywhere] * len(before),
            out_specs=[anywhere] * 2 + [pl.BlockSpec(s, lambda b, m, n=len(s): (0,) * n) for s in small],
            scratch_shapes=scratch,
        ),
        out_shape=[jax.ShapeDtypeStruct(shape, F32) for shape in list(shapes) + list(small)],
        input_output_aliases={9: 0, 10: 1} if before else {},
        compiler_params=pltpu.CompilerParams(vmem_limit_bytes=VMEM_LIMIT),
        name="place_attention",
    )(*args)


def on_device(sizes, tokens, kinds, interp, pos_base, ln_gain, ln_bias, w_qkv, qv_bias, w_out, out_bias, w_fc1, fc1_bias, w_fc2, fc2_bias, cotangent):
    count, rows, width = tokens.shape
    layers = w_qkv.shape[0]
    padded = -(-rows // 16) * 16
    per = 2 if count % 2 == 0 else 1
    g, d = lax.axis_index("grp"), lax.axis_index("dp")
    bit = lambda value, index: lax.bitwise_and(lax.shift_right_logical(value, index), 1)
    low = lax.bitwise_and(d, 3)
    me = jnp.stack(
        [
            bit(g, 0) * 16 + bit(g, 1) * 8 + bit(g, 2) * 4 + low,
            bit(g, 0) * 16 + bit(g, 2) * 8 + bit(g, 1) * 4 + low,
        ]
    ).astype(jnp.int32)
    mixed, a, qkv, lse, o, c, gp, gh, xh1, r1, xh2, r2 = forward(
        kinds, tokens, interp, pos_base, ln_gain, ln_bias, w_qkv, qv_bias, w_out, out_bias, w_fc1, fc1_bias, w_fc2, fc2_bias, padded, per
    )
    args = (kinds, me)
    small = (pos_base.shape, ln_gain.shape, ln_bias.shape, qv_bias.shape, out_bias.shape, fc1_bias.shape, fc2_bias.shape)
    dx, after, sums, rounds = cotangent, [], [], {}
    for layer in reversed(range(layers)):
        dmid, keep1, send1, keep2, send2, mlp_sums = mlp_back(
            layer, layer == layers - 1, *args, dx, c, gh, gp, xh2, r2, ln_gain, w_fc1, w_fc2, padded, per, after
        )
        after = sum([item.advance() for item in rounds.values()], [])
        item = rounds["mlp", layer] = Round(((keep1, send1, 2, 4), (keep2, send2, 4, 2)), sizes)
        item.advance()
        after += item.advance()
        out = attn_back(
            layer, layer == 0, *args, dmid, o, qkv, lse, a, xh1, r1, ln_gain, w_qkv, w_out, interp, tokens, [mlp_sums] + sums, padded, per, after
        )
        dx, keep1, send1, keep2, send2 = out[:5]
        after = sum([item.advance() for item in rounds.values()], [])
        item = rounds["attn", layer] = Round(((keep1, send1, 2, 4), (keep2, send2, 4, 2)), sizes)
        item.advance()
        after += item.advance()
        sums = [mlp_sums] + list(out[5:]) + sums
    while any(item.stage < 8 for item in rounds.values()):
        for item in rounds.values():
            if item.stage < 8:
                item.advance()
    mlp_out, attn_out = (), ()
    for layer in reversed(range(layers)):
        mlp_out = place_mlp(layer, me, rounds["mlp", layer].finish(), mlp_out, (w_fc1.shape, w_fc2.shape))
        attn_out = place_attn(
            layer, layers, me, rounds["attn", layer].finish(), attn_out[:2], (w_qkv.shape, w_out.shape), () if layer else small
        )
    gqkv, gout, gpos, ggain, gbias, gqvb, goutb, gb1, gb2 = attn_out
    return mixed, dx, gpos, ggain, gbias, gqkv, gqvb, gout, goutb, mlp_out[0], gb1, mlp_out[1], gb2


def solution(mesh):
    split = P(("grp", "dp"), None, None)
    return jax.shard_map(
        partial(on_device, dict(mesh.shape)),
        mesh=mesh,
        in_specs=(split, P(("grp", "dp"))) + (P(),) * 12 + (split,),
        out_specs=(split, split) + (P(),) * 11,
        check_vma=False,
    )
```

profile of v0, /device:TPU:0, one launch (start us, length us, event | category | flops | bytes accessed | tf_op | source)
XLA Modules:
  0.0 347.3 jit_solution(15623017504594297737)
XLA Ops:
  1.3 33.9 %encoder_forward.1 = (bf16[6,197,384]{2,1,0:T(8,128)(2,1)}, bf16[2,1248,384]{2,1,0:T(8,128)(2,1)}, bf16[2,1248,1152]{2,1,0:T(8,128)(2,1)}, f32[2,6,8,208]{3,2,1,...) custom-call(s32[6]{0:T(128)} %refs_0_.7, ...), custom_call_target="tpu_custom_call" | custom-call | tf_op jit(solution)/shard_map/encoder_forward/pallas_call | solution.py:181
  35.1 17.3 %mlp_backward.2 = (f32[1248,384]{1,0:T(8,128)}, f32[16,48,384]{2,1,0:T(8,128)}, f32[16,48,384]{2,1,0:T(8,128)}, f32[16,48,384]{2,1,0:T(8,128)}, f32[16,48,384]{2,1,0:T(8,128)}, /*index=5*/f32[16,384]{1,0:T(8,128)}) custom-call(s32[6]{0:T(128)} %refs_0_.7, s32[2]{0:T(128)} %pad_add_fusion.refs_1_.me, bf16[6,197,384]{2,1,0:T(8,128)(2,1)} %refs_2_.1, ...), custom_call_target="tpu_custom_call" | custom-call | flops 5888802816 | bytes 14376960 | tf_op jit(solution)/shard_map/mlp_backward/pallas_call | solution.py:341
  53.0 2.6 collective-permute-done
  55.6 1.5 slice_add_fusion.5
  57.1 2.9 collective-permute-start.2
  60.2 1.6 collective-permute-start.3
  61.8 19.4 %attention_backward.2 = (f32[1248,384]{1,0:T(8,128)}, f32[16,24,384]{2,1,0:T(8,128)}, f32[16,24,384]{2,1,0:T(8,128)}, f32[16,24,384]{2,1,0:T(8,128)}, f32[16,24,384]{2,1,0:T(8,128)}, /*index=5*/f32[16,384]{1,0:T(8,128)}) custom-call(s32[6]{0:T(128)} %refs_0_.7, s32[2]{0:T(128)} %pad_add_fusion.refs_1_.me, f32[1248,384]{1,0:T(8,128)} %get-tuple-element.69.refs_2_, ...), custom_call_target="tpu_custom_call" | custom-call | flops 5888802816 | bytes 14376960 | tf_op jit(solution)/shard_map/attention_backward/pallas_call | solution.py:546
  83.5 1.4 collective-permute-start.8
  85.0 1.3 collective-permute-start.9
  86.3 17.4 %mlp_backward.3 = (f32[1248,384]{1,0:T(8,128)}, f32[16,48,384]{2,1,0:T(8,128)}, f32[16,48,384]{2,1,0:T(8,128)}, f32[16,48,384]{2,1,0:T(8,128)}, f32[16,48,384]{2,1,0:T(8,128)}, /*index=5*/f32[16,384]{1,0:T(8,128)}) custom-call(s32[6]{0:T(128)} %refs_0_.7, s32[2]{0:T(128)} %pad_add_fusion.refs_1_.me, f32[1248,384]{1,0:T(8,128)} %get-tuple-element.80.refs_2_, ...), custom_call_target="tpu_custom_call" | custom-call | flops 5888802816 | bytes 14376960 | tf_op jit(solution)/shard_map/mlp_backward/pallas_call | solution.py:341
  109.9 1.3 collective-permute-done.32
  113.7 3.7 %collective-permute-start.36 = (f32[48,384]{1,0:T(8,128)S(1)}, f32[48,384]{1,0:T(8,128)S(1)}, u32[]{:S(2)}, u32[]{:S(2)}) collective-permute-start(f32[48,384]{1,0:T(8,128)S(1)} %get-tuple-element.145), channel_id=1, source_target_pairs={{0,3},{1,2},{2,1},{3,0},{4,7},{5,6},{6,5},{7,4},{8,11},{9,10},{10,... | collective-permute-start | bytes 221192 | tf_op jit(solution)/shard_map/ppermute | solution.py:563
  118.2 2.0 collective-permute-done.36
  120.2 3.8 %collective-permute-start.68 = (f32[96,384]{1,0:T(8,128)S(1)}, f32[96,384]{1,0:T(8,128)S(1)}, u32[]{:S(2)}, u32[]{:S(2)}) collective-permute-start(f32[96,384]{1,0:T(8,128)S(1)} %get-tuple-element.136.refs_18_), channel_id=1, source_target_pairs={{0,3},{1,2},{2,1},{3,0},{4,7},{5,6},{6,5},{7,4},{8,11},{9,10},{10,... | collective-permute-start | bytes 442376 | tf_op jit(solution)/shard_map/ppermute | solution.py:563
  123.9 4.6 %collective-permute-done.35 = f32[48,384]{1,0:T(8,128)S(1)} collective-permute-done((f32[48,384]{1,0:T(8,128)S(1)}, f32[48,384]{1,0:T(8,128)S(1)}, u32[]{:S(2)}, u32[]{:S(2)}) %collective-permute-start.35) | collective-permute-done | bytes 73760 | tf_op jit(solution)/shard_map/ppermute | solution.py:563
  128.5 2.8 collective-permute-start.66
  131.4 1.6 collective-permute-start.39
  133.0 5.0 %collective-permute-done.67 = f32[96,384]{1,0:T(8,128)S(1)} collective-permute-done((f32[96,384]{1,0:T(8,128)S(1)}, f32[96,384]{1,0:T(8,128)S(1)}, u32[]{:S(2)}, u32[]{:S(2)}) %collective-permute-start.67) | collective-permute-done | bytes 147488 | tf_op jit(solution)/shard_map/ppermute | solution.py:563
  138.0 3.0 collective-permute-start.37
  141.0 1.5 collective-permute-start.71
  142.5 6.2 %collective-permute-done.38 = f32[48,384]{1,0:T(8,128)S(1)} collective-permute-done((f32[48,384]{1,0:T(8,128)S(1)}, f32[48,384]{1,0:T(8,128)S(1)}, u32[]{:S(2)}, u32[]{:S(2)}) %collective-permute-start.38) | collective-permute-done | bytes 73760 | tf_op jit(solution)/shard_map/ppermute | solution.py:563
  148.8 2.3 collective-permute-start.69
  151.1 1.3 collective-permute-start.40
  152.5 2.9 collective-permute-done.70
  155.8 1.0 slice_add_fusion.1
  158.3 20.6 %attention_backward.3 = (f32[6,197,384]{2,1,0:T(8,128)}, f32[16,24,384]{2,1,0:T(8,128)}, f32[16,24,384]{2,1,0:T(8,128)}, f32[16,32,384]{2,1,0:T(8,128)}, f32[16,32,384]{2,1,0:T(8,128)}) custom-call(s32[6]{0:T(128)} %refs_0_.7, s32[2]{0:T(128)} %pad_add_fusion.refs_1_.me, f32[1248,384]{1,0:T(8,128)} %get-tuple-element.85.refs_2_, ...), custom_call_target="tpu_custom_call" | custom-call | flops 5888802816 | bytes 14376960 | tf_op jit(solution)/shard_map/attention_backward/pallas_call | solution.py:546
  179.0 1.3 collective-permute-start.72
  180.7 1.6 collective-permute-start.76
  182.8 4.2 %collective-permute-done.44 = f32[4,24,384]{2,1,0:T(8,128)S(1)} collective-permute-done((f32[4,24,384]{2,1,0:T(8,128)S(1)}, f32[4,24,384]{2,1,0:T(8,128)S(1)}, u32[]{:S(2)}, u32[]{:S(2)}) %collective-permute-start.44) | collective-permute-done | bytes 147488 | tf_op jit(solution)/shard_map/ppermute | solution.py:563
  189.7 16.3 %collective-permute-done.48 = f32[8,48,384]{2,1,0:T(8,128)S(1)} collective-permute-done((f32[8,48,384]{2,1,0:T(8,128)S(1)}, f32[8,48,384]{2,1,0:T(8,128)S(1)}, u32[]{:S(2)}, u32[]{:S(2)}) %collective-permute-start.48) | collective-permute-done | bytes 589856 | tf_op jit(solution)/shard_map/ppermute | solution.py:563
  206.4 1.1 collective-permute-start.49
  207.6 1.4 collective-permute-start.51
  209.1 9.5 %collective-permute-done.13 = f32[8,24,384]{2,1,0:T(8,128)S(1)} collective-permute-done((f32[8,24,384]{2,1,0:T(8,128)S(1)}, f32[8,24,384]{2,1,0:T(8,128)S(1)}, u32[]{:S(2)}, u32[]{:S(2)}) %collective-permute-start.13) | collective-permute-done | bytes 294944 | tf_op jit(solution)/shard_map/ppermute | solution.py:563
  219.4 1.3 collective-permute-start.14
  220.8 3.4 collective-permute-done.51
  224.3 2.2 collective-permute-start.54
  226.5 4.9 %collective-permute-done.14 = f32[4,24,384]{2,1,0:T(8,128)S(1)} collective-permute-done((f32[4,24,384]{2,1,0:T(8,128)S(1)}, f32[4,24,384]{2,1,0:T(8,128)S(1)}, u32[]{:S(2)}, u32[]{:S(2)}) %collective-permute-start.14) | collective-permute-done | bytes 147488 | tf_op jit(solution)/shard_map/ppermute | solution.py:563
  231.4 1.1 collective-permute-start.53
  232.6 1.6 collective-permute-start.52
  234.4 4.6 %collective-permute-done.53 = f32[96,384]{1,0:T(8,128)S(1)} collective-permute-done((f32[96,384]{1,0:T(8,128)S(1)}, f32[96,384]{1,0:T(8,128)S(1)}, u32[]{:S(2)}, u32[]{:S(2)}) %collective-permute-start.53) | collective-permute-done | bytes 147488 | tf_op jit(solution)/shard_map/ppermute | solution.py:563
  240.6 4.9 %collective-permute-done.17 = f32[4,32,384]{2,1,0:T(8,128)S(1)} collective-permute-done((f32[4,32,384]{2,1,0:T(8,128)S(1)}, f32[4,32,384]{2,1,0:T(8,128)S(1)}, u32[]{:S(2)}, u32[]{:S(2)}) %collective-permute-start.17) | collective-permute-done | bytes 196640 | tf_op jit(solution)/shard_map/ppermute | solution.py:563
  245.5 2.0 collective-permute-start.57
  247.7 1.9 collective-permute-start.20
  249.6 2.0 collective-permute-start.19
  252.7 8.8 %collective-permute-done.56 = f32[96,384]{1,0:T(8,128)S(1)} collective-permute-done((f32[96,384]{1,0:T(8,128)S(1)}, f32[96,384]{1,0:T(8,128)S(1)}, u32[]{:S(2)}, u32[]{:S(2)}) %collective-permute-start.56) | collective-permute-done | bytes 147488 | tf_op jit(solution)/shard_map/ppermute | solution.py:563
  264.5 5.3 %collective-permute-done.55 = f32[96,384]{1,0:T(8,128)S(1)} collective-permute-done((f32[96,384]{1,0:T(8,128)S(1)}, f32[96,384]{1,0:T(8,128)S(1)}, u32[]{:S(2)}, u32[]{:S(2)}) %collective-permute-start.55) | collective-permute-done | bytes 147488 | tf_op jit(solution)/shard_map/ppermute | solution.py:563
  269.8 2.0 collective-permute-start.23
  272.3 4.4 %collective-permute-done.23 = f32[56,384]{1,0:T(8,128)S(1)} collective-permute-done((f32[56,384]{1,0:T(8,128)S(1)}, f32[56,384]{1,0:T(8,128)S(1)}, u32[]{:S(2)}, u32[]{:S(2)}) %collective-permute-start.23) | collective-permute-done | bytes 86048 | tf_op jit(solution)/shard_map/ppermute | solution.py:563
  276.7 2.3 collective-permute-start.21
  279.0 1.1 collective-permute-done.22
  281.5 1.3 collective-permute-start.24
  283.4 6.6 %collective-permute-done.58 = f32[4,48,384]{2,1,0:T(8,128)S(1)} collective-permute-done((f32[4,48,384]{2,1,0:T(8,128)S(1)}, f32[4,48,384]{2,1,0:T(8,128)S(1)}, u32[]{:S(2)}, u32[]{:S(2)}) %collective-permute-start.58) | collective-permute-done | bytes 294944 | tf_op jit(solution)/shard_map/ppermute | solution.py:563
  290.0 2.1 collective-permute-done.24
  292.1 1.1 collective-permute-start.62
  294.3 7.7 %collective-permute-done.62 = f32[4,48,384]{2,1,0:T(8,128)S(1)} collective-permute-done((f32[4,48,384]{2,1,0:T(8,128)S(1)}, f32[4,48,384]{2,1,0:T(8,128)S(1)}, u32[]{:S(2)}, u32[]{:S(2)}) %collective-permute-start.62) | collective-permute-done | bytes 294944 | tf_op jit(solution)/shard_map/ppermute | solution.py:563
  302.0 1.1 collective-permute-start.25
  304.2 1.1 collective-permute-start.63
  306.3 1.2 collective-permute-start.29
  307.5 5.1 %collective-permute-done.25.refs_1_ = f32[8,24,384]{2,1,0:T(8,128)S(1)} collective-permute-done((f32[8,24,384]{2,1,0:T(8,128)S(1)}, f32[8,24,384]{2,1,0:T(8,128)S(1)}, u32[]{:S(2)}, u32[]{:S(2)}) %collective-permute-start.25) | collective-permute-done | bytes 294944 | tf_op jit(solution)/shard_map/ppermute | solution.py:563
  313.3 9.9 %collective-permute-done.59.refs_1_ = f32[8,48,384]{2,1,0:T(8,128)} collective-permute-done((f32[8,48,384]{2,1,0:T(8,128)S(1)}, f32[8,48,384]{2,1,0:T(8,128)}, u32[]{:S(2)}, u32[]{:S(2)}) %collective-permute-start.59) | collective-permute-done | bytes 589856 | tf_op jit(solution)/shard_map/ppermute | solution.py:563
  325.0 4.2 %place_attention.2 = (f32[2,384,1152]{2,1,0:T(8,128)}, f32[2,384,384]{2,1,0:T(8,128)}) custom-call(s32[2]{0:T(128)} %pad_add_fusion.refs_1_.me, f32[8,24,384]{2,1,0:T(8,128)} %copy-done.5, f32[8,24,384]{2,1,0:T(8,128)} %copy-done.32, f32[8,24,384]{2,1,0:T(8,128)} %copy-done.33, f32[8,24,384]{2,1,0:T(8,128)} %copy-done.36, f32[8,24,384]{2,1,0:T(8,128)} %copy-done.6, ...), custom_call_target="tpu_custom_call" | custom-call | tf_op jit(solution)/shard_map/place_attention/pallas_call | solution.py:728
  329.3 5.7 %place_mlp.2 = (f32[2,384,1536]{2,1,0:T(8,128)}, f32[2,1536,384]{2,1,0:T(8,128)}) custom-call(s32[2]{0:T(128)} %pad_add_fusion.refs_1_.me, f32[8,48,384]{2,1,0:T(8,128)} %copy-done, f32[8,48,384]{2,1,0:T(8,128)} %copy-done.16, f32[8,48,384]{2,1,0:T(8,128)} %copy-done.18, f32[8,48,384]{2,1,0:T(8,128)} %copy-done.20, f32[8,48,384]{2,1,0:T(8,128)} %copy-done.1, ...), custom_call_target="tpu_custom_call" | custom-call | tf_op jit(solution)/shard_map/place_mlp/pallas_call | solution.py:650
  335.0 5.5 %place_attention.3 = (f32[2,384,1152]{2,1,0:T(8,128)}, f32[2,384,384]{2,1,0:T(8,128)}, f32[197,384]{1,0:T(8,128)}, f32[2,2,384]{2,1,0:T(2,128)}, f32[2,2,384]{2,...) custom-call(s32[2]{0:T(128)} %pad_add_fusion.refs_1_.me, ...), custom_call_target="tpu_custom_call", output_to_operand_aliasing={{0}: (9, {}), {1}: (10, {})} | custom-call | tf_op jit(solution)/shard_map/place_attention/pallas_call | solution.py:728
  341.4 5.7 %place_mlp.3 = (f32[2,384,1536]{2,1,0:T(8,128)}, f32[2,1536,384]{2,1,0:T(8,128)}) custom-call(s32[2]{0:T(128)} %pad_add_fusion.refs_1_.me, f32[8,48,384]{2,1,0:T(8,128)} %copy-done.2, f32[8,48,384]{2,1,0:T(8,128)} %collective-permute-done.59.refs_1_, f32[8,48,384]{2,1,0:T(8,128)} %copy-done.23, ...), custom_call_target="tpu_custom_call", output_to_operand_aliasing={{0}: (9, {}), {1}: (10, {})} | custom-call | tf_op jit(solution)/shard_map/place_mlp/pallas_call | solution.py:650
  (248 shorter events, 35.0 us)
Async XLA Ops:
  57.1 24.6 %collective-permute-start.2 = (f32[8,48,384]{2,1,0:T(8,128)S(1)}, f32[8,48,384]{2,1,0:T(8,128)S(1)}, u32[]{:S(2)}, u32[]{:S(2)}) collective-permute-start(f32[8,48,384]{2,1,0:T(8,128)S(1)} %get-tuple-element.120.refs_12_), channel_id=1, source_target_pairs={{0,8},{4,12},{8,0},{12,4},{16,24},{20,28},{24,16},{28,20},{1,9},{5... | collective-permute-start | bytes 1769480 | tf_op jit(solution)/shard_map/ppermute | solution.py:563
  60.2 22.4 %collective-permute-start.3 = (f32[8,48,384]{2,1,0:T(8,128)S(1)}, f32[8,48,384]{2,1,0:T(8,128)S(1)}, u32[]{:S(2)}, u32[]{:S(2)}) collective-permute-start(f32[8,48,384]{2,1,0:T(8,128)S(1)} %get-tuple-element.118.refs_13_), channel_id=1, source_target_pairs={{0,16},{4,20},{8,24},{12,28},{16,0},{20,4},{24,8},{28,12},{1,17},{... | collective-permute-start | bytes 1769480 | tf_op jit(solution)/shard_map/ppermute | solution.py:563
  81.8 25.3 %collective-permute-start.6 = (f32[4,48,384]{2,1,0:T(8,128)S(1)}, f32[4,48,384]{2,1,0:T(8,128)}, u32[]{:S(2)}, u32[]{:S(2)}) collective-permute-start(f32[4,48,384]{2,1,0:T(8,128)S(1)} %slice_add_fusion.23.refs_11_), channel_id=1, source_target_pairs={{0,16},{4,20},{8,24},{12,28},{16,0},{20,4},{24,8},{28,12},{1,17},{... | collective-permute-start | bytes 884744 | tf_op jit(solution)/shard_map/ppermute | solution.py:563
  82.7 26.2 %collective-permute-start.7 = (f32[4,48,384]{2,1,0:T(8,128)S(1)}, f32[4,48,384]{2,1,0:T(8,128)}, u32[]{:S(2)}, u32[]{:S(2)}) collective-permute-start(f32[4,48,384]{2,1,0:T(8,128)S(1)} %slice_add_fusion.22.refs_12_), channel_id=1, source_target_pairs={{0,8},{4,12},{8,0},{12,4},{16,24},{20,28},{24,16},{28,20},{1,9},{5... | collective-permute-start | bytes 884744 | tf_op jit(solution)/shard_map/ppermute | solution.py:563
  83.5 20.3 %collective-permute-start.8 = (f32[8,24,384]{2,1,0:T(8,128)S(1)}, f32[8,24,384]{2,1,0:T(8,128)}, u32[]{:S(2)}, u32[]{:S(2)}) collective-permute-start(f32[8,24,384]{2,1,0:T(8,128)S(1)} %get-tuple-element.128.refs_13_), channel_id=1, source_target_pairs={{0,8},{4,12},{8,0},{12,4},{16,24},{20,28},{24,16},{28,20},{1,9},{5... | collective-permute-start | bytes 884744 | tf_op jit(solution)/shard_map/ppermute | solution.py:563
  85.0 20.3 %collective-permute-start.9 = (f32[8,24,384]{2,1,0:T(8,128)S(1)}, f32[8,24,384]{2,1,0:T(8,128)}, u32[]{:S(2)}, u32[]{:S(2)}) collective-permute-start(f32[8,24,384]{2,1,0:T(8,128)S(1)} %get-tuple-element.126.refs_14_), channel_id=1, source_target_pairs={{0,16},{4,20},{8,24},{12,28},{16,0},{20,4},{24,8},{28,12},{1,17},{... | collective-permute-start | bytes 884744 | tf_op jit(solution)/shard_map/ppermute | solution.py:563
  103.8 52.0 %collective-permute-start.10 = (f32[16,48,384]{2,1,0:T(8,128)}, f32[16,48,384]{2,1,0:T(8,128)S(1)}, u32[]{:S(2)}, u32[]{:S(2)}) collective-permute-start(f32[16,48,384]{2,1,0:T(8,128)} %get-tuple-element.90), channel_id=1, source_target_pairs={{0,4},{4,0},{8,12},{12,8},{16,20},{20,16},{24,28},{28,24},{1,5},{5... | collective-permute-start | bytes 3538952 | tf_op jit(solution)/shard_map/ppermute | solution.py:563
  103.9 52.9 %collective-permute-start.11 = (f32[16,48,384]{2,1,0:T(8,128)}, f32[16,48,384]{2,1,0:T(8,128)S(1)}, u32[]{:S(2)}, u32[]{:S(2)}) collective-permute-start(f32[16,48,384]{2,1,0:T(8,128)} %get-tuple-element.92), channel_id=1, source_target_pairs={{0,4},{4,0},{8,12},{12,8},{16,20},{20,16},{24,28},{28,24},{1,5},{5... | collective-permute-start | bytes 3538952 | tf_op jit(solution)/shard_map/ppermute | solution.py:563
  117.4 11.1 %collective-permute-start.35 = (f32[48,384]{1,0:T(8,128)S(1)}, f32[48,384]{1,0:T(8,128)S(1)}, u32[]{:S(2)}, u32[]{:S(2)}) collective-permute-start(f32[48,384]{1,0:T(8,128)S(1)} %get-tuple-element.146), channel_id=1, source_target_pairs={{0,2},{1,3},{2,0},{3,1},{4,6},{5,7},{6,4},{7,5},{8,10},{9,11},{10,... | collective-permute-start | bytes 221192 | tf_op jit(solution)/shard_map/ppermute | solution.py:563
  117.4 11.1 %collective-permute-start.34 = (f32[48,384]{1,0:T(8,128)S(1)}, f32[48,384]{1,0:T(8,128)S(1)}, u32[]{:S(2)}, u32[]{:S(2)}) collective-permute-start(f32[48,384]{1,0:T(8,128)S(1)} %get-tuple-element.144), channel_id=1, source_target_pairs={{0,1},{1,0},{2,3},{3,2},{4,5},{5,4},{6,7},{7,6},{8,9},{9,8},{10,11... | collective-permute-start | bytes 221192 | tf_op jit(solution)/shard_map/ppermute | solution.py:563
  120.2 11.2 %collective-permute-start.68 = (f32[96,384]{1,0:T(8,128)S(1)}, f32[96,384]{1,0:T(8,128)S(1)}, u32[]{:S(2)}, u32[]{:S(2)}) collective-permute-start(f32[96,384]{1,0:T(8,128)S(1)} %get-tuple-element.136.refs_18_), channel_id=1, source_target_pairs={{0,3},{1,2},{2,1},{3,0},{4,7},{5,6},{6,5},{7,4},{8,11},{9,10},{10,... | collective-permute-start | bytes 442376 | tf_op jit(solution)/shard_map/ppermute | solution.py:563
  128.5 9.5 %collective-permute-start.67 = (f32[96,384]{1,0:T(8,128)S(1)}, f32[96,384]{1,0:T(8,128)S(1)}, u32[]{:S(2)}, u32[]{:S(2)}) collective-permute-start(f32[96,384]{1,0:T(8,128)S(1)} %get-tuple-element.138.refs_17_), channel_id=1, source_target_pairs={{0,2},{1,3},{2,0},{3,1},{4,6},{5,7},{6,4},{7,5},{8,10},{9,11},{10,... | collective-permute-start | bytes 442376 | tf_op jit(solution)/shard_map/ppermute | solution.py:563
  128.5 9.5 %collective-permute-start.66 = (f32[96,384]{1,0:T(8,128)S(1)}, f32[96,384]{1,0:T(8,128)S(1)}, u32[]{:S(2)}, u32[]{:S(2)}) collective-permute-start(f32[96,384]{1,0:T(8,128)S(1)} %get-tuple-element.137.refs_16_), channel_id=1, source_target_pairs={{0,1},{1,0},{2,3},{3,2},{4,5},{5,4},{6,7},{7,6},{8,9},{9,8},{10,11... | collective-permute-start | bytes 442376 | tf_op jit(solution)/shard_map/ppermute | solution.py:563
  131.4 9.7 %collective-permute-start.39 = (f32[48,384]{1,0:T(8,128)S(1)}, f32[48,384]{1,0:T(8,128)S(1)}, u32[]{:S(2)}, u32[]{:S(2)}) collective-permute-start(f32[48,384]{1,0:T(8,128)S(1)} %fusion.44), channel_id=1, source_target_pairs={{0,3},{1,2},{2,1},{3,0},{4,7},{5,6},{6,5},{7,4},{8,11},{9,10},{10,... | collective-permute-start | bytes 221192 | tf_op jit(solution)/shard_map/ppermute | solution.py:563
  138.0 10.7 %collective-permute-start.38 = (f32[48,384]{1,0:T(8,128)S(1)}, f32[48,384]{1,0:T(8,128)S(1)}, u32[]{:S(2)}, u32[]{:S(2)}) collective-permute-start(f32[48,384]{1,0:T(8,128)S(1)} %fusion.44), channel_id=1, source_target_pairs={{0,2},{1,3},{2,0},{3,1},{4,6},{5,7},{6,4},{7,5},{8,10},{9,11},{10,... | collective-permute-start | bytes 221192 | tf_op jit(solution)/shard_map/ppermute | solution.py:563
  138.0 10.7 %collective-permute-start.37 = (f32[48,384]{1,0:T(8,128)S(1)}, f32[48,384]{1,0:T(8,128)S(1)}, u32[]{:S(2)}, u32[]{:S(2)}) collective-permute-start(f32[48,384]{1,0:T(8,128)S(1)} %fusion.44), channel_id=1, source_target_pairs={{0,1},{1,0},{2,3},{3,2},{4,5},{5,4},{6,7},{7,6},{8,9},{9,8},{10,11... | collective-permute-start | bytes 221192 | tf_op jit(solution)/shard_map/ppermute | solution.py:563
  141.0 10.1 %collective-permute-start.71 = (f32[96,384]{1,0:T(8,128)S(1)}, f32[96,384]{1,0:T(8,128)S(1)}, u32[]{:S(2)}, u32[]{:S(2)}) collective-permute-start(f32[96,384]{1,0:T(8,128)S(1)} %fusion.23), channel_id=1, source_target_pairs={{0,3},{1,2},{2,1},{3,0},{4,7},{5,6},{6,5},{7,4},{8,11},{9,10},{10,... | collective-permute-start | bytes 442376 | tf_op jit(solution)/shard_map/ppermute | solution.py:563
  151.1 31.2 %collective-permute-start.40 = (f32[4,24,384]{2,1,0:T(8,128)S(1)}, f32[4,24,384]{2,1,0:T(8,128)S(1)}, u32[]{:S(2)}, u32[]{:S(2)}) collective-permute-start(f32[4,24,384]{2,1,0:T(8,128)S(1)} %get-tuple-element.143), channel_id=1, source_target_pairs={{0,16},{4,20},{8,24},{12,28},{16,0},{20,4},{24,8},{28,12},{1,17},{... | collective-permute-start | bytes 442376 | tf_op jit(solution)/shard_map/ppermute | solution.py:563
  178.9 9.7 %collective-permute-start.12 = (f32[16,24,384]{2,1,0:T(8,128)}, f32[16,24,384]{2,1,0:T(8,128)S(1)}, u32[]{:S(2)}, u32[]{:S(2)}) collective-permute-start(f32[16,24,384]{2,1,0:T(8,128)} %get-tuple-element.95), channel_id=1, source_target_pairs={{0,4},{4,0},{8,12},{12,8},{16,20},{20,16},{24,28},{28,24},{1,5},{5... | collective-permute-start | bytes 1769480 | tf_op jit(solution)/shard_map/ppermute | solution.py:563
  179.0 9.5 %collective-permute-start.72 = (f32[4,48,384]{2,1,0:T(8,128)S(1)}, f32[4,48,384]{2,1,0:T(8,128)S(1)}, u32[]{:S(2)}, u32[]{:S(2)}) collective-permute-start(f32[4,48,384]{2,1,0:T(8,128)S(1)} %get-tuple-element.130), channel_id=1, source_target_pairs={{0,16},{4,20},{8,24},{12,28},{16,0},{20,4},{24,8},{28,12},{1,17},{... | collective-permute-start | bytes 884744 | tf_op jit(solution)/shard_map/ppermute | solution.py:563
  180.7 66.9 %collective-permute-start.76 = (f32[4,48,384]{2,1,0:T(8,128)S(1)}, f32[4,48,384]{2,1,0:T(8,128)S(1)}, u32[]{:S(2)}, u32[]{:S(2)}) collective-permute-start(f32[4,48,384]{2,1,0:T(8,128)S(1)} %get-tuple-element.129), channel_id=1, source_target_pairs={{0,8},{4,12},{8,0},{12,4},{16,24},{20,28},{24,16},{28,20},{1,9},{5... | collective-permute-start | bytes 884744 | tf_op jit(solution)/shard_map/ppermute | solution.py:563
  182.3 23.6 %collective-permute-start.48 = (f32[8,48,384]{2,1,0:T(8,128)S(1)}, f32[8,48,384]{2,1,0:T(8,128)S(1)}, u32[]{:S(2)}, u32[]{:S(2)}) collective-permute-start(f32[8,48,384]{2,1,0:T(8,128)S(1)} %copy-done.25), channel_id=1, source_target_pairs={{0,8},{4,12},{8,0},{12,4},{16,24},{20,28},{24,16},{28,20},{1,9},{5... | collective-permute-start | bytes 1769480 | tf_op jit(solution)/shard_map/ppermute | solution.py:563
  187.0 19.4 %collective-permute-start.50 = (f32[8,48,384]{2,1,0:T(8,128)S(1)}, f32[8,48,384]{2,1,0:T(8,128)S(1)}, u32[]{:S(2)}, u32[]{:S(2)}) collective-permute-start(f32[8,48,384]{2,1,0:T(8,128)S(1)} %copy-done.24), channel_id=1, source_target_pairs={{0,16},{4,20},{8,24},{12,28},{16,0},{20,4},{24,8},{28,12},{1,17},{... | collective-permute-start | bytes 1769480 | tf_op jit(solution)/shard_map/ppermute | solution.py:563
  188.5 19.0 %collective-permute-start.15 = (f32[16,32,384]{2,1,0:T(8,128)S(1)}, f32[16,32,384]{2,1,0:T(8,128)S(1)}, u32[]{:S(2)}, u32[]{:S(2)}) collective-permute-start(f32[16,32,384]{2,1,0:T(8,128)S(1)} %copy-done.46), channel_id=1, source_target_pairs={{0,4},{4,0},{8,12},{12,8},{16,20},{20,16},{24,28},{28,24},{1,5},{5... | collective-permute-start | bytes 2359304 | tf_op jit(solution)/shard_map/ppermute | solution.py:563
  188.6 59.1 %collective-permute-start.41 = (f32[8,24,384]{2,1,0:T(8,128)S(1)}, f32[8,24,384]{2,1,0:T(8,128)S(1)}, u32[]{:S(2)}, u32[]{:S(2)}) collective-permute-start(f32[8,24,384]{2,1,0:T(8,128)S(1)} %pad_maximum_fusion.9.refs_0_), channel_id=1, source_target_pairs={{0,8},{4,12},{8,0},{12,4},{16,24},{20,28},{24,16},{28,20},{1,9},{5... | collective-permute-start | bytes 884744 | tf_op jit(solution)/shard_map/ppermute | solution.py:563
  205.9 12.6 %collective-permute-start.13 = (f32[8,24,384]{2,1,0:T(8,128)S(1)}, f32[8,24,384]{2,1,0:T(8,128)S(1)}, u32[]{:S(2)}, u32[]{:S(2)}) collective-permute-start(f32[8,24,384]{2,1,0:T(8,128)S(1)} %get-tuple-element.124), channel_id=1, source_target_pairs={{0,8},{4,12},{8,0},{12,4},{16,24},{20,28},{24,16},{28,20},{1,9},{5... | collective-permute-start | bytes 884744 | tf_op jit(solution)/shard_map/ppermute | solution.py:563
  206.4 13.0 %collective-permute-start.49 = (f32[4,48,384]{2,1,0:T(8,128)S(1)}, f32[4,48,384]{2,1,0:T(8,128)S(1)}, u32[]{:S(2)}, u32[]{:S(2)}) collective-permute-start(f32[4,48,384]{2,1,0:T(8,128)S(1)} %slice_add_fusion.12), channel_id=1, source_target_pairs={{0,16},{4,20},{8,24},{12,28},{16,0},{20,4},{24,8},{28,12},{1,17},{... | collective-permute-start | bytes 884744 | tf_op jit(solution)/shard_map/ppermute | solution.py:563
  207.6 16.6 %collective-permute-start.51 = (f32[4,48,384]{2,1,0:T(8,128)S(1)}, f32[4,48,384]{2,1,0:T(8,128)S(1)}, u32[]{:S(2)}, u32[]{:S(2)}) collective-permute-start(f32[4,48,384]{2,1,0:T(8,128)S(1)} %slice_add_fusion.10), channel_id=1, source_target_pairs={{0,8},{4,12},{8,0},{12,4},{16,24},{20,28},{24,16},{28,20},{1,9},{5... | collective-permute-start | bytes 884744 | tf_op jit(solution)/shard_map/ppermute | solution.py:563
  218.6 14.0 %collective-permute-start.16 = (f32[8,32,384]{2,1,0:T(8,128)S(1)}, f32[8,32,384]{2,1,0:T(8,128)S(1)}, u32[]{:S(2)}, u32[]{:S(2)}) collective-permute-start(f32[8,32,384]{2,1,0:T(8,128)S(1)} %get-tuple-element.122), channel_id=1, source_target_pairs={{0,16},{4,20},{8,24},{12,28},{16,0},{20,4},{24,8},{28,12},{1,17},{... | collective-permute-start | bytes 1179656 | tf_op jit(solution)/shard_map/ppermute | solution.py:563
  219.4 12.0 %collective-permute-start.14 = (f32[4,24,384]{2,1,0:T(8,128)S(1)}, f32[4,24,384]{2,1,0:T(8,128)S(1)}, u32[]{:S(2)}, u32[]{:S(2)}) collective-permute-start(f32[4,24,384]{2,1,0:T(8,128)S(1)} %slice_add_fusion.28), channel_id=1, source_target_pairs={{0,16},{4,20},{8,24},{12,28},{16,0},{20,4},{24,8},{28,12},{1,17},{... | collective-permute-start | bytes 442376 | tf_op jit(solution)/shard_map/ppermute | solution.py:563
  224.3 10.0 %collective-permute-start.54 = (f32[96,384]{1,0:T(8,128)S(1)}, f32[96,384]{1,0:T(8,128)S(1)}, u32[]{:S(2)}, u32[]{:S(2)}) collective-permute-start(f32[96,384]{1,0:T(8,128)S(1)} %get-tuple-element.134), channel_id=1, source_target_pairs={{0,3},{1,2},{2,1},{3,0},{4,7},{5,6},{6,5},{7,4},{8,11},{9,10},{10,... | collective-permute-start | bytes 442376 | tf_op jit(solution)/shard_map/ppermute | solution.py:563
  231.4 7.6 %collective-permute-start.53 = (f32[96,384]{1,0:T(8,128)S(1)}, f32[96,384]{1,0:T(8,128)S(1)}, u32[]{:S(2)}, u32[]{:S(2)}) collective-permute-start(f32[96,384]{1,0:T(8,128)S(1)} %get-tuple-element.135), channel_id=1, source_target_pairs={{0,2},{1,3},{2,0},{3,1},{4,6},{5,7},{6,4},{7,5},{8,10},{9,11},{10,... | collective-permute-start | bytes 442376 | tf_op jit(solution)/shard_map/ppermute | solution.py:563
  232.6 7.2 %collective-permute-start.52 = (f32[96,384]{1,0:T(8,128)S(1)}, f32[96,384]{1,0:T(8,128)S(1)}, u32[]{:S(2)}, u32[]{:S(2)}) collective-permute-start(f32[96,384]{1,0:T(8,128)S(1)} %get-tuple-element.133), channel_id=1, source_target_pairs={{0,1},{1,0},{2,3},{3,2},{4,5},{5,4},{6,7},{7,6},{8,9},{9,8},{10,11... | collective-permute-start | bytes 442376 | tf_op jit(solution)/shard_map/ppermute | solution.py:563
  234.3 15.3 %collective-permute-start.42 = (f32[8,24,384]{2,1,0:T(8,128)S(1)}, f32[8,24,384]{2,1,0:T(8,128)S(1)}, u32[]{:S(2)}, u32[]{:S(2)}) collective-permute-start(f32[8,24,384]{2,1,0:T(8,128)S(1)} %pad_maximum_fusion.9.refs_0_), channel_id=1, source_target_pairs={{0,4},{4,0},{8,12},{12,8},{16,20},{20,16},{24,28},{28,24},{1,5},{5... | collective-permute-start | bytes 884744 | tf_op jit(solution)/shard_map/ppermute | solution.py:563
  239.0 12.6 %collective-permute-start.45 = (f32[8,24,384]{2,1,0:T(8,128)S(1)}, f32[8,24,384]{2,1,0:T(8,128)S(1)}, u32[]{:S(2)}, u32[]{:S(2)}) collective-permute-start(f32[8,24,384]{2,1,0:T(8,128)S(1)} %pad_maximum_fusion.10.refs_4_), channel_id=1, source_target_pairs={{0,16},{4,20},{8,24},{12,28},{16,0},{20,4},{24,8},{28,12},{1,17},{... | collective-permute-start | bytes 884744 | tf_op jit(solution)/shard_map/ppermute | solution.py:563
  247.6 13.9 %collective-permute-start.56 = (f32[96,384]{1,0:T(8,128)S(1)}, f32[96,384]{1,0:T(8,128)S(1)}, u32[]{:S(2)}, u32[]{:S(2)}) collective-permute-start(f32[96,384]{1,0:T(8,128)S(1)} %fusion.11), channel_id=1, source_target_pairs={{0,2},{1,3},{2,0},{3,1},{4,6},{5,7},{6,4},{7,5},{8,10},{9,11},{10,... | collective-permute-start | bytes 442376 | tf_op jit(solution)/shard_map/ppermute | solution.py:563
  247.7 14.5 %collective-permute-start.20 = (f32[56,384]{1,0:T(8,128)S(1)}, f32[56,384]{1,0:T(8,128)S(1)}, u32[]{:S(2)}, u32[]{:S(2)}) collective-permute-start(f32[56,384]{1,0:T(8,128)S(1)} %get-tuple-element.140), channel_id=1, source_target_pairs={{0,3},{1,2},{2,1},{3,0},{4,7},{5,6},{6,5},{7,4},{8,11},{9,10},{10,... | collective-permute-start | bytes 258056 | tf_op jit(solution)/shard_map/ppermute | solution.py:563
  249.6 13.9 %collective-permute-start.19 = (f32[56,384]{1,0:T(8,128)S(1)}, f32[56,384]{1,0:T(8,128)S(1)}, u32[]{:S(2)}, u32[]{:S(2)}) collective-permute-start(f32[56,384]{1,0:T(8,128)S(1)} %get-tuple-element.141), channel_id=1, source_target_pairs={{0,2},{1,3},{2,0},{3,1},{4,6},{5,7},{6,4},{7,5},{8,10},{9,11},{10,... | collective-permute-start | bytes 258056 | tf_op jit(solution)/shard_map/ppermute | solution.py:563
  251.6 11.9 %collective-permute-start.18 = (f32[56,384]{1,0:T(8,128)S(1)}, f32[56,384]{1,0:T(8,128)S(1)}, u32[]{:S(2)}, u32[]{:S(2)}) collective-permute-start(f32[56,384]{1,0:T(8,128)S(1)} %get-tuple-element.139), channel_id=1, source_target_pairs={{0,1},{1,0},{2,3},{3,2},{4,5},{5,4},{6,7},{7,6},{8,9},{9,8},{10,11... | collective-permute-start | bytes 258056 | tf_op jit(solution)/shard_map/ppermute | solution.py:563
  252.7 19.1 %collective-permute-start.46 = (f32[8,24,384]{2,1,0:T(8,128)S(1)}, f32[8,24,384]{2,1,0:T(8,128)S(1)}, u32[]{:S(2)}, u32[]{:S(2)}) collective-permute-start(f32[8,24,384]{2,1,0:T(8,128)S(1)} %pad_maximum_fusion.10.refs_4_), channel_id=1, source_target_pairs={{0,4},{4,0},{8,12},{12,8},{16,20},{20,16},{24,28},{28,24},{1,5},{5... | collective-permute-start | bytes 884744 | tf_op jit(solution)/shard_map/ppermute | solution.py:563
  261.5 21.3 %collective-permute-start.73 = (f32[8,48,384]{2,1,0:T(8,128)S(1)}, f32[8,48,384]{2,1,0:T(8,128)S(1)}, u32[]{:S(2)}, u32[]{:S(2)}) collective-permute-start(f32[8,48,384]{2,1,0:T(8,128)S(1)} %pad_maximum_fusion.4.refs_0_), channel_id=1, source_target_pairs={{0,8},{4,12},{8,0},{12,4},{16,24},{20,28},{24,16},{28,20},{1,9},{5... | collective-permute-start | bytes 1769480 | tf_op jit(solution)/shard_map/ppermute | solution.py:563
  262.2 20.9 %collective-permute-start.77 = (f32[8,48,384]{2,1,0:T(8,128)S(1)}, f32[8,48,384]{2,1,0:T(8,128)S(1)}, u32[]{:S(2)}, u32[]{:S(2)}) collective-permute-start(f32[8,48,384]{2,1,0:T(8,128)S(1)} %pad_maximum_fusion.5.refs_4_), channel_id=1, source_target_pairs={{0,16},{4,20},{8,24},{12,28},{16,0},{20,4},{24,8},{28,12},{1,17},{... | collective-permute-start | bytes 1769480 | tf_op jit(solution)/shard_map/ppermute | solution.py:563
  263.5 8.4 %collective-permute-start.43 = (f32[8,24,384]{2,1,0:T(8,128)S(1)}, f32[8,24,384]{2,1,0:T(8,128)S(1)}, u32[]{:S(2)}, u32[]{:S(2)}) collective-permute-start(f32[8,24,384]{2,1,0:T(8,128)S(1)} %collective-permute-done.41.refs_1_), channel_id=1, source_target_pairs={{0,4},{4,0},{8,12},{12,8},{16,20},{20,16},{24,28},{28,24},{1,5},{5... | collective-permute-start | bytes 884744 | tf_op jit(solution)/shard_map/ppermute | solution.py:563
  271.9 9.6 %collective-permute-start.47 = (f32[8,24,384]{2,1,0:T(8,128)S(1)}, f32[8,24,384]{2,1,0:T(8,128)S(1)}, u32[]{:S(2)}, u32[]{:S(2)}) collective-permute-start(f32[8,24,384]{2,1,0:T(8,128)S(1)} %collective-permute-done.45.refs_5_), channel_id=1, source_target_pairs={{0,4},{4,0},{8,12},{12,8},{16,20},{20,16},{24,28},{28,24},{1,5},{5... | collective-permute-start | bytes 884744 | tf_op jit(solution)/shard_map/ppermute | solution.py:563
  272.0 8.1 %collective-permute-start.22 = (f32[56,384]{1,0:T(8,128)S(1)}, f32[56,384]{1,0:T(8,128)S(1)}, u32[]{:S(2)}, u32[]{:S(2)}) collective-permute-start(f32[56,384]{1,0:T(8,128)S(1)} %fusion.34), channel_id=1, source_target_pairs={{0,2},{1,3},{2,0},{3,1},{4,6},{5,7},{6,4},{7,5},{8,10},{9,11},{10,... | collective-permute-start | bytes 258056 | tf_op jit(solution)/shard_map/ppermute | solution.py:563
  280.1 9.9 %collective-permute-start.58 = (f32[4,48,384]{2,1,0:T(8,128)S(1)}, f32[4,48,384]{2,1,0:T(8,128)S(1)}, u32[]{:S(2)}, u32[]{:S(2)}) collective-permute-start(f32[4,48,384]{2,1,0:T(8,128)S(1)} %get-tuple-element.132), channel_id=1, source_target_pairs={{0,16},{4,20},{8,24},{12,28},{16,0},{20,4},{24,8},{28,12},{1,17},{... | collective-permute-start | bytes 884744 | tf_op jit(solution)/shard_map/ppermute | solution.py:563
  281.5 11.8 %collective-permute-start.74 = (f32[8,48,384]{2,1,0:T(8,128)S(1)}, f32[8,48,384]{2,1,0:T(8,128)S(1)}, u32[]{:S(2)}, u32[]{:S(2)}) collective-permute-start(f32[8,48,384]{2,1,0:T(8,128)S(1)} %pad_maximum_fusion.4.refs_0_), channel_id=1, source_target_pairs={{0,4},{4,0},{8,12},{12,8},{16,20},{20,16},{24,28},{28,24},{1,5},{5... | collective-permute-start | bytes 1769480 | tf_op jit(solution)/shard_map/ppermute | solution.py:563
  281.5 10.5 %collective-permute-start.24 = (f32[4,24,384]{2,1,0:T(8,128)S(1)}, f32[4,24,384]{2,1,0:T(8,128)S(1)}, u32[]{:S(2)}, u32[]{:S(2)}) collective-permute-start(f32[4,24,384]{2,1,0:T(8,128)S(1)} %pad_maximum_fusion.16), channel_id=1, source_target_pairs={{0,16},{4,20},{8,24},{12,28},{16,0},{20,4},{24,8},{28,12},{1,17},{... | collective-permute-start | bytes 442376 | tf_op jit(solution)/shard_map/ppermute | solution.py:563
  282.8 20.4 %collective-permute-start.78 = (f32[8,48,384]{2,1,0:T(8,128)S(1)}, f32[8,48,384]{2,1,0:T(8,128)S(1)}, u32[]{:S(2)}, u32[]{:S(2)}) collective-permute-start(f32[8,48,384]{2,1,0:T(8,128)S(1)} %pad_maximum_fusion.5.refs_4_), channel_id=1, source_target_pairs={{0,4},{4,0},{8,12},{12,8},{16,20},{20,16},{24,28},{28,24},{1,5},{5... | collective-permute-start | bytes 1769480 | tf_op jit(solution)/shard_map/ppermute | solution.py:563
  283.1 21.1 %collective-permute-start.75 = (f32[8,48,384]{2,1,0:T(8,128)S(1)}, f32[8,48,384]{2,1,0:T(8,128)S(1)}, u32[]{:S(2)}, u32[]{:S(2)}) collective-permute-start(f32[8,48,384]{2,1,0:T(8,128)S(1)} %collective-permute-done.73.refs_1_), channel_id=1, source_target_pairs={{0,4},{4,0},{8,12},{12,8},{16,20},{20,16},{24,28},{28,24},{1,5},{5... | collective-permute-start | bytes 1769480 | tf_op jit(solution)/shard_map/ppermute | solution.py:563
  290.0 16.3 %collective-permute-start.79 = (f32[8,48,384]{2,1,0:T(8,128)S(1)}, f32[8,48,384]{2,1,0:T(8,128)S(1)}, u32[]{:S(2)}, u32[]{:S(2)}) collective-permute-start(f32[8,48,384]{2,1,0:T(8,128)S(1)} %collective-permute-done.77.refs_5_), channel_id=1, source_target_pairs={{0,4},{4,0},{8,12},{12,8},{16,20},{20,16},{24,28},{28,24},{1,5},{5... | collective-permute-start | bytes 1769480 | tf_op jit(solution)/shard_map/ppermute | solution.py:563
  292.1 9.9 %collective-permute-start.62 = (f32[4,48,384]{2,1,0:T(8,128)S(1)}, f32[4,48,384]{2,1,0:T(8,128)S(1)}, u32[]{:S(2)}, u32[]{:S(2)}) collective-permute-start(f32[4,48,384]{2,1,0:T(8,128)S(1)} %get-tuple-element.131), channel_id=1, source_target_pairs={{0,8},{4,12},{8,0},{12,4},{16,24},{20,28},{24,16},{28,20},{1,9},{5... | collective-permute-start | bytes 884744 | tf_op jit(solution)/shard_map/ppermute | solution.py:563
  293.3 12.9 %collective-permute-start.28 = (f32[4,32,384]{2,1,0:T(8,128)S(1)}, f32[4,32,384]{2,1,0:T(8,128)S(1)}, u32[]{:S(2)}, u32[]{:S(2)}) collective-permute-start(f32[4,32,384]{2,1,0:T(8,128)S(1)} %pad_maximum_fusion.11), channel_id=1, source_target_pairs={{0,8},{4,12},{8,0},{12,4},{16,24},{20,28},{24,16},{28,20},{1,9},{5... | collective-permute-start | bytes 589832 | tf_op jit(solution)/shard_map/ppermute | solution.py:563
  302.0 10.5 %collective-permute-start.25 = (f32[8,24,384]{2,1,0:T(8,128)S(1)}, f32[8,24,384]{2,1,0:T(8,128)S(1)}, u32[]{:S(2)}, u32[]{:S(2)}) collective-permute-start(f32[8,24,384]{2,1,0:T(8,128)S(1)} %pad_maximum_fusion.7.refs_0_), channel_id=1, source_target_pairs={{0,8},{4,12},{8,0},{12,4},{16,24},{20,28},{24,16},{28,20},{1,9},{5... | collective-permute-start | bytes 884744 | tf_op jit(solution)/shard_map/ppermute | solution.py:563
  303.2 20.0 %collective-permute-start.59 = (f32[8,48,384]{2,1,0:T(8,128)S(1)}, f32[8,48,384]{2,1,0:T(8,128)}, u32[]{:S(2)}, u32[]{:S(2)}) collective-permute-start(f32[8,48,384]{2,1,0:T(8,128)S(1)} %pad_maximum_fusion.1.refs_0_), channel_id=1, source_target_pairs={{0,8},{4,12},{8,0},{12,4},{16,24},{20,28},{24,16},{28,20},{1,9},{5... | collective-permute-start | bytes 1769480 | tf_op jit(solution)/shard_map/ppermute | solution.py:563
  304.2 19.1 %collective-permute-start.63 = (f32[8,48,384]{2,1,0:T(8,128)S(1)}, f32[8,48,384]{2,1,0:T(8,128)S(1)}, u32[]{:S(2)}, u32[]{:S(2)}) collective-permute-start(f32[8,48,384]{2,1,0:T(8,128)S(1)} %pad_maximum_fusion.2.refs_4_), channel_id=1, source_target_pairs={{0,16},{4,20},{8,24},{12,28},{16,0},{20,4},{24,8},{28,12},{1,17},{... | collective-permute-start | bytes 1769480 | tf_op jit(solution)/shard_map/ppermute | solution.py:563
  306.3 17.5 %collective-permute-start.29 = (f32[8,32,384]{2,1,0:T(8,128)S(1)}, f32[8,32,384]{2,1,0:T(8,128)}, u32[]{:S(2)}, u32[]{:S(2)}) collective-permute-start(f32[8,32,384]{2,1,0:T(8,128)S(1)} %pad_maximum_fusion.6.refs_4_), channel_id=1, source_target_pairs={{0,16},{4,20},{8,24},{12,28},{16,0},{20,4},{24,8},{28,12},{1,17},{... | collective-permute-start | bytes 1179656 | tf_op jit(solution)/shard_map/ppermute | solution.py:563
  312.5 11.3 %collective-permute-start.30 = (f32[8,32,384]{2,1,0:T(8,128)S(1)}, f32[8,32,384]{2,1,0:T(8,128)S(1)}, u32[]{:S(2)}, u32[]{:S(2)}) collective-permute-start(f32[8,32,384]{2,1,0:T(8,128)S(1)} %pad_maximum_fusion.6.refs_4_), channel_id=1, source_target_pairs={{0,4},{4,0},{8,12},{12,8},{16,20},{20,16},{24,28},{28,24},{1,5},{5... | collective-permute-start | bytes 1179656 | tf_op jit(solution)/shard_map/ppermute | solution.py:563
  312.6 11.8 %collective-permute-start.27 = (f32[8,24,384]{2,1,0:T(8,128)S(1)}, f32[8,24,384]{2,1,0:T(8,128)S(1)}, u32[]{:S(2)}, u32[]{:S(2)}) collective-permute-start(f32[8,24,384]{2,1,0:T(8,128)S(1)} %collective-permute-done.25.refs_1_), channel_id=1, source_target_pairs={{0,4},{4,0},{8,12},{12,8},{16,20},{20,16},{24,28},{28,24},{1,5},{5... | collective-permute-start | bytes 884744 | tf_op jit(solution)/shard_map/ppermute | solution.py:563
  323.3 17.3 %collective-permute-start.60 = (f32[8,48,384]{2,1,0:T(8,128)S(1)}, f32[8,48,384]{2,1,0:T(8,128)S(1)}, u32[]{:S(2)}, u32[]{:S(2)}) collective-permute-start(f32[8,48,384]{2,1,0:T(8,128)S(1)} %pad_maximum_fusion.1.refs_0_), channel_id=1, source_target_pairs={{0,4},{4,0},{8,12},{12,8},{16,20},{20,16},{24,28},{28,24},{1,5},{5... | collective-permute-start | bytes 1769480 | tf_op jit(solution)/shard_map/ppermute | solution.py:563
  323.3 17.3 %collective-permute-start.64 = (f32[8,48,384]{2,1,0:T(8,128)S(1)}, f32[8,48,384]{2,1,0:T(8,128)}, u32[]{:S(2)}, u32[]{:S(2)}) collective-permute-start(f32[8,48,384]{2,1,0:T(8,128)S(1)} %pad_maximum_fusion.2.refs_4_), channel_id=1, source_target_pairs={{0,4},{4,0},{8,12},{12,8},{16,20},{20,16},{24,28},{28,24},{1,5},{5... | collective-permute-start | bytes 1769480 | tf_op jit(solution)/shard_map/ppermute | solution.py:563
  323.8 16.8 %collective-permute-start.61 = (f32[8,48,384]{2,1,0:T(8,128)}, f32[8,48,384]{2,1,0:T(8,128)}, u32[]{:S(2)}, u32[]{:S(2)}) collective-permute-start(f32[8,48,384]{2,1,0:T(8,128)} %collective-permute-done.59.refs_1_), channel_id=1, source_target_pairs={{0,4},{4,0},{8,12},{12,8},{16,20},{20,16},{24,28},{28,24},{1,5},{5... | collective-permute-start | bytes 1769480 | tf_op jit(solution)/shard_map/ppermute | solution.py:563
  323.9 16.7 %collective-permute-start.65 = (f32[8,48,384]{2,1,0:T(8,128)S(1)}, f32[8,48,384]{2,1,0:T(8,128)}, u32[]{:S(2)}, u32[]{:S(2)}) collective-permute-start(f32[8,48,384]{2,1,0:T(8,128)S(1)} %collective-permute-done.63.refs_5_), channel_id=1, source_target_pairs={{0,4},{4,0},{8,12},{12,8},{16,20},{20,16},{24,28},{28,24},{1,5},{5... | collective-permute-start | bytes 1769480 | tf_op jit(solution)/shard_map/ppermute | solution.py:563
  324.6 10.4 %collective-permute-start.31 = (f32[8,32,384]{2,1,0:T(8,128)}, f32[8,32,384]{2,1,0:T(8,128)}, u32[]{:S(2)}, u32[]{:S(2)}) collective-permute-start(f32[8,32,384]{2,1,0:T(8,128)} %collective-permute-done.29.refs_5_), channel_id=1, source_target_pairs={{0,4},{4,0},{8,12},{12,8},{16,20},{20,16},{24,28},{28,24},{1,5},{5... | collective-permute-start | bytes 1179656 | tf_op jit(solution)/shard_map/ppermute | solution.py:563
  (63 other events, 951.3 us)
where the time goes:
time: 348 us; the launch traced here: 347 us
  Pallas kernels  130 us (37%)
  waiting for transfers between devices  127 us (36%)
  starting transfers between devices  75.1 us (22%)
  other arithmetic  11.2 us (3%)
    ppermute x80, waiting for transfers between devices, exchange(): return lax.ppermute(x, axis, [(i, i ^ bits) for i in range(size)])  127 us
    ppermute x80, starting transfers between devices, exchange(): return lax.ppermute(x, axis, [(i, i ^ bits) for i in range(size)])  75.1 us
    pallas_call x2, Pallas kernels, attn_back(): pl.pallas_call(drop(attn_back_kernel, (bottom, layers), first, len(after)...  39.9 us
    pallas_call x2, Pallas kernels, mlp_back(): pl.pallas_call(drop(mlp_back_kernel, (top,), 11, len(after)), grid_spec=p...  34.7 us
    pallas_call x1, Pallas kernels, forward(): pl.pallas_call(fwd_kernel, grid_spec=pltpu.PrefetchScalarGridSpec(num_sca...  33.9 us
    pallas_call x2, Pallas kernels, place_mlp(): pl.pallas_call(partial(place_mlp_kernel, layer), grid_spec=pltpu.Prefetch...  11.4 us
    pallas_call x2, Pallas kernels, place_attn(): pl.pallas_call(partial(place_attn_kernel, layer, layers, last), grid_spec...  9.72 us
  transfers between devices with their start and end apart: 80, of which 31 were waited for; matrix products, arithmetic and copies ran while one was open for 3% of the time, Pallas kernels for 21%

commit v1 on v0

v1 whole, which is shorter than its diff:
```python
from functools import partial

import jax
import jax.numpy as jnp
from jax import lax
from jax.experimental import pallas as pl
from jax.experimental.pallas import tpu as pltpu
from jax.sharding import PartitionSpec as P

HEADS = 6
HEAD = 64
BASE = 197
CROP_B = 181
CROP_C = 193
EPS = 1e-06
F32 = jnp.float32
BF16 = jnp.bfloat16
VMEM_LIMIT = 60 * 1024 * 1024

ERF_P = 0.39
ERF_C = (0.11766263, 0.04569411, 0.32477995, -0.31770045, 0.44333237, -0.11376861)


def dot(a, b):
    return lax.dot_general(a, b, (((1,), (0,)), ((), ())), preferred_element_type=F32)


def dot_bt(a, b):
    return lax.dot_general(a, b, (((1,), (1,)), ((), ())), preferred_element_type=F32)


def dot_at(a, b):
    return lax.dot_general(a, b, (((0,), (0,)), ((), ())), preferred_element_type=F32)


def split3(x):
    hi = x.astype(BF16)
    rest = x - hi.astype(F32)
    mid = rest.astype(BF16)
    low = (rest - mid.astype(F32)).astype(BF16)
    return hi, mid, low


def length_of(kind):
    return jnp.where(kind == 0, BASE, jnp.where(kind == 1, CROP_B, CROP_C)).astype(jnp.int32)


def pick(ref, layer):
    row = ref[0:1].astype(F32)
    for index in range(1, ref.shape[0]):
        row = jnp.where(layer == index, ref[index : index + 1].astype(F32), row)
    return row


def norm(x):
    width = x.shape[-1]
    mean = jnp.sum(x, -1, keepdims=True) * (1.0 / width)
    centered = x - mean
    var = jnp.sum(centered * centered, -1, keepdims=True) * (1.0 / width)
    rstd = lax.rsqrt(var + EPS)
    return centered * rstd, rstd


def norm_back(dc, xhat, rstd, gain):
    width = dc.shape[-1]
    dxh = dc * gain
    m1 = jnp.sum(dxh, -1, keepdims=True) * (1.0 / width)
    m2 = jnp.sum(dxh * xhat, -1, keepdims=True) * (1.0 / width)
    return rstd * (dxh - m1 - xhat * m2)


def gelu_parts(x):
    phi = 0.5 + 0.5 * lax.erf(x * 0.5**0.5)
    return x * phi, phi + x * (jnp.exp2(x * x * (-0.5 * 1.4426950408889634)) * 0.3989422804014327)


def head_masks():
    first = lax.broadcasted_iota(jnp.int32, (1, 2 * HEAD), 1) < HEAD
    plain = [jnp.where(first, 1.0, 0.0), jnp.where(first, 0.0, 1.0)]
    return [x.astype(BF16) for x in plain], [(x * HEAD**-0.5).astype(BF16) for x in plain]


def fwd_kernel(
    kinds, tok, interp, pos, gain, bias, w_qkv, qvb, w_out, outb, w1, b1, w2, b2,
    mixed, a_o, qkv_o, lse_o, o_o, c_o, gp_o, gh_o, xh1_o, r1_o, xh2_o, r2_o,
    x_all, table_s, mid_s, o_s,
):
    layer, block = pl.program_id(0), pl.program_id(1)
    x_s = x_all.at[block]
    images, rows, width = tok.shape
    padded = x_all.shape[2]
    flat = images * padded
    heads_pair = 2 * HEAD

    @pl.when((block == 0) & (layer == 0))
    def _():
        for kind in range(interp.shape[0]):
            total = jnp.zeros((rows, width), F32)
            for part in split3(interp[kind])[::-1]:
                total += dot(part, pos[...])
            table_s[kind, 0:rows, :] = total

    @pl.when(layer == 0)
    def _():
        for i in range(images):
            kind = kinds[block * images + i]
            here = lax.broadcasted_iota(jnp.int32, (rows, 1), 0) < length_of(kind)
            h0 = tok[i].astype(F32) + table_s[kind, 0:rows, :]
            x_s[i] = jnp.zeros((padded, width), F32)
            x_s[i, 0:rows, :] = jnp.where(here, h0, 0.0)

    x = x_s[...].reshape(flat, width)
    xhat, rstd = norm(x)
    a = (xhat * gain[0, 0:1].astype(F32) + bias[0, 0:1].astype(F32)).astype(BF16)
    a_o[0] = a
    xh1_o[0] = xhat.astype(BF16)
    r1_o[0] = rstd
    bias_row = qvb[0].astype(F32)
    bias_row = jnp.concatenate([bias_row[0:1], jnp.zeros((1, width), F32), bias_row[1:2]], 1)
    qkv_o[0] = (dot(a, w_qkv[0]) + bias_row).astype(BF16)
    plain, scaled = head_masks()
    for i in range(images):
        r0 = i * padded
        length = length_of(kinds[block * images + i])
        key_ok = lax.broadcasted_iota(jnp.int32, (1, padded, 1), 1) < length
        for pair in range(HEADS // 2):
            c0 = pair * heads_pair
            q2 = qkv_o[0, r0 : r0 + padded, c0 : c0 + heads_pair]
            k2 = qkv_o[0, r0 : r0 + padded, width + c0 : width + c0 + heads_pair]
            v2 = qkv_o[0, r0 : r0 + padded, 2 * width + c0 : 2 * width + c0 + heads_pair]
            ks = jnp.concatenate([k2 * keep for keep in scaled], 0)
            vs = jnp.concatenate([v2 * keep for keep in plain], 0)
            s = jnp.where(key_ok, dot_bt(ks, q2).reshape(2, padded, padded), -1e9)
            top = jnp.max(s, 1, keepdims=True)
            e = jnp.exp(s - top)
            total = jnp.sum(e, 1, keepdims=True)
            lse_o[0, i, 2 * pair : 2 * pair + 2, :] = (top + jnp.log(total)).reshape(2, padded)
            p = (e * (1.0 / total)).astype(BF16).reshape(2 * padded, padded)
            o_s[r0 : r0 + padded, c0 : c0 + heads_pair] = dot_at(p, vs).astype(BF16)
    o = o_s[...]
    o_o[0] = o
    mid = x_s[...].reshape(flat, width) + dot(o, w_out[0]) + pick(outb, layer)
    mid_s[...] = mid
    xhat, rstd = norm(mid)
    c = (xhat * gain[0, 1:2].astype(F32) + bias[0, 1:2].astype(F32)).astype(BF16)
    c_o[0] = c
    xh2_o[0] = xhat.astype(BF16)
    r2_o[0] = rstd
    hidden = w1.shape[2]
    bias1 = pick(b1, layer)
    step = 256
    total = mid_s[...] + pick(b2, layer)
    for f in range(0, hidden, step):
        pre = dot(c, w1[0, :, f : f + step]) + bias1[:, f : f + step]
        gh, gp = gelu_parts(pre)
        gh = gh.astype(BF16)
        gh_o[0, :, f : f + step] = gh
        gp_o[0, :, f : f + step] = gp.astype(BF16)
        total += dot(gh, w2[0, f : f + step, :])
    x_s[...] = total.reshape(images, padded, width)

    @pl.when(layer == pl.num_programs(0) - 1)
    def _():
        for i in range(images):
            kind = kinds[block * images + i]
            here = lax.broadcasted_iota(jnp.int32, (rows, 1), 0) < length_of(kind)
            mixed[i] = jnp.where(here, x_s[i, 0:rows, :], 0.0).astype(BF16)


def forward(kinds, tokens, interp, pos_base, ln_gain, ln_bias, w_qkv, qv_bias, w_out, out_bias, w_fc1, fc1_bias, w_fc2, fc2_bias, padded, per):
    count, rows, width = tokens.shape
    layers, _, hidden = w_fc1.shape
    blocks = count // per
    flat = per * padded
    whole = lambda shape: pl.BlockSpec(shape, lambda l, b, k: (0,) * len(shape))
    by_layer = lambda shape: pl.BlockSpec((1,) + shape, lambda l, b, k: (l,) + (0,) * len(shape))
    read_image = pl.BlockSpec((per, rows, width), lambda l, b, k: (jnp.where(l == 0, b, blocks - 1), 0, 0))
    write_image = pl.BlockSpec((per, rows, width), lambda l, b, k: (jnp.where(l == layers - 1, b, 0), 0, 0))
    saved = lambda feat: pl.BlockSpec((1, flat, feat), lambda l, b, k: (l, b, 0))
    shape = lambda feat, dtype: jax.ShapeDtypeStruct((layers, count * padded, feat), dtype)
    return pl.pallas_call(
        fwd_kernel,
        grid_spec=pltpu.PrefetchScalarGridSpec(
            num_scalar_prefetch=1,
            grid=(layers, blocks),
            in_specs=[
                read_image,
                whole(interp.shape),
                whole(pos_base.shape),
                by_layer((2, width)),
                by_layer((2, width)),
                by_layer((width, 3 * width)),
                by_layer((2, width)),
                by_layer((width, width)),
                whole(out_bias.shape),
                by_layer((width, hidden)),
                whole(fc1_bias.shape),
                by_layer((hidden, width)),
                whole(fc2_bias.shape),
            ],
            out_specs=[
                write_image,
                saved(width),
                saved(3 * width),
                pl.BlockSpec((1, per, 8, padded), lambda l, b, k: (l, b, 0, 0)),
                saved(width),
                saved(width),
                saved(hidden),
                saved(hidden),
                saved(width),
                saved(1),
                saved(width),
                saved(1),
            ],
            scratch_shapes=[
                pltpu.VMEM((blocks, per, padded, width), F32),
                pltpu.VMEM((3, padded, width), F32),
                pltpu.VMEM((flat, width), F32),
                pltpu.VMEM((flat, width), BF16),
            ],
        ),
        out_shape=[
            jax.ShapeDtypeStruct(tokens.shape, BF16),
            shape(width, BF16),
            shape(3 * width, BF16),
            jax.ShapeDtypeStruct((layers, count, 8, padded), F32),
            shape(width, BF16),
            shape(width, BF16),
            shape(hidden, BF16),
            shape(hidden, BF16),
            shape(width, BF16),
            shape(1, F32),
            shape(width, BF16),
            shape(1, F32),
        ],
        compiler_params=pltpu.CompilerParams(vmem_limit_bytes=VMEM_LIMIT),
        name="encoder_forward",
    )(kinds, tokens, interp, pos_base, ln_gain, ln_bias, w_qkv, qv_bias, w_out, out_bias, w_fc1, fc1_bias, w_fc2, fc2_bias)


PIECES = 32
HALF = PIECES // 2
GROUP = 4
MISC_ROWS = 256
MISC_BASE = 200
MISC_LAYER = 16


def spot(me, r, rows):
    j = lax.bitwise_xor(me, jnp.int32(r))
    return lax.shift_right_logical(j, 3), pl.multiple_of(lax.bitwise_and(j, 7) * rows, 8)


def emit(me, source, keep, send, first, sems):
    rows = source.shape[1] // 8
    copies = []
    for r in range(PIECES):
        block, row = spot(me[r // HALF], r % HALF, rows)
        target = (keep, send)[r // HALF].at[r % HALF, pl.ds(first, rows)]
        copies.append(pltpu.make_async_copy(source.at[block, pl.ds(row, rows)], target, sems.at[r]))
    for item in copies:
        item.start()
    return copies


def mlp_back_kernel(top, kinds, me, dx_ref, c, gh, gp, xh, rstd, gain, w1, w2, dmid, *rest):
    if top:
        keep, send, sums, gw1, sems, gw2, dx_s = rest
    else:
        keep, send, sums, gw1, sems = rest
    block = pl.program_id(0)

    @pl.when(block == 0)
    def _():
        gw1[...] = jnp.zeros_like(gw1)
        if top:
            gw2[...] = jnp.zeros_like(gw2)
        sums[...] = jnp.zeros_like(sums)

    if top:
        images, rows, width = dx_ref.shape
        padded = dx_s.shape[1]
        for i in range(images):
            kind = kinds[block * images + i]
            here = lax.broadcasted_iota(jnp.int32, (rows, 1), 0) < length_of(kind)
            dx_s[i] = jnp.zeros((padded, width), F32)
            dx_s[i, 0:rows, :] = jnp.where(here, dx_ref[i].astype(F32), 0.0)
        dx = dx_s[...].reshape(images * padded, width)
    else:
        dx = dx_ref[...]
    flat, width = dx.shape
    hidden = w1.shape[2]
    dz = dx.astype(BF16)
    sums[11:12, :] += jnp.sum(dz.astype(F32), 0, keepdims=True)
    if top:
        for k in range(gw2.shape[0]):
            gw2[k] += dot_at(gh[0, :, k * width : (k + 1) * width], dz)
    dgh = dot_bt(dz, w2[0])
    dpre = (dgh * gp[0].astype(F32)).astype(BF16)
    column = jnp.sum(dpre.astype(F32), 0, keepdims=True)
    grad = dot_at(c[0], dpre)
    for k in range(hidden // width):
        here = slice(k * width, (k + 1) * width)
        sums[7 + k : 8 + k, :] += column[:, here]
        gw1[k] += grad[:, here]
    dc = dot_bt(dpre, w1[0])
    xhat = xh[0].astype(F32)
    sums[1:2, :] += jnp.sum(dc * xhat, 0, keepdims=True)
    sums[3:4, :] += jnp.sum(dc, 0, keepdims=True)
    dmid[...] = dx + norm_back(dc, xhat, rstd[0], gain[0, 1:2].astype(F32))

    @pl.when(block == pl.num_programs(0) - 1)
    def _():
        copies = emit(me, gw1, keep, send, 0, sems)
        if top:
            copies += emit(me, gw2, keep, send, width // 8, sems.at[pl.ds(PIECES, PIECES)])
        for item in copies:
            item.wait()


def drop(kernel, fixed, first, count):
    def body(*refs):
        return kernel(*fixed, *refs[:first], *refs[first + count :])

    return body


def pieces_of(rows, width):
    return [jax.ShapeDtypeStruct((HALF, rows, width), F32)] * 2


def mlp_back(layer, top, kinds, me, dx, c, gh, gp, xh, rstd, gain, w1, w2, padded, per, after):
    layers, width, hidden = w1.shape
    total = c.shape[1]
    flat = per * padded
    saved = lambda feat: pl.BlockSpec((1, flat, feat), lambda b, k, m: (layer, b, 0))
    param = lambda *shape: pl.BlockSpec((1,) + shape, lambda b, k, m: (layer, 0, 0))
    fixed = lambda *shape: pl.BlockSpec(shape, lambda b, k, m: (0,) * len(shape))
    rows_spec = pl.BlockSpec((flat, width), lambda b, k, m: (b, 0))
    anywhere = pl.BlockSpec(memory_space=pl.ANY)
    if top:
        dx_spec = pl.BlockSpec((per,) + dx.shape[1:], lambda b, k, m: (b, 0, 0))
        scratch = [pltpu.VMEM((hidden // width, width, width), F32), pltpu.VMEM((per, padded, width), F32)]
    else:
        dx_spec = rows_spec
        scratch = []
    out_specs = [anywhere] * 2
    out_shape = pieces_of((2 if top else 1) * hidden // PIECES, width)
    scratch = [pltpu.VMEM((hidden // width, width, width), F32), pltpu.SemaphoreType.DMA((2 * PIECES,))] + scratch
    return pl.pallas_call(
        drop(mlp_back_kernel, (top,), 11, len(after)),
        grid_spec=pltpu.PrefetchScalarGridSpec(
            num_scalar_prefetch=2,
            grid=(total // flat,),
            in_specs=[
                dx_spec,
                saved(width),
                saved(hidden) if top else anywhere,
                saved(hidden),
                saved(width),
                saved(1),
                param(2, width),
                param(width, hidden),
                param(hidden, width),
            ]
            + [anywhere] * len(after),
            out_specs=[rows_spec] + out_specs + [fixed(16, width)],
            scratch_shapes=scratch,
        ),
        out_shape=[jax.ShapeDtypeStruct((total, width), F32)] + out_shape + [jax.ShapeDtypeStruct((16, width), F32)],
        compiler_params=pltpu.CompilerParams(vmem_limit_bytes=VMEM_LIMIT),
        cost_estimate=pl.CostEstimate(flops=8 * total * width * hidden, bytes_accessed=30 * total * width, transcendentals=0),
        name="mlp_backward",
    )(kinds, me, dx, c, gh, gp, xh, rstd, gain, w1, w2, *after)


def attn_back_kernel(bottom, layers, kinds, me, dmid, o, qkv, lse, a, xh, rstd, gain, w_qkv, w_out, *rest):
    if bottom:
        interp, dx_ref, keep, send, dqkv_s, do_s, gw, sems, sums, kind_s, misc = rest[:1] + rest[2 * layers :]
        others = rest[1 : 2 * layers]
    else:
        gh_next, dx_ref, keep, send, sums, dqkv_s, do_s, gw, sems, gw2 = rest
    block = pl.program_id(0)
    images = lse.shape[1]
    flat, width = dmid.shape
    padded = flat // images

    @pl.when(block == 0)
    def _():
        gw[...] = jnp.zeros_like(gw)
        sums[...] = jnp.zeros_like(sums)
        if bottom:
            kind_s[...] = jnp.zeros_like(kind_s)
        else:
            gw2[...] = jnp.zeros_like(gw2)

    dy = dmid[...].astype(BF16)
    sums[6:7, :] += jnp.sum(dy.astype(F32), 0, keepdims=True)
    do_s[...] = dot_bt(dy, w_out[0]).astype(BF16)
    gw[3] += dot_at(o[0], dy)
    pair_width = 2 * HEAD
    plain, scaled = head_masks()
    first = lax.broadcasted_iota(jnp.int32, (1, pair_width), 1) < HEAD
    for i in range(images):
        rows = slice(i * padded, (i + 1) * padded)
        length = length_of(kinds[block * images + i])
        key_ok = lax.broadcasted_iota(jnp.int32, (1, padded, 1), 1) < length
        for pair in range(HEADS // 2):
            c0 = pair * pair_width
            part = lambda base: slice(base + c0, base + c0 + pair_width)
            q2, k2, v2 = qkv[0, rows, part(0)], qkv[0, rows, part(width)], qkv[0, rows, part(2 * width)]
            do2 = do_s[rows, part(0)]
            ks = jnp.concatenate([k2 * keep for keep in scaled], 0)
            vs = jnp.concatenate([v2 * keep for keep in plain], 0)
            s = jnp.where(key_ok, dot_bt(ks, q2).reshape(2, padded, padded), -1e9)
            p = jnp.exp(s - lse[0, i, 2 * pair : 2 * pair + 2, :].reshape(2, 1, padded))
            dp = dot_bt(vs, do2).reshape(2, padded, padded)
            delta = jnp.sum(dp * p, 1, keepdims=True)
            ds = (p * (dp - delta)).astype(BF16).reshape(2 * padded, padded)
            dv = dot(p.astype(BF16).reshape(2 * padded, padded), do2)
            dk = dot(ds, q2)
            dqkv_s[rows, part(0)] = dot_at(ds, ks).astype(BF16)
            dqkv_s[rows, part(width)] = (jnp.where(first, dk[:padded], dk[padded:]) * HEAD**-0.5).astype(BF16)
            dqkv_s[rows, part(2 * width)] = jnp.where(first, dv[:padded], dv[padded:]).astype(BF16)
    d = dqkv_s[...]
    for index in (0, 2):
        row = 4 + index // 2
        sums[row : row + 1, :] += jnp.sum(d[:, index * width : (index + 1) * width].astype(F32), 0, keepdims=True)
    grad = dot_at(a[0], d)
    for index in range(3):
        gw[index] += grad[:, index * width : (index + 1) * width]
    da = dot_bt(d, w_qkv[0])
    xhat = xh[0].astype(F32)
    sums[0:1, :] += jnp.sum(da * xhat, 0, keepdims=True)
    sums[2:3, :] += jnp.sum(da, 0, keepdims=True)
    dx = dmid[...] + norm_back(da, xhat, rstd[0], gain[0, 0:1].astype(F32))
    if bottom:
        real = dx_ref.shape[1]
        for i in range(images):
            kind = kinds[block * images + i]
            here = lax.broadcasted_iota(jnp.int32, (padded, 1), 0) < length_of(kind)
            mine = jnp.where(here, dx[i * padded : (i + 1) * padded], 0.0)
            dx_ref[i] = mine[0:real]
            kind_s[kind] += mine
    else:
        dx_ref[...] = dx
        dz = dx.astype(BF16)
        for k in range(gw2.shape[0]):
            gw2[k] += dot_at(gh_next[0, :, k * width : (k + 1) * width], dz)

    @pl.when(block == pl.num_programs(0) - 1)
    def _():
        rows = width // 8
        copies = emit(me, gw, keep, send, 0, sems)
        if not bottom:
            copies += emit(me, gw2, keep, send, rows, sems.at[pl.ds(PIECES, PIECES)])
        if bottom:
            total = jnp.zeros((real, width), F32)
            for kind in range(interp.shape[0]):
                hi, mid, _ = split3(interp[kind])
                ghi, gmid, _ = split3(kind_s[kind, 0:real, :])
                total += dot_at(mid, ghi) + dot_at(hi, gmid) + dot_at(hi, ghi)
            misc[...] = jnp.zeros_like(misc)
            misc[0:real, :] = total
            misc[MISC_BASE : MISC_BASE + 16, :] = sums[...] + others[0][...]
            for layer in range(1, layers):
                start = MISC_BASE + MISC_LAYER * layer
                misc[start : start + 16, :] = others[2 * layer - 1][...] + others[2 * layer][...]
            tail = misc.shape[0] // PIECES
            for r in range(PIECES):
                j = lax.bitwise_xor(me[r // HALF], jnp.int32(r % HALF))
                target = (keep, send)[r // HALF].at[r % HALF, pl.ds(rows, tail)]
                item = pltpu.make_async_copy(misc.at[pl.ds(pl.multiple_of(j * tail, 8), tail)], target, sems.at[PIECES + r])
                item.start()
                copies.append(item)
        for item in copies:
            item.wait()


def attn_back(layer, bottom, kinds, me, dmid, o, qkv, lse, a, xh, rstd, gain, w_qkv, w_out, gh, interp, like, others, padded, per, after):
    width = dmid.shape[1]
    total = dmid.shape[0]
    layers = w_qkv.shape[0]
    flat = per * padded
    blocks = total // flat
    saved = lambda feat: pl.BlockSpec((1, flat, feat), lambda b, k, m: (layer, b, 0))
    param = lambda *shape: pl.BlockSpec((1,) + shape, lambda b, k, m: (layer, 0, 0))
    fixed = lambda *shape: pl.BlockSpec(shape, lambda b, k, m: (0,) * len(shape))
    anywhere = pl.BlockSpec(memory_space=pl.ANY)
    in_specs = [
        pl.BlockSpec((flat, width), lambda b, k, m: (b, 0)),
        saved(width),
        saved(3 * width),
        pl.BlockSpec((1, per, 8, padded), lambda b, k, m: (layer, b, 0, 0)),
        saved(width),
        saved(width),
        saved(1),
        param(2, width),
        param(width, 3 * width),
        param(width, width),
    ]
    tail = MISC_ROWS // PIECES if bottom else width // 8
    grads = pieces_of(width // 8 + tail, width)
    scratch = [
        pltpu.VMEM((flat, 3 * width), BF16),
        pltpu.VMEM((flat, width), BF16),
        pltpu.VMEM((4, width, width), F32),
        pltpu.SemaphoreType.DMA((2 * PIECES,)),
    ]
    args = [kinds, me, dmid, o, qkv, lse, a, xh, rstd, gain, w_qkv, w_out]
    if bottom:
        rows = like.shape[1]
        in_specs += [fixed(*interp.shape)] + [fixed(16, width)] * len(others)
        args += [interp] + others
        out_specs = [pl.BlockSpec((per, rows, width), lambda b, k, m: (b, 0, 0))] + [anywhere] * 2
        out_shape = [jax.ShapeDtypeStruct(like.shape, F32)] + grads
        scratch += [pltpu.VMEM((16, width), F32), pltpu.VMEM((3, padded, width), F32), pltpu.VMEM((MISC_ROWS, width), F32)]
    else:
        hidden = gh.shape[2]
        in_specs += [pl.BlockSpec((1, flat, hidden), lambda b, k, m: (layer - 1, b, 0))]
        args += [gh]
        out_specs = [pl.BlockSpec((flat, width), lambda b, k, m: (b, 0))] + [anywhere] * 2 + [fixed(16, width)]
        out_shape = [jax.ShapeDtypeStruct((total, width), F32)] + grads + [jax.ShapeDtypeStruct((16, width), F32)]
        scratch += [pltpu.VMEM((hidden // width, width, width), F32)]
    first = len(args)
    in_specs += [anywhere] * len(after)
    args += after
    return pl.pallas_call(
        drop(attn_back_kernel, (bottom, layers), first, len(after)),
        grid_spec=pltpu.PrefetchScalarGridSpec(
            num_scalar_prefetch=2,
            grid=(blocks,),
            in_specs=in_specs,
            out_specs=out_specs,
            scratch_shapes=scratch,
        ),
        out_shape=out_shape,
        compiler_params=pltpu.CompilerParams(vmem_limit_bytes=VMEM_LIMIT),
        cost_estimate=pl.CostEstimate(flops=32 * total * width * width, bytes_accessed=30 * total * width, transcendentals=0),
        name="attention_backward",
    )(*args)


def exchange(x, axis, bits, size):
    return lax.ppermute(x, axis, [(i, i ^ bits) for i in range(size)])


def combine(tasks, after, through):
    args = sum([list(inputs) for _, inputs, _ in tasks], [])
    shapes = sum([list(results) for _, _, results in tasks], [])

    def body(*refs):
        ins, outs = refs[: len(args)], refs[len(args) + len(through) + len(after) :]
        for function, inputs, results in tasks:
            function(ins[: len(inputs)], outs[: len(results)])
            ins, outs = ins[len(inputs) :], outs[len(results) :]

    vmem = pl.BlockSpec(memory_space=pltpu.VMEM)
    anywhere = pl.BlockSpec(memory_space=pl.ANY)
    moved = sum(x.size for x in args) * 4
    out = pl.pallas_call(
        body,
        in_specs=[vmem] * len(args) + [anywhere] * (len(through) + len(after)),
        out_specs=[vmem] * len(shapes) + [anywhere] * len(through),
        out_shape=[jax.ShapeDtypeStruct(shape, F32) for shape in shapes] + [jax.ShapeDtypeStruct(x.shape, F32) for x in through],
        input_output_aliases={len(args) + k: len(shapes) + k for k in range(len(through))},
        compiler_params=pltpu.CompilerParams(vmem_limit_bytes=VMEM_LIMIT),
        cost_estimate=pl.CostEstimate(flops=moved, bytes_accessed=2 * moved, transcendentals=0),
        name="combine",
    )(*args, *through, *after)
    result = []
    for _, _, results in tasks:
        result.append(list(out[: len(results)]))
        out = out[len(results) :]
    return result, list(out)


def halve(ins, outs):
    keep, got = ins
    half = keep.shape[0] // 2
    outs[0][...] = keep[half:] + got[half:]
    outs[1][...] = keep[:half] + got[:half]


def split_four(ins, outs):
    start = 0
    for keep, got in zip(ins[::2], ins[1::2]):
        rows = keep.shape[1]
        for k, out in enumerate(outs):
            out[start : start + rows] = keep[k] + got[k]
        start += rows


def total_of(ins, outs):
    start = 0
    for a, b, c, d in zip(ins[::4], ins[1::4], ins[2::4], ins[3::4]):
        rows = a.shape[0]
        outs[0][start : start + rows] = (a[...] + b[...]) + (c[...] + d[...])
        start += rows


def stack(ins, outs):
    for k, x in enumerate(ins):
        outs[0][k] = x[...]


class Round:
    def __init__(self, keep, send, sizes):
        self.keep, self.send, self.sizes, self.stage = keep, send, sizes, 0
        self.shape = keep.shape[1:]
        self.more = []

    def merge(self, other):
        assert self.stage == other.stage
        self.more = [other.keep, *other.got]
        self.shape = (self.shape[0] + other.shape[0], self.shape[1])
        return self

    def across(self, x, which):
        bits = lambda i: (2, 4)[(i & 1) ^ which]
        return lax.ppermute(x, "grp", [(i, i ^ bits(i)) for i in range(self.sizes["grp"])])

    def swap(self, x, axis, bits):
        return exchange(x, axis, bits, self.sizes[axis])

    def tasks(self):
        stage, n = self.stage, self.shape
        args = [self.keep, *getattr(self, "got", ()), *self.more]
        self.more = []
        if stage in (1, 2):
            return [(halve, args, ((PIECES >> (stage + 1),) + n,) * 2)]
        if stage == 3:
            return [(split_four, args, (n,) * 4)]
        if stage == 4:
            return [(total_of, args, (n,))]
        if stage == 5:
            return [(stack, args, ((4,) + n,))]
        return []

    def launch(self, done):
        stage = self.stage
        self.stage += 1
        if stage == 0:
            self.got = [self.swap(self.send, "grp", 1)]
        elif stage <= 2:
            self.keep, self.got = done[1], [self.across(done[0], stage - 1)]
        elif stage == 3:
            self.keep, self.got = done[0], [self.swap(done[k], "dp", k) for k in range(1, 4)]
        elif stage == 4:
            total = done[0]
            for axis, bit in (("grp", 8), ("dp", 4)):
                while bit < self.sizes[axis]:
                    total = total + self.swap(total, axis, bit)
                    bit *= 2
            self.keep, self.got = total, [self.swap(total, "dp", k) for k in range(1, 4)]
        elif stage == 5:
            self.own = done[0]
            self.second, self.first = self.across(self.own, 1), self.across(self.own, 0)
            self.pieces = [self.own, self.second, self.first, None, self.swap(self.own, "grp", 1)]
        elif stage == 6:
            self.pieces[3] = self.across(self.second, 0)
            self.pieces += [self.swap(self.second, "grp", 1), self.swap(self.first, "grp", 1)]
        else:
            self.pieces.append(self.swap(self.pieces[3], "grp", 1))


class Order:
    def __init__(self):
        self.after = []

    def step(self, *rounds, new=None):
        tasks = [item.tasks() for item in rounds]
        flat = sum(tasks, [])
        if flat:
            done, through = combine(flat, self.after, [new.send] if new else [])
            for item, own in zip(rounds, tasks):
                item.launch([x for result in done[: len(own)] for x in result])
                if own:
                    self.after = [done[0][0]]
                done = done[len(own) :]
            if new:
                new.send = through[0]
        else:
            for item in rounds:
                item.launch([])
        if new:
            new.launch([])


def place(me, pieces, parts, shapes, before, after, small=()):
    names = sorted({name for name, _ in parts} | ({"out"} if "qkv" in dict(parts) else set()))
    old = [name for name in names if name in before]
    width = shapes["out"][-1]
    rows = width // 8
    count = len(pieces)

    def body(me, *refs):
        here = refs[:count]
        refs = refs[count + len(old) + len(after) :]
        outs = dict(zip(names, refs))
        smalls, (sems, *more) = refs[len(names) : len(names) + len(small)], refs[len(names) + len(small) :]
        waits = []
        if small:
            misc, tail_sems = more
            tail = MISC_ROWS // PIECES
            tails = []
            for r in range(PIECES):
                j = lax.bitwise_xor(me[r // HALF], jnp.int32(r % HALF))
                source = here[r // GROUP].at[r % GROUP, pl.ds(len(parts) * rows, tail)]
                item = pltpu.make_async_copy(source, misc.at[pl.ds(pl.multiple_of(j * tail, 8), tail)], tail_sems.at[r])
                item.start()
                tails.append(item)
        for index, (name, layer) in enumerate(parts):
            for r in range(PIECES):
                block, row = spot(me[r // HALF], r % HALF, rows)
                source = here[r // GROUP].at[r % GROUP, pl.ds(index * rows, rows)]
                sem = sems.at[index * PIECES + r]
                column = pl.ds(pl.multiple_of(block * width, 128), width)
                if name == "fc1":
                    item = pltpu.make_async_copy(source, outs[name].at[layer, pl.ds(row, rows), column], sem)
                    item.start()
                elif name == "fc2":
                    item = pltpu.make_async_copy(source, outs[name].at[layer, pl.ds(pl.multiple_of(block * width + row, 8), rows)], sem)
                    item.start()
                else:
                    item = pltpu.make_async_copy(source, outs["out"].at[layer, pl.ds(row, rows)], sem)

                    @pl.when(block < 3)
                    def _():
                        pltpu.make_async_copy(source, outs["qkv"].at[layer, pl.ds(row, rows), column], sem).start()

                    @pl.when(block == 3)
                    def _():
                        item.start()

                waits.append(item)
        if small:
            for item in tails:
                item.wait()
            gpos, ggain, gbias, gqvb, goutb, gb1, gb2 = smalls
            gpos[...] = misc[0 : gpos.shape[0], :]
            for index in range(ggain.shape[0]):
                base = MISC_BASE + MISC_LAYER * index
                ggain[index] = misc[base : base + 2, :]
                gbias[index] = misc[base + 2 : base + 4, :]
                gqvb[index] = misc[base + 4 : base + 6, :]
                goutb[index : index + 1, :] = misc[base + 6 : base + 7, :]
                for k in range(gb1.shape[1] // width):
                    gb1[index : index + 1, k * width : (k + 1) * width] = misc[base + 7 + k : base + 8 + k, :]
                gb2[index : index + 1, :] = misc[base + 11 : base + 12, :]
        for item in waits:
            item.wait()

    anywhere = pl.BlockSpec(memory_space=pl.ANY)
    vmem = pl.BlockSpec(memory_space=pltpu.VMEM)
    scratch = [pltpu.SemaphoreType.DMA((len(parts) * PIECES,))]
    if small:
        scratch += [pltpu.VMEM((MISC_ROWS, width), F32), pltpu.SemaphoreType.DMA((PIECES,))]
    out = pl.pallas_call(
        body,
        in_specs=[pl.BlockSpec(memory_space=pltpu.SMEM)] + [vmem] * count + [anywhere] * (len(old) + len(after)),
        out_specs=[anywhere] * len(names) + [vmem] * len(small),
        out_shape=[jax.ShapeDtypeStruct(shapes[name], F32) for name in names] + [jax.ShapeDtypeStruct(shape, F32) for shape in small],
        scratch_shapes=scratch,
        input_output_aliases={1 + count + index: names.index(name) for index, name in enumerate(old)},
        compiler_params=pltpu.CompilerParams(vmem_limit_bytes=VMEM_LIMIT),
        name="place",
    )(me, *pieces, *[before[name] for name in old], *after)
    return {**before, **dict(zip(names, out))}, list(out[len(names) :])


def on_device(sizes, tokens, kinds, interp, pos_base, ln_gain, ln_bias, w_qkv, qv_bias, w_out, out_bias, w_fc1, fc1_bias, w_fc2, fc2_bias, cotangent):
    count, rows, width = tokens.shape
    layers = w_qkv.shape[0]
    padded = -(-rows // 16) * 16
    per = 2 if count % 2 == 0 else 1
    g, d = lax.axis_index("grp"), lax.axis_index("dp")
    core, x, y = [lax.bitwise_and(lax.shift_right_logical(g, k), 1) for k in range(3)]
    low = lax.bitwise_and(d, 3)
    on_first, on_second = x * 8 + y * 4 + low, 16 + y * 8 + x * 4 + low
    me = jnp.where(core == 0, jnp.stack([on_first, on_second]), jnp.stack([on_second, on_first])).astype(jnp.int32)
    mixed, a, qkv, lse, o, c, gp, gh, xh1, r1, xh2, r2 = forward(
        kinds, tokens, interp, pos_base, ln_gain, ln_bias, w_qkv, qv_bias, w_out, out_bias, w_fc1, fc1_bias, w_fc2, fc2_bias, padded, per
    )
    small = (pos_base.shape, ln_gain.shape, ln_bias.shape, qv_bias.shape, out_bias.shape, fc1_bias.shape, fc2_bias.shape)
    shapes = {"fc1": w_fc1.shape, "fc2": w_fc2.shape, "qkv": w_qkv.shape, "out": w_out.shape}
    top = layers - 1

    def mlp(layer, dx, after):
        return mlp_back(layer, layer == top, kinds, me, dx, c, gh, gp, xh2, r2, ln_gain, w_fc1, w_fc2, padded, per, after)

    def attention(layer, dmid, sums, after):
        return attn_back(
            layer, layer == 0, kinds, me, dmid, o, qkv, lse, a, xh1, r1, ln_gain, w_qkv, w_out, gh, interp, tokens, sums, padded, per, after
        )

    order = Order()
    step = order.step
    parts = ((("fc1", 1), ("fc2", 1)), (("qkv", 1), ("fc2", 0)), (("fc1", 0),), (("qkv", 0),))
    done = {}
    rest = ()
    dmid, keep, send, sums1 = mlp(1, cotangent, [])
    order.after = [sums1]
    q0 = Round(keep, send, sizes)
    step(q0)
    step(q0)
    dx, keep, send, sums2 = attention(1, dmid, [], order.after)
    order.after = [sums2]
    q1 = Round(keep, send, sizes)
    step(q0, new=q1)
    dmid, keep, send, sums0 = mlp(0, dx, order.after)
    order.after = [sums0]
    q2 = Round(keep, send, sizes)
    step(q1, q0, new=q2)
    dx, keep, send = attention(0, dmid, [sums0, sums1, sums2], order.after)
    order.after = [keep]
    q3 = Round(keep, send, sizes)
    step(q1, q2, new=q3)
    step(q3)
    step(q1)
    step(q2, q3)
    upper = q0.merge(q1)
    step(upper)
    lower = q2.merge(q3)
    step(lower)
    step(upper)
    step(lower)
    step(upper)
    step(upper)
    step(lower)
    done, _ = place(me, upper.pieces, (("fc1", 1), ("fc2", 1), ("qkv", 1), ("fc2", 0)), shapes, {}, order.after)
    step(lower)
    step(lower)
    done, rest = place(me, lower.pieces, (("fc1", 0), ("qkv", 0)), shapes, done, [], small)
    gpos, ggain, gbias, gqvb, goutb, gb1, gb2 = rest
    return mixed, dx, gpos, ggain, gbias, done["qkv"], gqvb, done["out"], goutb, done["fc1"], gb1, done["fc2"], gb2


def solution(mesh):
    split = P(("grp", "dp"), None, None)
    return jax.shard_map(
        partial(on_device, dict(mesh.shape)),
        mesh=mesh,
        in_specs=(split, P(("grp", "dp"))) + (P(),) * 12 + (split,),
        out_specs=(split, split) + (P(),) * 11,
        check_vma=False,
    )
```

time: 348 us -> 314 us (0.902)
  waiting for transfers between devices: 127 us -> 95.6 us
  starting transfers between devices: 75.1 us -> 45.2 us
  Pallas kernels: 130 us -> 157 us
  local copies, waits for them, and re-layouts: 2.03 us -> 13.8 us
  other arithmetic: 11.2 us -> 0.61 us
    ppermute x80 -> x27, waiting for transfers between devices: 127 us -> 55.6 us  [exchange(): return lax.ppermute(x, axis, [(i, i ^ bits) for i in range(size)])]
    ppermute x80 -> x27, starting transfers between devices: 75.1 us -> 28 us  [exchange(): return lax.ppermute(x, axis, [(i, i ^ bits) for i in range(size)])]
    ppermute x0 -> x14, waiting for transfers between devices: none -> 40 us  [across(): lax.ppermute(x, 'grp', [(i, i ^ bits(i)) for i in range(self.sizes['grp'])])]
    pallas_call x4 -> x14, Pallas kernels: 21.1 us -> 48.2 us  [the longest x12 32.9 us: combine(): pl.pallas_call(body, in_specs=[vmem] * len(args) + [anywhere] * (len(thro...]
    ppermute x0 -> x14, starting transfers between devices: none -> 17.2 us  [across(): lax.ppermute(x, 'grp', [(i, i ^ bits(i)) for i in range(self.sizes['grp'])])]
    unnamed x94 -> x80, local copies, waits for them, and re-layouts: 1.93 us -> 13.8 us
    add x28 -> x0, other arithmetic: 10.1 us -> none  [the longest x8 4.08 us: advance(): keep + got]
    pallas_call x2, Pallas kernels: 34.7 us -> 30.9 us  [mlp_back(): pl.pallas_call(drop(mlp_back_kernel, (top,), 11, len(after)), grid_spec=p...]
  transfers between devices with their start and end apart: 80 -> 41, of which waited for: 31 -> 15; matrix products, arithmetic and copies ran while one was open for 3% -> 0% of each run, Pallas kernels for 21% -> 25%
where the time goes in v1:
time: 314 us; the launch traced here: 313 us
  Pallas kernels  157 us (50%)
  waiting for transfers between devices  95.6 us (30%)
  starting transfers between devices  45.2 us (14%)
  local copies, waits for them, and re-layouts  13.8 us (4%)
    ppermute x27, waiting for transfers between devices, exchange(): return lax.ppermute(x, axis, [(i, i ^ bits) for i in range(size)])  55.6 us
    pallas_call x2, Pallas kernels, attn_back(): pl.pallas_call(drop(attn_back_kernel, (bottom, layers), first, len(after)...  43.6 us
    ppermute x14, waiting for transfers between devices, across(): lax.ppermute(x, 'grp', [(i, i ^ bits(i)) for i in range(self.sizes['grp'])])  40 us
    pallas_call x1, Pallas kernels, forward(): pl.pallas_call(fwd_kernel, grid_spec=pltpu.PrefetchScalarGridSpec(num_sca...  33.9 us
    pallas_call x12, Pallas kernels, combine(): pl.pallas_call(body, in_specs=[vmem] * len(args) + [anywhere] * (len(thro...  32.9 us
    pallas_call x2, Pallas kernels, mlp_back(): pl.pallas_call(drop(mlp_back_kernel, (top,), 11, len(after)), grid_spec=p...  30.9 us
    ppermute x27, starting transfers between devices, exchange(): return lax.ppermute(x, axis, [(i, i ^ bits) for i in range(size)])  28 us
    ppermute x14, starting transfers between devices, across(): lax.ppermute(x, 'grp', [(i, i ^ bits(i)) for i in range(self.sizes['grp'])])  17.2 us
  transfers between devices with their start and end apart: 41, of which 15 were waited for; matrix products, arithmetic and copies ran while one was open for 0% of the time, Pallas kernels for 25%

profile of v1, /device:TPU:0, one launch (start us, length us, event | category | flops | bytes accessed | tf_op | source)
XLA Modules:
  0.0 313.0 jit_solution(16394266469322251790)
XLA Ops:
  1.3 33.9 %encoder_forward.1 = (bf16[6,197,384]{2,1,0:T(8,128)(2,1)}, bf16[2,1248,384]{2,1,0:T(8,128)(2,1)}, bf16[2,1248,1152]{2,1,0:T(8,128)(2,1)}, f32[2,6,8,208]{3,2,1,...) custom-call(s32[6]{0:T(128)} %refs_0_.7, ...), custom_call_target="tpu_custom_call" | custom-call | tf_op jit(solution)/shard_map/encoder_forward/pallas_call | solution.py:181
  35.2 17.5 %mlp_backward.2 = (f32[1248,384]{1,0:T(8,128)}, f32[16,96,384]{2,1,0:T(8,128)}, f32[16,96,384]{2,1,0:T(8,128)}, f32[16,384]{1,0:T(8,128)}) custom-call(s32[6]{0:T(128)} %refs_0_.7, s32[2]{0:T(128)} %broadcast_select_fusion.refs_1_.me, bf16[6,197,384]{2,1,0:T(8,128)(2,1)} %refs_2_.1, bf16[2,1248,384]{2,1,0:T(8,128)(2,1)} %get-tuple-element.86.refs_3_, ...), custom_call_target="tpu_custom_call" | custom-call | flops 5888802816 | bytes 14376960 | tf_op jit(solution)/shard_map/mlp_backward/pallas_call | solution.py:350
  53.2 4.4 %collective-permute-done.refs_1_ = f32[16,96,384]{2,1,0:T(8,128)S(1)} collective-permute-done((f32[16,96,384]{2,1,0:T(8,128)}, f32[16,96,384]{2,1,0:T(8,128)S(1)}, u32[]{:S(2)}, u32[]{:S(2)}) %collective-permute-start) | collective-permute-done | bytes 2359328 | tf_op jit(solution)/shard_map/ppermute | solution.py:545
  57.6 1.4 copy-done.1
  59.0 3.9 %combine.12 = (f32[8,96,384]{2,1,0:T(8,128)}, f32[8,96,384]{2,1,0:T(8,128)}) custom-call(f32[16,96,384]{2,1,0:T(8,128)} %get-tuple-element.98.refs_0_, f32[16,96,384]{2,1,0:T(8,128)} %copy-done.1, f32[16,384]{1,0:T(8,128)} %get-tuple-element.100.refs_2_.refs_14_), custom_call_target="tpu_custom_call" | custom-call | flops 4718592 | bytes 9437184 | tf_op jit(solution)/shard_map/combine/pallas_call | solution.py:561
  62.9 2.9 collective-permute-start.1
  65.7 23.6 %attention_backward.2 = (f32[1248,384]{1,0:T(8,128)}, f32[16,96,384]{2,1,0:T(8,128)}, f32[16,96,384]{2,1,0:T(8,128)}, f32[16,384]{1,0:T(8,128)}) custom-call(s32[6]{0:T(128)} %refs_0_.7, s32[2]{0:T(128)} %broadcast_select_fusion.refs_1_.me, f32[1248,384]{1,0:T(8,128)} %get-tuple-element.91.refs_2_, bf16[2,1248,384]{2,1,0:T(8,128)(2,1)} %get-tuple-element.92.refs_3_, ...), custom_call_target="tpu_custom_call" | custom-call | flops 5888802816 | bytes 14376960 | tf_op jit(solution)/shard_map/attention_backward/pallas_call | solution.py:528
  89.3 1.0 copy-done.12
  90.3 2.7 combine.13
  93.1 1.5 collective-permute-start.3
  94.6 13.4 %mlp_backward.3 = (f32[1248,384]{1,0:T(8,128)}, f32[16,48,384]{2,1,0:T(8,128)}, f32[16,48,384]{2,1,0:T(8,128)}, f32[16,384]{1,0:T(8,128)}) custom-call(s32[6]{0:T(128)} %refs_0_.7, s32[2]{0:T(128)} %broadcast_select_fusion.refs_1_.me, f32[1248,384]{1,0:T(8,128)} %get-tuple-element.102.refs_2_, bf16[2,1248,384]{2,1,0:T(8,128)(2,1)} %get-tuple-element.86.refs_3_, ...), custom_call_target="tpu_custom_call" | custom-call | flops 5888802816 | bytes 14376960 | tf_op jit(solution)/shard_map/mlp_backward/pallas_call | solution.py:350
  108.0 0.8 copy-done.18
  108.8 0.8 copy-done.2
  109.6 4.4 %combine.14 = (f32[8,96,384]{2,1,0:T(8,128)}, f32[8,96,384]{2,1,0:T(8,128)}, f32[96,384]{1,0:T(8,128)}, f32[96,384]{1,0:T(8,128)}, f32[96,384]{1,0:T(8,128)}, /*index=5*/f32[96,384]{1,0:T(8,128)}, f32[16,48,384]{2,1,0:T(8,128)}) custom-call(f32[16,96,384]{2,1,0:T(8,128)} %get-tuple-element.109.refs_0_, ...), custom_call_target="tpu_custom_call", output_to_operand_aliasing={{6}: (4, {})} | custom-call | flops 5898240 | bytes 11796480 | tf_op jit(solution)/shard_map/combine/pallas_call | solution.py:561
  114.5 20.0 %attention_backward.3 = (f32[6,197,384]{2,1,0:T(8,128)}, f32[16,56,384]{2,1,0:T(8,128)}, f32[16,56,384]{2,1,0:T(8,128)}) custom-call(s32[6]{0:T(128)} %refs_0_.7, s32[2]{0:T(128)} %broadcast_select_fusion.refs_1_.me, f32[1248,384]{1,0:T(8,128)} %get-tuple-element.107.refs_2_, bf16[2,1248,384]{2,1,0:T(8,128)(2,1)} %get-tuple-element.92.refs_3_, ...), custom_call_target="tpu_custom_call" | custom-call | flops 5888802816 | bytes 14376960 | tf_op jit(solution)/shard_map/attention_backward/pallas_call | solution.py:528
  134.6 1.0 copy-done.10
  136.0 3.8 %combine.15 = (f32[4,96,384]{2,1,0:T(8,128)}, f32[4,96,384]{2,1,0:T(8,128)}, f32[8,48,384]{2,1,0:T(8,128)}, f32[8,48,384]{2,1,0:T(8,128)}, f32[16,56,384]{2,1,0:T(8,128)}) custom-call(f32[8,96,384]{2,1,0:T(8,128)} %get-tuple-element.115.refs_0_, f32[8,96,384]{2,1,0:T(8,128)} %copy-done.10, ...), custom_call_target="tpu_custom_call", output_to_operand_aliasing={{4}: (4, {})} | custom-call | flops 4718592 | bytes 9437184 | tf_op jit(solution)/shard_map/combine/pallas_call | solution.py:561
  140.4 3.0 collective-permute-done.7.refs_1_
  143.3 1.1 copy-done.3
  144.4 2.9 combine.16
  147.3 1.5 collective-permute-start.8
  149.3 1.4 collective-permute-start.6
  150.7 1.6 collective-permute-start.12
  152.2 2.6 collective-permute-start.13
  154.9 10.2 %collective-permute-done.9.refs_1_ = f32[4,96,384]{2,1,0:T(8,128)S(1)} collective-permute-done((f32[4,96,384]{2,1,0:T(8,128)S(1)}, f32[4,96,384]{2,1,0:T(8,128)S(1)}, u32[]{:S(2)}, u32[]{:S(2)}) %collective-permute-start.9) | collective-permute-done | bytes 589856 | tf_op jit(solution)/shard_map/ppermute | solution.py:621
  165.0 3.6 %collective-permute-start.14 = (f32[96,384]{1,0:T(8,128)S(1)}, f32[96,384]{1,0:T(8,128)S(1)}, u32[]{:S(2)}, u32[]{:S(2)}) collective-permute-start(f32[96,384]{1,0:T(8,128)S(1)} %copy-done.37), channel_id=1, source_target_pairs={{0,3},{1,2},{2,1},{3,0},{4,7},{5,6},{6,5},{7,4},{8,11},{9,10},{10,... | collective-permute-start | bytes 442376 | tf_op jit(solution)/shard_map/ppermute | solution.py:545
  168.7 2.1 combine.17
  171.1 2.6 collective-permute-start.16
  173.7 1.5 collective-permute-start.17
  175.2 2.7 combine.18
  178.0 0.8 collective-permute-start.11
  178.8 1.3 collective-permute-start.10
  180.1 5.0 %collective-permute-done.16.refs_6_ = f32[96,384]{1,0:T(8,128)S(1)} collective-permute-done((f32[96,384]{1,0:T(8,128)}, f32[96,384]{1,0:T(8,128)S(1)}, u32[]{:S(2)}, u32[]{:S(2)}) %collective-permute-start.16) | collective-permute-done | bytes 147488 | tf_op jit(solution)/shard_map/ppermute | solution.py:545
  186.4 2.1 combine.19.refs_4_.refs_0_
  188.5 3.1 collective-permute-start.23
  191.6 0.9 collective-permute-start.22
  193.8 2.1 combine.20
  195.9 4.0 %collective-permute-done.23.refs_3_ = f32[192,384]{1,0:T(8,128)S(1)} collective-permute-done((f32[192,384]{1,0:T(8,128)}, f32[192,384]{1,0:T(8,128)S(1)}, u32[]{:S(2)}, u32[]{:S(2)}) %collective-permute-start.23) | collective-permute-done | bytes 294944 | tf_op jit(solution)/shard_map/ppermute | solution.py:545
  199.9 16.5 %collective-permute-done.22.refs_2_ = f32[192,384]{1,0:T(8,128)S(1)} collective-permute-done((f32[192,384]{1,0:T(8,128)}, f32[192,384]{1,0:T(8,128)S(1)}, u32[]{:S(2)}, u32[]{:S(2)}) %collective-permute-start.22) | collective-permute-done | bytes 294944 | tf_op jit(solution)/shard_map/ppermute | solution.py:545
  216.5 0.7 copy-done.21
  217.3 2.3 combine.21.refs_4_.refs_0_
  219.6 2.0 collective-permute-start.34
  221.7 0.8 collective-permute-start.18
  222.5 3.3 %collective-permute-start.19 = (f32[104,384]{1,0:T(8,128)}, f32[104,384]{1,0:T(8,128)S(1)}, u32[]{:S(2)}, u32[]{:S(2)}) collective-permute-start(f32[104,384]{1,0:T(8,128)} %get-tuple-element.141), channel_id=1, source_target_pairs={{0,2},{1,3},{2,0},{3,1},{4,6},{5,7},{6,4},{7,5},{8,10},{9,11},{10,... | collective-permute-start | bytes 479240 | tf_op jit(solution)/shard_map/ppermute | solution.py:545
  226.1 4.3 %collective-permute-done.18.refs_1_ = f32[104,384]{1,0:T(8,128)S(1)} collective-permute-done((f32[104,384]{1,0:T(8,128)}, f32[104,384]{1,0:T(8,128)S(1)}, u32[]{:S(2)}, u32[]{:S(2)}) %collective-permute-start.18) | collective-permute-done | bytes 159776 | tf_op jit(solution)/shard_map/ppermute | solution.py:545
  230.3 7.5 %collective-permute-done.19.refs_2_ = f32[104,384]{1,0:T(8,128)S(1)} collective-permute-done((f32[104,384]{1,0:T(8,128)}, f32[104,384]{1,0:T(8,128)S(1)}, u32[]{:S(2)}, u32[]{:S(2)}) %collective-permute-start.19) | collective-permute-done | bytes 159776 | tf_op jit(solution)/shard_map/ppermute | solution.py:545
  239.2 1.8 combine.22.refs_0_.refs_4_
  241.0 2.4 collective-permute-start.26
  243.4 1.2 collective-permute-start.25
  244.6 0.8 collective-permute-start.24
  245.4 4.7 %collective-permute-done.26.refs_3_ = f32[104,384]{1,0:T(8,128)S(1)} collective-permute-done((f32[104,384]{1,0:T(8,128)}, f32[104,384]{1,0:T(8,128)S(1)}, u32[]{:S(2)}, u32[]{:S(2)}) %collective-permute-start.26) | collective-permute-done | bytes 159776 | tf_op jit(solution)/shard_map/ppermute | solution.py:545
  250.1 6.3 %collective-permute-done.25.refs_2_ = f32[104,384]{1,0:T(8,128)S(1)} collective-permute-done((f32[104,384]{1,0:T(8,128)}, f32[104,384]{1,0:T(8,128)S(1)}, u32[]{:S(2)}, u32[]{:S(2)}) %collective-permute-start.25) | collective-permute-done | bytes 159776 | tf_op jit(solution)/shard_map/ppermute | solution.py:545
  257.7 2.0 combine.23.refs_8_.refs_0_
  259.7 1.3 collective-permute-start.28
  261.0 0.7 collective-permute-start.36
  261.7 1.4 collective-permute-start.27
  263.7 11.9 %collective-permute-done.28.refs_2_ = f32[4,104,384]{2,1,0:T(8,128)} collective-permute-done((f32[4,104,384]{2,1,0:T(8,128)}, f32[4,104,384]{2,1,0:T(8,128)}, u32[]{:S(2)}, u32[]{:S(2)}) %collective-permute-start.28) | collective-permute-done | bytes 639008 | tf_op jit(solution)/shard_map/ppermute | solution.py:621
  275.6 3.8 %collective-permute-done.27.refs_1_ = f32[4,104,384]{2,1,0:T(8,128)} collective-permute-done((f32[4,104,384]{2,1,0:T(8,128)}, f32[4,104,384]{2,1,0:T(8,128)}, u32[]{:S(2)}, u32[]{:S(2)}) %collective-permute-start.27) | collective-permute-done | bytes 639008 | tf_op jit(solution)/shard_map/ppermute | solution.py:621
  279.4 1.3 collective-permute-start.29
  280.7 7.4 %collective-permute-done.36.refs_3_ = f32[4,192,384]{2,1,0:T(8,128)S(1)} collective-permute-done((f32[4,192,384]{2,1,0:T(8,128)S(1)}, f32[4,192,384]{2,1,0:T(8,128)S(1)}, u32[]{:S(2)}, u32[]{:S(2)}) %collective-permute-start.36) | collective-permute-done | bytes 1179680 | tf_op jit(solution)/shard_map/ppermute | solution.py:621
  288.6 6.4 %collective-permute-done.29.refs_3_ = f32[4,104,384]{2,1,0:T(8,128)} collective-permute-done((f32[4,104,384]{2,1,0:T(8,128)}, f32[4,104,384]{2,1,0:T(8,128)}, u32[]{:S(2)}, u32[]{:S(2)}) %collective-permute-start.29) | collective-permute-done | bytes 639008 | tf_op jit(solution)/shard_map/ppermute | solution.py:621
  296.6 8.4 %place.2 = (f32[2,384,1536]{2,1,0:T(8,128)}, f32[2,1536,384]{2,1,0:T(8,128)}, f32[2,384,384]{2,1,0:T(8,128)}, f32[2,384,1152]{2,1,0:T(8,128)}) custom-call(s32[2]{0:T(128)} %broadcast_select_fusion.refs_1_.me, f32[4,192,384]{2,1,0:T(8,128)} %combine.21.refs_4_.refs_0_, f32[4,192,384]{2,1,0:T(8,128)} %copy-done.4, f32[4,192,384]{2,1,0:T(8,128)} %copy-done.5, ...), custom_call_target="tpu_custom_call" | custom-call | tf_op jit(solution)/shard_map/place/pallas_call | solution.py:759
  305.1 0.8 copy-done.14
  305.9 6.9 %place.3 = (f32[2,384,1536]{2,1,0:T(8,128)}, f32[2,384,384]{2,1,0:T(8,128)}, f32[2,384,1152]{2,1,0:T(8,128)}, f32[197,384]{1,0:T(8,128)}, f32[2,2,384]{2,1,0:T(2...) custom-call(s32[2]{0:T(128)} %broadcast_select_fusion.refs_1_.me, ...), custom_call_target="tpu_custom_call", output_to_operand_aliasing={{0}: (9, {}), {1}: (10, {}), {2}: (11, {})} | custom-call | tf_op jit(solution)/shard_map/place/pallas_call | solution.py:759
  (118 shorter events, 12.0 us)
Async XLA Ops:
  52.7 4.9 %collective-permute-start = (f32[16,96,384]{2,1,0:T(8,128)}, f32[16,96,384]{2,1,0:T(8,128)S(1)}, u32[]{:S(2)}, u32[]{:S(2)}) collective-permute-start(f32[16,96,384]{2,1,0:T(8,128)} %get-tuple-element.99), channel_id=1, source_target_pairs={{0,4},{4,0},{8,12},{12,8},{16,20},{20,16},{24,28},{28,24},{1,5},{5... | collective-permute-start | bytes 7077896 | tf_op jit(solution)/shard_map/ppermute | solution.py:545
  57.6 1.4 copy-start.1
  62.9 26.4 %collective-permute-start.1 = (f32[8,96,384]{2,1,0:T(8,128)}, f32[8,96,384]{2,1,0:T(8,128)S(1)}, u32[]{:S(2)}, u32[]{:S(2)}) collective-permute-start(f32[8,96,384]{2,1,0:T(8,128)} %get-tuple-element.101.refs_13_), channel_id=1, source_target_pairs={{0,8},{4,20},{8,0},{12,28},{16,24},{20,4},{24,16},{28,12},{1,9},{5... | collective-permute-start | bytes 3538952 | tf_op jit(solution)/shard_map/ppermute | solution.py:621
  93.1 14.9 %collective-permute-start.2 = (f32[16,96,384]{2,1,0:T(8,128)}, f32[16,96,384]{2,1,0:T(8,128)S(1)}, u32[]{:S(2)}, u32[]{:S(2)}) collective-permute-start(f32[16,96,384]{2,1,0:T(8,128)} %get-tuple-element.110), channel_id=1, source_target_pairs={{0,4},{4,0},{8,12},{12,8},{16,20},{20,16},{24,28},{28,24},{1,5},{5... | collective-permute-start | bytes 7077896 | tf_op jit(solution)/shard_map/ppermute | solution.py:545
  93.1 14.9 %collective-permute-start.3 = (f32[4,96,384]{2,1,0:T(8,128)}, f32[4,96,384]{2,1,0:T(8,128)S(1)}, u32[]{:S(2)}, u32[]{:S(2)}) collective-permute-start(f32[4,96,384]{2,1,0:T(8,128)} %get-tuple-element.106.refs_11_), channel_id=1, source_target_pairs={{0,16},{4,12},{8,24},{12,4},{16,0},{20,28},{24,8},{28,20},{1,17},{... | collective-permute-start | bytes 1769480 | tf_op jit(solution)/shard_map/ppermute | solution.py:621
  108.0 1.6 copy-start.2
  113.9 20.6 %collective-permute-start.4 = (f32[8,96,384]{2,1,0:T(8,128)}, f32[8,96,384]{2,1,0:T(8,128)S(1)}, u32[]{:S(2)}, u32[]{:S(2)}) collective-permute-start(f32[8,96,384]{2,1,0:T(8,128)} %get-tuple-element.116), channel_id=1, source_target_pairs={{0,8},{4,20},{8,0},{12,28},{16,24},{20,4},{24,16},{28,12},{1,9},{5... | collective-permute-start | bytes 3538952 | tf_op jit(solution)/shard_map/ppermute | solution.py:621
  114.5 20.1 %collective-permute-start.5 = (f32[16,48,384]{2,1,0:T(8,128)}, f32[16,48,384]{2,1,0:T(8,128)S(1)}, u32[]{:S(2)}, u32[]{:S(2)}) collective-permute-start(f32[16,48,384]{2,1,0:T(8,128)} %get-tuple-element.118), channel_id=1, source_target_pairs={{0,4},{4,0},{8,12},{12,8},{16,20},{20,16},{24,28},{28,24},{1,5},{5... | collective-permute-start | bytes 3538952 | tf_op jit(solution)/shard_map/ppermute | solution.py:545
  134.6 1.4 copy-start.11
  139.8 9.0 %copy-start.36 = (f32[4,96,384]{2,1,0:T(8,128)S(1)}, f32[4,96,384]{2,1,0:T(8,128)}, u32[]{:S(2)}) copy-start(f32[4,96,384]{2,1,0:T(8,128)} %get-tuple-element.127) | copy-start | bytes 1769476
  139.8 9.5 %copy-start.15 = (f32[8,48,384]{2,1,0:T(8,128)S(1)}, f32[8,48,384]{2,1,0:T(8,128)}, u32[]{:S(2)}) copy-start(f32[8,48,384]{2,1,0:T(8,128)} %get-tuple-element.122.refs_2_) | copy-start | bytes 1769476
  139.8 10.9 %copy-start.39 = (f32[96,384]{1,0:T(8,128)S(1)}, f32[96,384]{1,0:T(8,128)}, u32[]{:S(2)}) copy-start(f32[96,384]{1,0:T(8,128)} %get-tuple-element.133) | copy-start | bytes 442372
  139.8 12.5 %copy-start.38 = (f32[96,384]{1,0:T(8,128)S(1)}, f32[96,384]{1,0:T(8,128)}, u32[]{:S(2)}) copy-start(f32[96,384]{1,0:T(8,128)} %get-tuple-element.134) | copy-start | bytes 442372
  139.8 25.3 %copy-start.37 = (f32[96,384]{1,0:T(8,128)S(1)}, f32[96,384]{1,0:T(8,128)}, u32[]{:S(2)}) copy-start(f32[96,384]{1,0:T(8,128)} %get-tuple-element.135) | copy-start | bytes 442372
  139.8 3.5 %collective-permute-start.7 = (f32[16,56,384]{2,1,0:T(8,128)}, f32[16,56,384]{2,1,0:T(8,128)S(1)}, u32[]{:S(2)}, u32[]{:S(2)}) collective-permute-start(f32[16,56,384]{2,1,0:T(8,128)} %get-tuple-element.123), channel_id=1, source_target_pairs={{0,4},{4,0},{8,12},{12,8},{16,20},{20,16},{24,28},{28,24},{1,5},{5... | collective-permute-start | bytes 4128776 | tf_op jit(solution)/shard_map/ppermute | solution.py:545
  147.3 26.4 %collective-permute-start.8 = (f32[8,56,384]{2,1,0:T(8,128)}, f32[8,56,384]{2,1,0:T(8,128)S(1)}, u32[]{:S(2)}, u32[]{:S(2)}) collective-permute-start(f32[8,56,384]{2,1,0:T(8,128)} %get-tuple-element.125.refs_2_), channel_id=1, source_target_pairs={{0,8},{4,20},{8,0},{12,28},{16,24},{20,4},{24,16},{28,12},{1,9},{5... | collective-permute-start | bytes 2064392 | tf_op jit(solution)/shard_map/ppermute | solution.py:621
  148.8 16.3 %collective-permute-start.9 = (f32[4,96,384]{2,1,0:T(8,128)S(1)}, f32[4,96,384]{2,1,0:T(8,128)S(1)}, u32[]{:S(2)}, u32[]{:S(2)}) collective-permute-start(f32[4,96,384]{2,1,0:T(8,128)S(1)} %copy-done.36), channel_id=1, source_target_pairs={{0,16},{4,12},{8,24},{12,4},{16,0},{20,28},{24,8},{28,20},{1,17},{... | collective-permute-start | bytes 1769480 | tf_op jit(solution)/shard_map/ppermute | solution.py:621
  149.3 21.8 %collective-permute-start.6 = (f32[8,48,384]{2,1,0:T(8,128)S(1)}, f32[8,48,384]{2,1,0:T(8,128)S(1)}, u32[]{:S(2)}, u32[]{:S(2)}) collective-permute-start(f32[8,48,384]{2,1,0:T(8,128)S(1)} %copy-done.15), channel_id=1, source_target_pairs={{0,8},{4,20},{8,0},{12,28},{16,24},{20,4},{24,16},{28,12},{1,9},{5... | collective-permute-start | bytes 1769480 | tf_op jit(solution)/shard_map/ppermute | solution.py:621
  150.7 20.1 %collective-permute-start.12 = (f32[96,384]{1,0:T(8,128)S(1)}, f32[96,384]{1,0:T(8,128)S(1)}, u32[]{:S(2)}, u32[]{:S(2)}) collective-permute-start(f32[96,384]{1,0:T(8,128)S(1)} %copy-done.39), channel_id=1, source_target_pairs={{0,1},{1,0},{2,3},{3,2},{4,5},{5,4},{6,7},{7,6},{8,9},{9,8},{10,11... | collective-permute-start | bytes 442376 | tf_op jit(solution)/shard_map/ppermute | solution.py:545
  152.2 25.7 %collective-permute-start.13 = (f32[96,384]{1,0:T(8,128)S(1)}, f32[96,384]{1,0:T(8,128)S(1)}, u32[]{:S(2)}, u32[]{:S(2)}) collective-permute-start(f32[96,384]{1,0:T(8,128)S(1)} %copy-done.38), channel_id=1, source_target_pairs={{0,2},{1,3},{2,0},{3,1},{4,6},{5,7},{6,4},{7,5},{8,10},{9,11},{10,... | collective-permute-start | bytes 442376 | tf_op jit(solution)/shard_map/ppermute | solution.py:545
  165.0 3.6 %copy-start.16 = (f32[4,96,384]{2,1,0:T(8,128)}, f32[4,96,384]{2,1,0:T(8,128)S(1)}, u32[]{:S(2)}) copy-start(f32[4,96,384]{2,1,0:T(8,128)S(1)} %collective-permute-done.9.refs_1_) | copy-start | bytes 1769476
  165.0 13.7 %collective-permute-start.14 = (f32[96,384]{1,0:T(8,128)S(1)}, f32[96,384]{1,0:T(8,128)S(1)}, u32[]{:S(2)}, u32[]{:S(2)}) collective-permute-start(f32[96,384]{1,0:T(8,128)S(1)} %copy-done.37), channel_id=1, source_target_pairs={{0,3},{1,2},{2,1},{3,0},{4,7},{5,6},{6,5},{7,4},{8,11},{9,10},{10,... | collective-permute-start | bytes 442376 | tf_op jit(solution)/shard_map/ppermute | solution.py:545
  170.8 14.3 %copy-start.30 = (f32[96,384]{1,0:T(8,128)}, f32[96,384]{1,0:T(8,128)S(1)}, u32[]{:S(2)}) copy-start(f32[96,384]{1,0:T(8,128)S(1)} %collective-permute-done.12.refs_1_) | copy-start | bytes 442372
  170.8 9.3 %collective-permute-start.15 = (f32[96,384]{1,0:T(8,128)}, f32[96,384]{1,0:T(8,128)S(1)}, u32[]{:S(2)}, u32[]{:S(2)}) collective-permute-start(f32[96,384]{1,0:T(8,128)} %get-tuple-element.136), channel_id=1, source_target_pairs={{0,1},{1,0},{2,3},{3,2},{4,5},{5,4},{6,7},{7,6},{8,9},{9,8},{10,11... | collective-permute-start | bytes 442376 | tf_op jit(solution)/shard_map/ppermute | solution.py:545
  171.1 4.1 %copy-start.17 = (f32[8,48,384]{2,1,0:T(8,128)}, f32[8,48,384]{2,1,0:T(8,128)S(1)}, u32[]{:S(2)}) copy-start(f32[8,48,384]{2,1,0:T(8,128)S(1)} %collective-permute-done.6.refs_1_) | copy-start | bytes 1769476
  171.1 13.9 %collective-permute-start.16 = (f32[96,384]{1,0:T(8,128)}, f32[96,384]{1,0:T(8,128)S(1)}, u32[]{:S(2)}, u32[]{:S(2)}) collective-permute-start(f32[96,384]{1,0:T(8,128)} %get-tuple-element.137), channel_id=1, source_target_pairs={{0,2},{1,3},{2,0},{3,1},{4,6},{5,7},{6,4},{7,5},{8,10},{9,11},{10,... | collective-permute-start | bytes 442376 | tf_op jit(solution)/shard_map/ppermute | solution.py:545
  173.7 1.6 copy-start.13
  173.7 11.4 %collective-permute-start.17 = (f32[96,384]{1,0:T(8,128)}, f32[96,384]{1,0:T(8,128)S(1)}, u32[]{:S(2)}, u32[]{:S(2)}) collective-permute-start(f32[96,384]{1,0:T(8,128)} %get-tuple-element.138), channel_id=1, source_target_pairs={{0,3},{1,2},{2,1},{3,0},{4,7},{5,6},{6,5},{7,4},{8,11},{9,10},{10,... | collective-permute-start | bytes 442376 | tf_op jit(solution)/shard_map/ppermute | solution.py:545
  178.0 7.1 %copy-start.31 = (f32[96,384]{1,0:T(8,128)}, f32[96,384]{1,0:T(8,128)S(1)}, u32[]{:S(2)}) copy-start(f32[96,384]{1,0:T(8,128)S(1)} %collective-permute-done.13.refs_2_) | copy-start | bytes 442372
  178.0 15.0 %collective-permute-start.11 = (f32[4,56,384]{2,1,0:T(8,128)}, f32[4,56,384]{2,1,0:T(8,128)S(1)}, u32[]{:S(2)}, u32[]{:S(2)}) collective-permute-start(f32[4,56,384]{2,1,0:T(8,128)} %get-tuple-element.132.refs_8_), channel_id=1, source_target_pairs={{0,16},{4,12},{8,24},{12,4},{16,0},{20,28},{24,8},{28,20},{1,17},{... | collective-permute-start | bytes 1032200 | tf_op jit(solution)/shard_map/ppermute | solution.py:621
  178.8 6.3 %copy-start.32 = (f32[96,384]{1,0:T(8,128)}, f32[96,384]{1,0:T(8,128)S(1)}, u32[]{:S(2)}) copy-start(f32[96,384]{1,0:T(8,128)S(1)} %collective-permute-done.14.refs_3_) | copy-start | bytes 442372
  178.8 14.2 %collective-permute-start.10 = (f32[4,48,384]{2,1,0:T(8,128)}, f32[4,48,384]{2,1,0:T(8,128)S(1)}, u32[]{:S(2)}, u32[]{:S(2)}) collective-permute-start(f32[4,48,384]{2,1,0:T(8,128)} %get-tuple-element.130), channel_id=1, source_target_pairs={{0,16},{4,12},{8,24},{12,4},{16,0},{20,28},{24,8},{28,20},{1,17},{... | collective-permute-start | bytes 884744 | tf_op jit(solution)/shard_map/ppermute | solution.py:621
  180.1 5.0 %copy-start.33 = (f32[96,384]{1,0:T(8,128)}, f32[96,384]{1,0:T(8,128)S(1)}, u32[]{:S(2)}) copy-start(f32[96,384]{1,0:T(8,128)S(1)} %collective-permute-done.15.refs_5_) | copy-start | bytes 442372
  188.5 11.5 %collective-permute-start.23 = (f32[192,384]{1,0:T(8,128)}, f32[192,384]{1,0:T(8,128)S(1)}, u32[]{:S(2)}, u32[]{:S(2)}) collective-permute-start(f32[192,384]{1,0:T(8,128)} %combine.19.refs_4_.refs_0_), channel_id=1, source_target_pairs={{0,3},{1,2},{2,1},{3,0},{4,7},{5,6},{6,5},{7,4},{8,11},{9,10},{10,... | collective-permute-start | bytes 884744 | tf_op jit(solution)/shard_map/ppermute | solution.py:545
  191.6 24.9 %collective-permute-start.22 = (f32[192,384]{1,0:T(8,128)}, f32[192,384]{1,0:T(8,128)S(1)}, u32[]{:S(2)}, u32[]{:S(2)}) collective-permute-start(f32[192,384]{1,0:T(8,128)} %combine.19.refs_4_.refs_0_), channel_id=1, source_target_pairs={{0,2},{1,3},{2,0},{3,1},{4,6},{5,7},{6,4},{7,5},{8,10},{9,11},{10,... | collective-permute-start | bytes 884744 | tf_op jit(solution)/shard_map/ppermute | solution.py:545
  192.4 24.0 %collective-permute-start.21 = (f32[192,384]{1,0:T(8,128)}, f32[192,384]{1,0:T(8,128)S(1)}, u32[]{:S(2)}, u32[]{:S(2)}) collective-permute-start(f32[192,384]{1,0:T(8,128)} %combine.19.refs_4_.refs_0_), channel_id=1, source_target_pairs={{0,1},{1,0},{2,3},{3,2},{4,5},{5,4},{6,7},{7,6},{8,9},{9,8},{10,11... | collective-permute-start | bytes 884744 | tf_op jit(solution)/shard_map/ppermute | solution.py:545
  199.9 16.5 %copy-start.20 = (f32[192,384]{1,0:T(8,128)}, f32[192,384]{1,0:T(8,128)S(1)}, u32[]{:S(2)}) copy-start(f32[192,384]{1,0:T(8,128)S(1)} %collective-permute-done.23.refs_3_) | copy-start | bytes 884740
  219.6 43.6 %copy-start = (f32[4,192,384]{2,1,0:T(8,128)S(1)}, f32[4,192,384]{2,1,0:T(8,128)}, u32[]{:S(2)}) copy-start(f32[4,192,384]{2,1,0:T(8,128)} %combine.21.refs_4_.refs_0_) | copy-start | bytes 3538948
  219.6 41.4 %collective-permute-start.34 = (f32[4,192,384]{2,1,0:T(8,128)}, f32[4,192,384]{2,1,0:T(8,128)S(1)}, u32[]{:S(2)}, u32[]{:S(2)}) collective-permute-start(f32[4,192,384]{2,1,0:T(8,128)} %combine.21.refs_4_.refs_0_), channel_id=1, source_target_pairs={{0,16},{4,12},{8,24},{12,4},{16,0},{20,28},{24,8},{28,20},{1,17},{... | collective-permute-start | bytes 3538952 | tf_op jit(solution)/shard_map/ppermute | solution.py:621
  221.6 41.6 %collective-permute-start.35 = (f32[4,192,384]{2,1,0:T(8,128)}, f32[4,192,384]{2,1,0:T(8,128)S(1)}, u32[]{:S(2)}, u32[]{:S(2)}) collective-permute-start(f32[4,192,384]{2,1,0:T(8,128)} %combine.21.refs_4_.refs_0_), channel_id=1, source_target_pairs={{0,8},{4,20},{8,0},{12,28},{16,24},{20,4},{24,16},{28,12},{1,9},{5... | collective-permute-start | bytes 3538952 | tf_op jit(solution)/shard_map/ppermute | solution.py:621
  221.7 8.6 %collective-permute-start.18 = (f32[104,384]{1,0:T(8,128)}, f32[104,384]{1,0:T(8,128)S(1)}, u32[]{:S(2)}, u32[]{:S(2)}) collective-permute-start(f32[104,384]{1,0:T(8,128)} %get-tuple-element.140), channel_id=1, source_target_pairs={{0,1},{1,0},{2,3},{3,2},{4,5},{5,4},{6,7},{7,6},{8,9},{9,8},{10,11... | collective-permute-start | bytes 479240 | tf_op jit(solution)/shard_map/ppermute | solution.py:545
  222.5 15.3 %collective-permute-start.19 = (f32[104,384]{1,0:T(8,128)}, f32[104,384]{1,0:T(8,128)S(1)}, u32[]{:S(2)}, u32[]{:S(2)}) collective-permute-start(f32[104,384]{1,0:T(8,128)} %get-tuple-element.141), channel_id=1, source_target_pairs={{0,2},{1,3},{2,0},{3,1},{4,6},{5,7},{6,4},{7,5},{8,10},{9,11},{10,... | collective-permute-start | bytes 479240 | tf_op jit(solution)/shard_map/ppermute | solution.py:545
  225.8 12.1 %collective-permute-start.20 = (f32[104,384]{1,0:T(8,128)}, f32[104,384]{1,0:T(8,128)S(1)}, u32[]{:S(2)}, u32[]{:S(2)}) collective-permute-start(f32[104,384]{1,0:T(8,128)} %get-tuple-element.142), channel_id=1, source_target_pairs={{0,3},{1,2},{2,1},{3,0},{4,7},{5,6},{6,5},{7,4},{8,11},{9,10},{10,... | collective-permute-start | bytes 479240 | tf_op jit(solution)/shard_map/ppermute | solution.py:545
  230.3 7.5 %copy-start.24 = (f32[104,384]{1,0:T(8,128)}, f32[104,384]{1,0:T(8,128)S(1)}, u32[]{:S(2)}) copy-start(f32[104,384]{1,0:T(8,128)S(1)} %collective-permute-done.18.refs_1_) | copy-start | bytes 479236
  241.0 9.0 %collective-permute-start.26 = (f32[104,384]{1,0:T(8,128)}, f32[104,384]{1,0:T(8,128)S(1)}, u32[]{:S(2)}, u32[]{:S(2)}) collective-permute-start(f32[104,384]{1,0:T(8,128)} %combine.22.refs_0_.refs_4_), channel_id=1, source_target_pairs={{0,3},{1,2},{2,1},{3,0},{4,7},{5,6},{6,5},{7,4},{8,11},{9,10},{10,... | collective-permute-start | bytes 479240 | tf_op jit(solution)/shard_map/ppermute | solution.py:545
  243.4 13.0 %collective-permute-start.25 = (f32[104,384]{1,0:T(8,128)}, f32[104,384]{1,0:T(8,128)S(1)}, u32[]{:S(2)}, u32[]{:S(2)}) collective-permute-start(f32[104,384]{1,0:T(8,128)} %combine.22.refs_0_.refs_4_), channel_id=1, source_target_pairs={{0,2},{1,3},{2,0},{3,1},{4,6},{5,7},{6,4},{7,5},{8,10},{9,11},{10,... | collective-permute-start | bytes 479240 | tf_op jit(solution)/shard_map/ppermute | solution.py:545
  244.6 11.7 %collective-permute-start.24 = (f32[104,384]{1,0:T(8,128)}, f32[104,384]{1,0:T(8,128)S(1)}, u32[]{:S(2)}, u32[]{:S(2)}) collective-permute-start(f32[104,384]{1,0:T(8,128)} %combine.22.refs_0_.refs_4_), channel_id=1, source_target_pairs={{0,1},{1,0},{2,3},{3,2},{4,5},{5,4},{6,7},{7,6},{8,9},{9,8},{10,11... | collective-permute-start | bytes 479240 | tf_op jit(solution)/shard_map/ppermute | solution.py:545
  250.1 6.3 %copy-start.26 = (f32[104,384]{1,0:T(8,128)}, f32[104,384]{1,0:T(8,128)S(1)}, u32[]{:S(2)}) copy-start(f32[104,384]{1,0:T(8,128)S(1)} %collective-permute-done.26.refs_3_) | copy-start | bytes 479236
  259.7 15.8 %collective-permute-start.28 = (f32[4,104,384]{2,1,0:T(8,128)}, f32[4,104,384]{2,1,0:T(8,128)}, u32[]{:S(2)}, u32[]{:S(2)}) collective-permute-start(f32[4,104,384]{2,1,0:T(8,128)} %combine.23.refs_8_.refs_0_), channel_id=1, source_target_pairs={{0,8},{4,20},{8,0},{12,28},{16,24},{20,4},{24,16},{28,12},{1,9},{5... | collective-permute-start | bytes 1916936 | tf_op jit(solution)/shard_map/ppermute | solution.py:621
  261.0 35.6 %copy-start.4 = (f32[4,192,384]{2,1,0:T(8,128)}, f32[4,192,384]{2,1,0:T(8,128)S(1)}, u32[]{:S(2)}) copy-start(f32[4,192,384]{2,1,0:T(8,128)S(1)} %collective-permute-done.34.refs_1_) | copy-start | bytes 3538948
  261.0 27.1 %collective-permute-start.36 = (f32[4,192,384]{2,1,0:T(8,128)S(1)}, f32[4,192,384]{2,1,0:T(8,128)S(1)}, u32[]{:S(2)}, u32[]{:S(2)}) collective-permute-start(f32[4,192,384]{2,1,0:T(8,128)S(1)} %collective-permute-done.34.refs_1_), channel_id=1, source_target_pairs={{0,8},{4,20},{8,0},{12,28},{16,24},{20,4},{24,16},{28,12},{1,9},{5... | collective-permute-start | bytes 3538952 | tf_op jit(solution)/shard_map/ppermute | solution.py:621
  261.7 17.6 %collective-permute-start.27 = (f32[4,104,384]{2,1,0:T(8,128)}, f32[4,104,384]{2,1,0:T(8,128)}, u32[]{:S(2)}, u32[]{:S(2)}) collective-permute-start(f32[4,104,384]{2,1,0:T(8,128)} %combine.23.refs_8_.refs_0_), channel_id=1, source_target_pairs={{0,16},{4,12},{8,24},{12,4},{16,0},{20,28},{24,8},{28,20},{1,17},{... | collective-permute-start | bytes 1916936 | tf_op jit(solution)/shard_map/ppermute | solution.py:621
  263.2 24.9 %collective-permute-start.37 = (f32[4,192,384]{2,1,0:T(8,128)S(1)}, f32[4,192,384]{2,1,0:T(8,128)S(1)}, u32[]{:S(2)}, u32[]{:S(2)}) collective-permute-start(f32[4,192,384]{2,1,0:T(8,128)S(1)} %copy-done), channel_id=1, source_target_pairs={{0,4},{4,0},{8,12},{12,8},{16,20},{20,16},{24,28},{28,24},{1,5},{5... | collective-permute-start | bytes 3538952 | tf_op jit(solution)/shard_map/ppermute | solution.py:545
  263.2 33.4 %copy-start.5 = (f32[4,192,384]{2,1,0:T(8,128)}, f32[4,192,384]{2,1,0:T(8,128)S(1)}, u32[]{:S(2)}) copy-start(f32[4,192,384]{2,1,0:T(8,128)S(1)} %collective-permute-done.35.refs_2_) | copy-start | bytes 3538948
  263.2 31.9 %collective-permute-start.39 = (f32[4,192,384]{2,1,0:T(8,128)S(1)}, f32[4,192,384]{2,1,0:T(8,128)S(1)}, u32[]{:S(2)}, u32[]{:S(2)}) collective-permute-start(f32[4,192,384]{2,1,0:T(8,128)S(1)} %collective-permute-done.35.refs_2_), channel_id=1, source_target_pairs={{0,4},{4,0},{8,12},{12,8},{16,20},{20,16},{24,28},{28,24},{1,5},{5... | collective-permute-start | bytes 3538952 | tf_op jit(solution)/shard_map/ppermute | solution.py:545
  275.6 20.0 %collective-permute-start.38 = (f32[4,192,384]{2,1,0:T(8,128)S(1)}, f32[4,192,384]{2,1,0:T(8,128)S(1)}, u32[]{:S(2)}, u32[]{:S(2)}) collective-permute-start(f32[4,192,384]{2,1,0:T(8,128)S(1)} %collective-permute-done.34.refs_1_), channel_id=1, source_target_pairs={{0,4},{4,0},{8,12},{12,8},{16,20},{20,16},{24,28},{28,24},{1,5},{5... | collective-permute-start | bytes 3538952 | tf_op jit(solution)/shard_map/ppermute | solution.py:545
  279.4 15.7 %collective-permute-start.29 = (f32[4,104,384]{2,1,0:T(8,128)}, f32[4,104,384]{2,1,0:T(8,128)}, u32[]{:S(2)}, u32[]{:S(2)}) collective-permute-start(f32[4,104,384]{2,1,0:T(8,128)} %collective-permute-done.27.refs_1_), channel_id=1, source_target_pairs={{0,8},{4,20},{8,0},{12,28},{16,24},{20,4},{24,16},{28,12},{1,9},{5... | collective-permute-start | bytes 1916936 | tf_op jit(solution)/shard_map/ppermute | solution.py:621
  288.1 7.5 %copy-start.6 = (f32[4,192,384]{2,1,0:T(8,128)}, f32[4,192,384]{2,1,0:T(8,128)S(1)}, u32[]{:S(2)}) copy-start(f32[4,192,384]{2,1,0:T(8,128)S(1)} %collective-permute-done.36.refs_3_) | copy-start | bytes 3538948
  288.1 8.5 %collective-permute-start.40 = (f32[4,192,384]{2,1,0:T(8,128)S(1)}, f32[4,192,384]{2,1,0:T(8,128)}, u32[]{:S(2)}, u32[]{:S(2)}) collective-permute-start(f32[4,192,384]{2,1,0:T(8,128)S(1)} %collective-permute-done.36.refs_3_), channel_id=1, source_target_pairs={{0,4},{4,0},{8,12},{12,8},{16,20},{20,16},{24,28},{28,24},{1,5},{5... | collective-permute-start | bytes 3538952 | tf_op jit(solution)/shard_map/ppermute | solution.py:545
  288.1 7.6 %copy-start.7 = (f32[4,192,384]{2,1,0:T(8,128)}, f32[4,192,384]{2,1,0:T(8,128)S(1)}, u32[]{:S(2)}) copy-start(f32[4,192,384]{2,1,0:T(8,128)S(1)} %collective-permute-done.37.refs_4_) | copy-start | bytes 3538948
  288.1 17.0 %collective-permute-start.30 = (f32[4,104,384]{2,1,0:T(8,128)}, f32[4,104,384]{2,1,0:T(8,128)S(1)}, u32[]{:S(2)}, u32[]{:S(2)}) collective-permute-start(f32[4,104,384]{2,1,0:T(8,128)} %combine.23.refs_8_.refs_0_), channel_id=1, source_target_pairs={{0,4},{4,0},{8,12},{12,8},{16,20},{20,16},{24,28},{28,24},{1,5},{5... | collective-permute-start | bytes 1916936 | tf_op jit(solution)/shard_map/ppermute | solution.py:545
  295.0 10.1 %collective-permute-start.31 = (f32[4,104,384]{2,1,0:T(8,128)}, f32[4,104,384]{2,1,0:T(8,128)}, u32[]{:S(2)}, u32[]{:S(2)}) collective-permute-start(f32[4,104,384]{2,1,0:T(8,128)} %collective-permute-done.27.refs_1_), channel_id=1, source_target_pairs={{0,4},{4,0},{8,12},{12,8},{16,20},{20,16},{24,28},{28,24},{1,5},{5... | collective-permute-start | bytes 1916936 | tf_op jit(solution)/shard_map/ppermute | solution.py:545
  295.0 10.1 %collective-permute-start.32 = (f32[4,104,384]{2,1,0:T(8,128)}, f32[4,104,384]{2,1,0:T(8,128)}, u32[]{:S(2)}, u32[]{:S(2)}) collective-permute-start(f32[4,104,384]{2,1,0:T(8,128)} %collective-permute-done.28.refs_2_), channel_id=1, source_target_pairs={{0,4},{4,0},{8,12},{12,8},{16,20},{20,16},{24,28},{28,24},{1,5},{5... | collective-permute-start | bytes 1916936 | tf_op jit(solution)/shard_map/ppermute | solution.py:545
  295.6 9.6 %collective-permute-start.33 = (f32[4,104,384]{2,1,0:T(8,128)}, f32[4,104,384]{2,1,0:T(8,128)}, u32[]{:S(2)}, u32[]{:S(2)}) collective-permute-start(f32[4,104,384]{2,1,0:T(8,128)} %collective-permute-done.29.refs_3_), channel_id=1, source_target_pairs={{0,4},{4,0},{8,12},{12,8},{16,20},{20,16},{24,28},{28,24},{1,5},{5... | collective-permute-start | bytes 1916936 | tf_op jit(solution)/shard_map/ppermute | solution.py:545
  (17 other events, 14.0 us)

commit v2 on v1

--- a/solution.py
+++ b/solution.py
@@ -16,6 +16,7 @@
 F32 = jnp.float32
 BF16 = jnp.bfloat16
 VMEM_LIMIT = 60 * 1024 * 1024
+STEP_LIMIT = 16 * 1024 * 1024
 
 ERF_P = 0.39
 ERF_C = (0.11766263, 0.04569411, 0.32477995, -0.31770045, 0.44333237, -0.11376861)
@@ -548,26 +549,35 @@
 def combine(tasks, after, through):
     args = sum([list(inputs) for _, inputs, _ in tasks], [])
     shapes = sum([list(results) for _, _, results in tasks], [])
+    parts = [(count,) + x.shape[1:] for x, _, count in args]
 
     def body(*refs):
-        ins, outs = refs[: len(args)], refs[len(args) + len(through) + len(after) :]
+        outs = refs[len(args) + len(through) + len(after) :]
+        ins, sems = outs[len(shapes) + len(through) : -1], outs[-1]
+        copies = []
+        for k, (_, first, count) in enumerate(args):
+            copies.append(pltpu.make_async_copy(refs[k].at[pl.ds(first, count)], ins[k], sems.at[k]))
+            copies[-1].start()
         for function, inputs, results in tasks:
+            for item in copies[: len(inputs)]:
+                item.wait()
             function(ins[: len(inputs)], outs[: len(results)])
-            ins, outs = ins[len(inputs) :], outs[len(results) :]
+            copies, ins, outs = copies[len(inputs) :], ins[len(inputs) :], outs[len(results) :]
 
     vmem = pl.BlockSpec(memory_space=pltpu.VMEM)
     anywhere = pl.BlockSpec(memory_space=pl.ANY)
-    moved = sum(x.size for x in args) * 4
+    moved = sum(x.size for x, _, _ in args) * 4
     out = pl.pallas_call(
         body,
-        in_specs=[vmem] * len(args) + [anywhere] * (len(through) + len(after)),
+        in_specs=[anywhere] * (len(args) + len(through) + len(after)),
         out_specs=[vmem] * len(shapes) + [anywhere] * len(through),
         out_shape=[jax.ShapeDtypeStruct(shape, F32) for shape in shapes] + [jax.ShapeDtypeStruct(x.shape, F32) for x in through],
+        scratch_shapes=[pltpu.VMEM(part, F32) for part in parts] + [pltpu.SemaphoreType.DMA((max(len(args), 1),))],
         input_output_aliases={len(args) + k: len(shapes) + k for k in range(len(through))},
-        compiler_params=pltpu.CompilerParams(vmem_limit_bytes=VMEM_LIMIT),
+        compiler_params=pltpu.CompilerParams(vmem_limit_bytes=STEP_LIMIT),
         cost_estimate=pl.CostEstimate(flops=moved, bytes_accessed=2 * moved, transcendentals=0),
         name="combine",
-    )(*args, *through, *after)
+    )(*[x for x, _, _ in args], *through, *after)
     result = []
     for _, _, results in tasks:
         result.append(list(out[: len(results)]))
@@ -575,19 +585,23 @@
     return result, list(out)
 
 
-def halve(ins, outs):
-    keep, got = ins
-    half = keep.shape[0] // 2
-    outs[0][...] = keep[half:] + got[half:]
-    outs[1][...] = keep[:half] + got[:half]
+def sum_of(refs):
+    total = refs[0][...]
+    for ref in refs[1:]:
+        total = total + ref[...]
+    return total
+
+
+def add(ins, outs):
+    outs[0][...] = sum_of(ins)
 
 
 def split_four(ins, outs):
     start = 0
-    for keep, got in zip(ins[::2], ins[1::2]):
-        rows = keep.shape[1]
+    for group in range(0, len(ins), 4):
+        rows = ins[group].shape[1]
         for k, out in enumerate(outs):
-            out[start : start + rows] = keep[k] + got[k]
+            out[start : start + rows] = sum_of([ref.at[k] for ref in ins[group : group + 4]])
         start += rows
 
 
@@ -600,8 +614,11 @@
 
 
 def stack(ins, outs):
-    for k, x in enumerate(ins):
-        outs[0][k] = x[...]
+    rows = ins[0].shape[0]
+    for k in range(4):
+        outs[0][k, :rows] = ins[k][...]
+        if len(ins) > 4:
+            outs[0][k, rows:] = ins[4][k]
 
 
 class Round:
@@ -609,10 +626,17 @@
         self.keep, self.send, self.sizes, self.stage = keep, send, sizes, 0
         self.shape = keep.shape[1:]
         self.more = []
+        self.parked = False
 
     def merge(self, other):
         assert self.stage == other.stage
-        self.more = [other.keep, *other.got]
+        self.more = list(other.terms if self.stage == 3 else [other.keep, *other.got])
+        self.shape = (self.shape[0] + other.shape[0], self.shape[1])
+        return self
+
+    def absorb(self, other):
+        assert self.stage == 5 and other.parked
+        self.more = [other.own]
         self.shape = (self.shape[0] + other.shape[0], self.shape[1])
         return self
 
@@ -625,12 +649,16 @@
 
     def tasks(self):
         stage, n = self.stage, self.shape
-        args = [self.keep, *getattr(self, "got", ()), *self.more]
-        self.more = []
         if stage in (1, 2):
-            return [(halve, args, ((PIECES >> (stage + 1),) + n,) * 2)]
+            half = PIECES >> (stage + 1)
+            return [(add, [(x, half, half) for x in self.terms], ((half,) + n,))]
         if stage == 3:
-            return [(split_four, args, (n,) * 4)]
+            args, self.more = self.terms + self.more, []
+            return [(split_four, [(x, 0, 4) for x in args], (n,) * 4)]
+        if stage not in (4, 5):
+            return []
+        args, self.more = [self.keep, *self.got, *self.more], []
+        args = [(x, 0, x.shape[0]) for x in args]
         if stage == 4:
             return [(total_of, args, (n,))]
         if stage == 5:
@@ -641,9 +669,9 @@
         stage = self.stage
         self.stage += 1
         if stage == 0:
-            self.got = [self.swap(self.send, "grp", 1)]
+            self.terms = [self.keep, self.swap(self.send, "grp", 1)]
         elif stage <= 2:
-            self.keep, self.got = done[1], [self.across(done[0], stage - 1)]
+            self.terms = self.terms + [self.across(done[0], stage - 1)]
         elif stage == 3:
             self.keep, self.got = done[0], [self.swap(done[k], "dp", k) for k in range(1, 4)]
         elif stage == 4:
@@ -655,6 +683,8 @@
             self.keep, self.got = total, [self.swap(total, "dp", k) for k in range(1, 4)]
         elif stage == 5:
             self.own = done[0]
+            if self.parked:
+                return
             self.second, self.first = self.across(self.own, 1), self.across(self.own, 0)
             self.pieces = [self.own, self.second, self.first, None, self.swap(self.own, "grp", 1)]
         elif stage == 6:
@@ -672,11 +702,10 @@
         tasks = [item.tasks() for item in rounds]
         flat = sum(tasks, [])
         if flat:
-            done, through = combine(flat, self.after, [new.send] if new else [])
+            done, through = combine(flat, [] if new else self.after, [new.send] if new else [])
+            self.after = [done[0][0]]
             for item, own in zip(rounds, tasks):
                 item.launch([x for result in done[: len(own)] for x in result])
-                if own:
-                    self.after = [done[0][0]]
                 done = done[len(own) :]
             if new:
                 new.send = through[0]
@@ -763,7 +792,7 @@
         out_shape=[jax.ShapeDtypeStruct(shapes[name], F32) for name in names] + [jax.ShapeDtypeStruct(shape, F32) for shape in small],
         scratch_shapes=scratch,
         input_output_aliases={1 + count + index: names.index(name) for index, name in enumerate(old)},
-        compiler_params=pltpu.CompilerParams(vmem_limit_bytes=VMEM_LIMIT),
+        compiler_params=pltpu.CompilerParams(vmem_limit_bytes=2 * STEP_LIMIT),
         name="place",
     )(me, *pieces, *[before[name] for name in old], *after)
     return {**before, **dict(zip(names, out))}, list(out[len(names) :])
@@ -800,35 +829,31 @@
     done = {}
     rest = ()
     dmid, keep, send, sums1 = mlp(1, cotangent, [])
-    order.after = [sums1]
     q0 = Round(keep, send, sizes)
     step(q0)
     step(q0)
     dx, keep, send, sums2 = attention(1, dmid, [], order.after)
-    order.after = [sums2]
     q1 = Round(keep, send, sizes)
     step(q0, new=q1)
     dmid, keep, send, sums0 = mlp(0, dx, order.after)
-    order.after = [sums0]
     q2 = Round(keep, send, sizes)
     step(q1, q0, new=q2)
     dx, keep, send = attention(0, dmid, [sums0, sums1, sums2], order.after)
-    order.after = [keep]
     q3 = Round(keep, send, sizes)
-    step(q1, q2, new=q3)
+    step(q1, q2, q0, new=q3)
     step(q3)
-    step(q1)
+    q0.parked = True
+    step(q1, q0)
     step(q2, q3)
-    upper = q0.merge(q1)
-    step(upper)
     lower = q2.merge(q3)
+    step(lower, q1)
     step(lower)
+    upper = q1.absorb(q0)
     step(upper)
     step(lower)
     step(upper)
     step(upper)
-    step(lower)
-    done, _ = place(me, upper.pieces, (("fc1", 1), ("fc2", 1), ("qkv", 1), ("fc2", 0)), shapes, {}, order.after)
+    done, _ = place(me, upper.pieces, (("qkv", 1), ("fc2", 0), ("fc1", 1), ("fc2", 1)), shapes, {}, order.after)
     step(lower)
     step(lower)
     done, rest = place(me, lower.pieces, (("fc1", 0), ("qkv", 0)), shapes, done, [], small)

time: 314 us -> 292 us (0.930)
  Pallas kernels: 157 us -> 135 us
  starting transfers between devices: 45.2 us -> 52.4 us
  local copies, waits for them, and re-layouts: 13.8 us -> 9.52 us
    pallas_call x12 -> x11, Pallas kernels: 32.9 us -> 15.4 us  [combine(): pl.pallas_call(body, in_specs=[anywhere] * (len(args) + len(through) + le...]
    ppermute x27 -> x30, starting transfers between devices: 28 us -> 35.5 us  [exchange(): return lax.ppermute(x, axis, [(i, i ^ bits) for i in range(size)])]
    pallas_call x2, Pallas kernels: 15.3 us -> 10.3 us  [place(): pl.pallas_call(body, in_specs=[pl.BlockSpec(memory_space=pltpu.SMEM)] + [...]
    unnamed x80 -> x26, local copies, waits for them, and re-layouts: 13.8 us -> 9.52 us
    ppermute x27 -> x30, waiting for transfers between devices: 55.6 us -> 55.4 us  [exchange(): return lax.ppermute(x, axis, [(i, i ^ bits) for i in range(size)])]
  transfers between devices with their start and end apart: 41 -> 44, of which waited for: 15 -> 17; matrix products, arithmetic and copies ran while one was open for 0% -> 0% of each run, Pallas kernels for 25% -> 23%
where the time goes in v2:
time: 292 us; the launch traced here: 291 us
  Pallas kernels  135 us (46%)
  waiting for transfers between devices  93.1 us (32%)
  starting transfers between devices  52.4 us (18%)
  local copies, waits for them, and re-layouts  9.52 us (3%)
    ppermute x30, waiting for transfers between devices, exchange(): return lax.ppermute(x, axis, [(i, i ^ bits) for i in range(size)])  55.4 us
    pallas_call x2, Pallas kernels, attn_back(): pl.pallas_call(drop(attn_back_kernel, (bottom, layers), first, len(after)...  43.9 us
    ppermute x14, waiting for transfers between devices, across(): lax.ppermute(x, 'grp', [(i, i ^ bits(i)) for i in range(self.sizes['grp'])])  37.8 us
    ppermute x30, starting transfers between devices, exchange(): return lax.ppermute(x, axis, [(i, i ^ bits) for i in range(size)])  35.5 us
    pallas_call x1, Pallas kernels, forward(): pl.pallas_call(fwd_kernel, grid_spec=pltpu.PrefetchScalarGridSpec(num_sca...  33.9 us
    pallas_call x2, Pallas kernels, mlp_back(): pl.pallas_call(drop(mlp_back_kernel, (top,), 11, len(after)), grid_spec=p...  31.1 us
    ppermute x14, starting transfers between devices, across(): lax.ppermute(x, 'grp', [(i, i ^ bits(i)) for i in range(self.sizes['grp'])])  16.9 us
    pallas_call x11, Pallas kernels, combine(): pl.pallas_call(body, in_specs=[anywhere] * (len(args) + len(through) + le...  15.4 us
  transfers between devices with their start and end apart: 44, of which 17 were waited for; matrix products, arithmetic and copies ran while one was open for 0% of the time, Pallas kernels for 23%

profile of v2, /device:TPU:0, one launch (start us, length us, event | category | flops | bytes accessed | tf_op | source)
XLA Modules:
  0.0 291.4 jit_solution(17877914416133201570)
XLA Ops:
  1.2 33.9 %encoder_forward.1 = (bf16[6,197,384]{2,1,0:T(8,128)(2,1)}, bf16[2,1248,384]{2,1,0:T(8,128)(2,1)}, bf16[2,1248,1152]{2,1,0:T(8,128)(2,1)}, f32[2,6,8,208]{3,2,1,...) custom-call(s32[6]{0:T(128)} %refs_0_.7, ...), custom_call_target="tpu_custom_call" | custom-call | tf_op jit(solution)/shard_map/encoder_forward/pallas_call | solution.py:182
  35.2 17.6 %mlp_backward.2 = (f32[1248,384]{1,0:T(8,128)}, f32[16,96,384]{2,1,0:T(8,128)}, f32[16,96,384]{2,1,0:T(8,128)}, f32[16,384]{1,0:T(8,128)}) custom-call(s32[6]{0:T(128)} %refs_0_.7, s32[2]{0:T(128)} %broadcast_select_fusion.refs_1_.me, bf16[6,197,384]{2,1,0:T(8,128)(2,1)} %refs_2_.1, bf16[2,1248,384]{2,1,0:T(8,128)(2,1)} %get-tuple-element.79.refs_3_, ...), custom_call_target="tpu_custom_call" | custom-call | flops 5888802816 | bytes 14376960 | tf_op jit(solution)/shard_map/mlp_backward/pallas_call | solution.py:351
  53.2 4.4 %collective-permute-done.refs_1_.refs_3_ = f32[16,96,384]{2,1,0:T(8,128)S(1)} collective-permute-done((f32[16,96,384]{2,1,0:T(8,128)}, f32[16,96,384]{2,1,0:T(8,128)S(1)}, u32[]{:S(2)}, u32[]{:S(2)}) %collective-permute-start) | collective-permute-done | bytes 2359328 | tf_op jit(solution)/shard_map/ppermute | solution.py:546
  57.6 2.5 copy-done.1
  60.1 1.6 combine.11.refs_13_
  61.8 2.9 collective-permute-start.1
  64.7 23.7 %attention_backward.2 = (f32[1248,384]{1,0:T(8,128)}, f32[16,96,384]{2,1,0:T(8,128)}, f32[16,96,384]{2,1,0:T(8,128)}, f32[16,384]{1,0:T(8,128)}) custom-call(s32[6]{0:T(128)} %refs_0_.7, s32[2]{0:T(128)} %broadcast_select_fusion.refs_1_.me, f32[1248,384]{1,0:T(8,128)} %get-tuple-element.84.refs_2_, bf16[2,1248,384]{2,1,0:T(8,128)(2,1)} %get-tuple-element.85.refs_3_, ...), custom_call_target="tpu_custom_call" | custom-call | flops 5888802816 | bytes 14376960 | tf_op jit(solution)/shard_map/attention_backward/pallas_call | solution.py:529
  88.4 1.7 copy-done.5
  90.1 1.3 combine.12
  91.5 1.6 collective-permute-start.3
  93.0 13.5 %mlp_backward.3 = (f32[1248,384]{1,0:T(8,128)}, f32[16,48,384]{2,1,0:T(8,128)}, f32[16,48,384]{2,1,0:T(8,128)}, f32[16,384]{1,0:T(8,128)}) custom-call(s32[6]{0:T(128)} %refs_0_.7, s32[2]{0:T(128)} %broadcast_select_fusion.refs_1_.me, f32[1248,384]{1,0:T(8,128)} %get-tuple-element.93.refs_2_, bf16[2,1248,384]{2,1,0:T(8,128)(2,1)} %get-tuple-element.79.refs_3_, ...), custom_call_target="tpu_custom_call" | custom-call | flops 5888802816 | bytes 14376960 | tf_op jit(solution)/shard_map/mlp_backward/pallas_call | solution.py:351
  106.6 1.7 copy-done.3
  108.3 1.7 copy-done.6
  109.9 2.9 combine.13
  114.1 1.6 collective-permute-start.6
  115.7 2.6 collective-permute-start.7
  118.5 20.2 %attention_backward.3 = (f32[6,197,384]{2,1,0:T(8,128)}, f32[16,56,384]{2,1,0:T(8,128)}, f32[16,56,384]{2,1,0:T(8,128)}) custom-call(s32[6]{0:T(128)} %refs_0_.7, s32[2]{0:T(128)} %broadcast_select_fusion.refs_1_.me, f32[1248,384]{1,0:T(8,128)} %get-tuple-element.96.refs_2_, bf16[2,1248,384]{2,1,0:T(8,128)(2,1)} %get-tuple-element.85.refs_3_, ...), custom_call_target="tpu_custom_call" | custom-call | flops 5888802816 | bytes 14376960 | tf_op jit(solution)/shard_map/attention_backward/pallas_call | solution.py:529
  138.8 1.3 copy-done.9
  140.1 1.8 combine.14
  142.0 3.1 %collective-permute-done.10.refs_1_.refs_4_.refs_5_ = f32[16,56,384]{2,1,0:T(8,128)S(1)} collective-permute-done((f32[16,56,384]{2,1,0:T(8,128)S(1)}, f32[16,56,384]{2,1,0:T(8,128)S(1)}, u32[]{:S(2)}, u32[]{:S(2)}) %collective-permute-start.10) | collective-permute-done | bytes 1376288 | tf_op jit(solution)/shard_map/ppermute | solution.py:546
  145.7 1.4 collective-permute-start.11
  147.1 0.7 collective-permute-start.12
  147.8 1.5 collective-permute-start.9
  149.3 3.6 %collective-permute-start.15 = (f32[96,384]{1,0:T(8,128)S(1)}, f32[96,384]{1,0:T(8,128)S(1)}, u32[]{:S(2)}, u32[]{:S(2)}) collective-permute-start(f32[96,384]{1,0:T(8,128)S(1)} %get-tuple-element.116.refs_4_), channel_id=1, source_target_pairs={{0,3},{1,2},{2,1},{3,0},{4,7},{5,6},{6,5},{7,4},{8,11},{9,10},{10,... | collective-permute-start | bytes 442376 | tf_op jit(solution)/shard_map/ppermute | solution.py:546
  152.9 5.0 %collective-permute-done.15.refs_7_ = f32[96,384]{1,0:T(8,128)S(1)} collective-permute-done((f32[96,384]{1,0:T(8,128)S(1)}, f32[96,384]{1,0:T(8,128)S(1)}, u32[]{:S(2)}, u32[]{:S(2)}) %collective-permute-start.15) | collective-permute-done | bytes 147488 | tf_op jit(solution)/shard_map/ppermute | solution.py:546
  157.9 5.0 %collective-permute-start.13 = (f32[96,384]{1,0:T(8,128)S(1)}, f32[96,384]{1,0:T(8,128)S(1)}, u32[]{:S(2)}, u32[]{:S(2)}) collective-permute-start(f32[96,384]{1,0:T(8,128)S(1)} %get-tuple-element.116.refs_4_), channel_id=1, source_target_pairs={{0,1},{1,0},{2,3},{3,2},{4,5},{5,4},{6,7},{7,6},{8,9},{9,8},{10,11... | collective-permute-start | bytes 442376 | tf_op jit(solution)/shard_map/ppermute | solution.py:546
  162.9 1.1 collective-permute-done.14.refs_6_
  164.0 2.0 collective-permute-done.13.refs_5_
  166.0 1.6 combine.16
  167.6 1.7 collective-permute-done.9.refs_2_
  169.3 1.2 combine.17
  170.5 1.0 collective-permute-start.17
  171.5 1.1 collective-permute-start.16
  172.6 0.7 collective-permute-start.18
  173.3 3.5 %collective-permute-start.19 = (f32[96,384]{1,0:T(8,128)S(1)}, f32[96,384]{1,0:T(8,128)S(1)}, u32[]{:S(2)}, u32[]{:S(2)}) collective-permute-start(f32[96,384]{1,0:T(8,128)S(1)} %get-tuple-element.121), channel_id=1, source_target_pairs={{0,2},{1,3},{2,0},{3,1},{4,6},{5,7},{6,4},{7,5},{8,10},{9,11},{10,... | collective-permute-start | bytes 442376 | tf_op jit(solution)/shard_map/ppermute | solution.py:546
  177.0 2.5 collective-permute-done.18.refs_9_
  179.5 7.6 %collective-permute-done.19.refs_10_ = f32[96,384]{1,0:T(8,128)S(1)} collective-permute-done((f32[96,384]{1,0:T(8,128)S(1)}, f32[96,384]{1,0:T(8,128)S(1)}, u32[]{:S(2)}, u32[]{:S(2)}) %collective-permute-start.19) | collective-permute-done | bytes 147488 | tf_op jit(solution)/shard_map/ppermute | solution.py:546
  187.1 1.7 combine.18
  188.9 2.2 collective-permute-start.21
  191.1 1.0 collective-permute-start.22
  192.1 1.4 collective-permute-start.23
  193.5 2.4 collective-permute-start.29
  196.1 2.1 collective-permute-start.27
  198.1 12.7 %collective-permute-done.22.refs_2_ = f32[104,384]{1,0:T(8,128)S(1)} collective-permute-done((f32[104,384]{1,0:T(8,128)S(1)}, f32[104,384]{1,0:T(8,128)S(1)}, u32[]{:S(2)}, u32[]{:S(2)}) %collective-permute-start.22) | collective-permute-done | bytes 159776 | tf_op jit(solution)/shard_map/ppermute | solution.py:546
  210.8 0.9 combine.19.refs_5_.refs_0_
  211.7 7.2 %collective-permute-done.28.refs_2_ = f32[96,384]{1,0:T(8,128)S(1)} collective-permute-done((f32[96,384]{1,0:T(8,128)S(1)}, f32[96,384]{1,0:T(8,128)S(1)}, u32[]{:S(2)}, u32[]{:S(2)}) %collective-permute-start.28) | collective-permute-done | bytes 147488 | tf_op jit(solution)/shard_map/ppermute | solution.py:546
  218.8 1.0 combine.20.refs_4_.refs_0_
  219.8 2.0 collective-permute-start.37
  221.9 2.4 collective-permute-start.26
  224.4 2.0 collective-permute-start.24
  226.3 4.5 %collective-permute-done.26.refs_3_ = f32[104,384]{1,0:T(8,128)S(1)} collective-permute-done((f32[104,384]{1,0:T(8,128)S(1)}, f32[104,384]{1,0:T(8,128)S(1)}, u32[]{:S(2)}, u32[]{:S(2)}) %collective-permute-start.26) | collective-permute-done | bytes 159776 | tf_op jit(solution)/shard_map/ppermute | solution.py:546
  230.8 5.3 %collective-permute-done.25.refs_2_ = f32[104,384]{1,0:T(8,128)S(1)} collective-permute-done((f32[104,384]{1,0:T(8,128)S(1)}, f32[104,384]{1,0:T(8,128)S(1)}, u32[]{:S(2)}, u32[]{:S(2)}) %collective-permute-start.25) | collective-permute-done | bytes 159776 | tf_op jit(solution)/shard_map/ppermute | solution.py:546
  236.1 0.9 combine.21.refs_8_.refs_0_
  237.0 1.7 collective-permute-start.31
  238.7 10.0 %collective-permute-done.37.refs_1_ = f32[4,192,384]{2,1,0:T(8,128)S(1)} collective-permute-done((f32[4,192,384]{2,1,0:T(8,128)S(1)}, f32[4,192,384]{2,1,0:T(8,128)S(1)}, u32[]{:S(2)}, u32[]{:S(2)}) %collective-permute-start.37) | collective-permute-done | bytes 1179680 | tf_op jit(solution)/shard_map/ppermute | solution.py:645
  248.8 1.8 collective-permute-start.39
  251.4 7.5 %collective-permute-done.31.refs_2_ = f32[4,104,384]{2,1,0:T(8,128)S(1)} collective-permute-done((f32[4,104,384]{2,1,0:T(8,128)S(1)}, f32[4,104,384]{2,1,0:T(8,128)S(1)}, u32[]{:S(2)}, u32[]{:S(2)}) %collective-permute-start.31) | collective-permute-done | bytes 639008 | tf_op jit(solution)/shard_map/ppermute | solution.py:645
  258.8 9.1 %collective-permute-done.30.refs_1_ = f32[4,104,384]{2,1,0:T(8,128)S(1)} collective-permute-done((f32[4,104,384]{2,1,0:T(8,128)S(1)}, f32[4,104,384]{2,1,0:T(8,128)S(1)}, u32[]{:S(2)}, u32[]{:S(2)}) %collective-permute-start.30) | collective-permute-done | bytes 639008 | tf_op jit(solution)/shard_map/ppermute | solution.py:645
  268.1 4.1 %collective-permute-done.39.refs_3_ = f32[4,192,384]{2,1,0:T(8,128)S(1)} collective-permute-done((f32[4,192,384]{2,1,0:T(8,128)S(1)}, f32[4,192,384]{2,1,0:T(8,128)S(1)}, u32[]{:S(2)}, u32[]{:S(2)}) %collective-permute-start.39) | collective-permute-done | bytes 1179680 | tf_op jit(solution)/shard_map/ppermute | solution.py:645
  272.2 1.6 collective-permute-start.43
  273.8 5.3 %collective-permute-done.32.refs_3_ = f32[4,104,384]{2,1,0:T(8,128)S(1)} collective-permute-done((f32[4,104,384]{2,1,0:T(8,128)S(1)}, f32[4,104,384]{2,1,0:T(8,128)S(1)}, u32[]{:S(2)}, u32[]{:S(2)}) %collective-permute-start.32) | collective-permute-done | bytes 639008 | tf_op jit(solution)/shard_map/ppermute | solution.py:645
  279.1 1.3 collective-permute-start.34
  280.9 5.3 %place.2 = (f32[2,384,1536]{2,1,0:T(8,128)}, f32[2,1536,384]{2,1,0:T(8,128)}, f32[2,384,384]{2,1,0:T(8,128)}, f32[2,384,1152]{2,1,0:T(8,128)}) custom-call(s32[2]{0:T(128)S(1)} %copy-done.12, f32[4,192,384]{2,1,0:T(8,128)S(1)} %combine.20.refs_4_.refs_0_, f32[4,192,384]{2,1,0:T(8,128)S(1)} %collective-permute-done.37.refs_1_, ...), custom_call_target="tpu_custom_call" | custom-call | tf_op jit(solution)/shard_map/place/pallas_call | solution.py:788
  286.2 5.1 %place.3 = (f32[2,384,1536]{2,1,0:T(8,128)}, f32[2,384,384]{2,1,0:T(8,128)}, f32[2,384,1152]{2,1,0:T(8,128)}, f32[197,384]{1,0:T(8,128)}, f32[2,2,384]{2,1,0:T(2...) custom-call(s32[2]{0:T(128)S(1)} %copy-done.12, ...), custom_call_target="tpu_custom_call", output_to_operand_aliasing={{0}: (9, {}), {1}: (10, {}), {2}: (11, {})} | custom-call | tf_op jit(solution)/shard_map/place/pallas_call | solution.py:788
  (69 shorter events, 5.4 us)
Async XLA Ops:
  52.7 4.9 %collective-permute-start = (f32[16,96,384]{2,1,0:T(8,128)}, f32[16,96,384]{2,1,0:T(8,128)S(1)}, u32[]{:S(2)}, u32[]{:S(2)}) collective-permute-start(f32[16,96,384]{2,1,0:T(8,128)} %get-tuple-element.92), channel_id=1, source_target_pairs={{0,4},{4,0},{8,12},{12,8},{16,20},{20,16},{24,28},{28,24},{1,5},{5... | collective-permute-start | bytes 7077896 | tf_op jit(solution)/shard_map/ppermute | solution.py:546
  57.6 4.2 %copy-start.4 = (f32[16,96,384]{2,1,0:T(8,128)}, f32[16,96,384]{2,1,0:T(8,128)S(1)}, u32[]{:S(2)}) copy-start(f32[16,96,384]{2,1,0:T(8,128)S(1)} %collective-permute-done.refs_1_.refs_3_) | copy-start | bytes 7077892
  57.6 2.5 copy-start.1
  61.8 26.6 %collective-permute-start.1 = (f32[8,96,384]{2,1,0:T(8,128)}, f32[8,96,384]{2,1,0:T(8,128)S(1)}, u32[]{:S(2)}, u32[]{:S(2)}) collective-permute-start(f32[8,96,384]{2,1,0:T(8,128)} %combine.11.refs_13_), channel_id=1, source_target_pairs={{0,8},{4,20},{8,0},{12,28},{16,24},{20,4},{24,16},{28,12},{1,9},{5... | collective-permute-start | bytes 3538952 | tf_op jit(solution)/shard_map/ppermute | solution.py:645
  64.7 23.7 %copy-start.2 = (f32[16,96,384]{2,1,0:T(8,128)S(1)}, f32[16,96,384]{2,1,0:T(8,128)}, u32[]{:S(2)}) copy-start(f32[16,96,384]{2,1,0:T(8,128)} %get-tuple-element.91.refs_0_.refs_2_) | copy-start | bytes 7077892
  88.4 1.7 copy-start.5
  91.4 15.2 %collective-permute-start.2 = (f32[16,96,384]{2,1,0:T(8,128)}, f32[16,96,384]{2,1,0:T(8,128)}, u32[]{:S(2)}, u32[]{:S(2)}) collective-permute-start(f32[16,96,384]{2,1,0:T(8,128)} %get-tuple-element.101), channel_id=1, source_target_pairs={{0,4},{4,0},{8,12},{12,8},{16,20},{20,16},{24,28},{28,24},{1,5},{5... | collective-permute-start | bytes 7077896 | tf_op jit(solution)/shard_map/ppermute | solution.py:546
  91.5 15.1 %collective-permute-start.3 = (f32[4,96,384]{2,1,0:T(8,128)}, f32[4,96,384]{2,1,0:T(8,128)S(1)}, u32[]{:S(2)}, u32[]{:S(2)}) collective-permute-start(f32[4,96,384]{2,1,0:T(8,128)} %get-tuple-element.95.refs_11_), channel_id=1, source_target_pairs={{0,16},{4,12},{8,24},{12,4},{16,0},{20,28},{24,8},{28,20},{1,17},{... | collective-permute-start | bytes 1769480 | tf_op jit(solution)/shard_map/ppermute | solution.py:645
  93.0 13.6 %copy-start = (f32[16,96,384]{2,1,0:T(8,128)S(1)}, f32[16,96,384]{2,1,0:T(8,128)}, u32[]{:S(2)}) copy-start(f32[16,96,384]{2,1,0:T(8,128)} %get-tuple-element.100.refs_0_) | copy-start | bytes 7077892
  106.6 1.7 copy-start.3
  108.3 1.7 copy-start.6
  112.8 0.7 copy-start.10
  113.5 25.3 %collective-permute-start.4 = (f32[16,48,384]{2,1,0:T(8,128)}, f32[16,48,384]{2,1,0:T(8,128)}, u32[]{:S(2)}, u32[]{:S(2)}) collective-permute-start(f32[16,48,384]{2,1,0:T(8,128)} %get-tuple-element.106), channel_id=1, source_target_pairs={{0,4},{4,0},{8,12},{12,8},{16,20},{20,16},{24,28},{28,24},{1,5},{5... | collective-permute-start | bytes 3538952 | tf_op jit(solution)/shard_map/ppermute | solution.py:546
  113.5 25.3 %collective-permute-start.5 = (f32[8,96,384]{2,1,0:T(8,128)}, f32[8,96,384]{2,1,0:T(8,128)}, u32[]{:S(2)}, u32[]{:S(2)}) collective-permute-start(f32[8,96,384]{2,1,0:T(8,128)} %get-tuple-element.103.refs_16_), channel_id=1, source_target_pairs={{0,8},{4,20},{8,0},{12,28},{16,24},{20,4},{24,16},{28,12},{1,9},{5... | collective-permute-start | bytes 3538952 | tf_op jit(solution)/shard_map/ppermute | solution.py:645
  114.1 24.6 %collective-permute-start.6 = (f32[96,384]{1,0:T(8,128)}, f32[96,384]{1,0:T(8,128)S(1)}, u32[]{:S(2)}, u32[]{:S(2)}) collective-permute-start(f32[96,384]{1,0:T(8,128)} %get-tuple-element.108), channel_id=1, source_target_pairs={{0,1},{1,0},{2,3},{3,2},{4,5},{5,4},{6,7},{7,6},{8,9},{9,8},{10,11... | collective-permute-start | bytes 442376 | tf_op jit(solution)/shard_map/ppermute | solution.py:546
  115.7 23.0 %collective-permute-start.7 = (f32[96,384]{1,0:T(8,128)}, f32[96,384]{1,0:T(8,128)S(1)}, u32[]{:S(2)}, u32[]{:S(2)}) collective-permute-start(f32[96,384]{1,0:T(8,128)} %get-tuple-element.109), channel_id=1, source_target_pairs={{0,2},{1,3},{2,0},{3,1},{4,6},{5,7},{6,4},{7,5},{8,10},{9,11},{10,... | collective-permute-start | bytes 442376 | tf_op jit(solution)/shard_map/ppermute | solution.py:546
  118.3 20.4 %collective-permute-start.8 = (f32[96,384]{1,0:T(8,128)}, f32[96,384]{1,0:T(8,128)S(1)}, u32[]{:S(2)}, u32[]{:S(2)}) collective-permute-start(f32[96,384]{1,0:T(8,128)} %get-tuple-element.110), channel_id=1, source_target_pairs={{0,3},{1,2},{2,1},{3,0},{4,7},{5,6},{6,5},{7,4},{8,11},{9,10},{10,... | collective-permute-start | bytes 442376 | tf_op jit(solution)/shard_map/ppermute | solution.py:546
  118.5 20.2 %copy-start.8 = (f32[16,48,384]{2,1,0:T(8,128)S(1)}, f32[16,48,384]{2,1,0:T(8,128)}, u32[]{:S(2)}) copy-start(f32[16,48,384]{2,1,0:T(8,128)} %get-tuple-element.105.refs_3_.refs_0_) | copy-start | bytes 3538948
  118.5 20.2 %copy-start.11 = (f32[96,384]{1,0:T(8,128)S(1)}, f32[96,384]{1,0:T(8,128)}, u32[]{:S(2)}) copy-start(f32[96,384]{1,0:T(8,128)} %copy-done.10) | copy-start | bytes 442372
  138.8 1.3 copy-start.9
  140.1 5.0 %copy-start.7 = (f32[16,56,384]{2,1,0:T(8,128)S(1)}, f32[16,56,384]{2,1,0:T(8,128)}, u32[]{:S(2)}) copy-start(f32[16,56,384]{2,1,0:T(8,128)} %get-tuple-element.113.refs_0_.refs_3_.refs_4_) | copy-start | bytes 4128772
  141.9 3.2 %collective-permute-start.10 = (f32[16,56,384]{2,1,0:T(8,128)S(1)}, f32[16,56,384]{2,1,0:T(8,128)S(1)}, u32[]{:S(2)}, u32[]{:S(2)}) collective-permute-start(f32[16,56,384]{2,1,0:T(8,128)S(1)} %get-tuple-element.114), channel_id=1, source_target_pairs={{0,4},{4,0},{8,12},{12,8},{16,20},{20,16},{24,28},{28,24},{1,5},{5... | collective-permute-start | bytes 4128776 | tf_op jit(solution)/shard_map/ppermute | solution.py:546
  145.7 23.6 %collective-permute-start.11 = (f32[8,56,384]{2,1,0:T(8,128)S(1)}, f32[8,56,384]{2,1,0:T(8,128)S(1)}, u32[]{:S(2)}, u32[]{:S(2)}) collective-permute-start(f32[8,56,384]{2,1,0:T(8,128)S(1)} %combine.15.refs_8_), channel_id=1, source_target_pairs={{0,8},{4,20},{8,0},{12,28},{16,24},{20,4},{24,16},{28,12},{1,9},{5... | collective-permute-start | bytes 2064392 | tf_op jit(solution)/shard_map/ppermute | solution.py:645
  147.1 18.9 %collective-permute-start.12 = (f32[4,96,384]{2,1,0:T(8,128)S(1)}, f32[4,96,384]{2,1,0:T(8,128)S(1)}, u32[]{:S(2)}, u32[]{:S(2)}) collective-permute-start(f32[4,96,384]{2,1,0:T(8,128)S(1)} %get-tuple-element.115.refs_2_), channel_id=1, source_target_pairs={{0,16},{4,12},{8,24},{12,4},{16,0},{20,28},{24,8},{28,20},{1,17},{... | collective-permute-start | bytes 1769480 | tf_op jit(solution)/shard_map/ppermute | solution.py:645
  147.8 21.5 %collective-permute-start.9 = (f32[8,48,384]{2,1,0:T(8,128)S(1)}, f32[8,48,384]{2,1,0:T(8,128)S(1)}, u32[]{:S(2)}, u32[]{:S(2)}) collective-permute-start(f32[8,48,384]{2,1,0:T(8,128)S(1)} %get-tuple-element.112), channel_id=1, source_target_pairs={{0,8},{4,20},{8,0},{12,28},{16,24},{20,4},{24,16},{28,12},{1,9},{5... | collective-permute-start | bytes 1769480 | tf_op jit(solution)/shard_map/ppermute | solution.py:645
  149.3 8.6 %collective-permute-start.15 = (f32[96,384]{1,0:T(8,128)S(1)}, f32[96,384]{1,0:T(8,128)S(1)}, u32[]{:S(2)}, u32[]{:S(2)}) collective-permute-start(f32[96,384]{1,0:T(8,128)S(1)} %get-tuple-element.116.refs_4_), channel_id=1, source_target_pairs={{0,3},{1,2},{2,1},{3,0},{4,7},{5,6},{6,5},{7,4},{8,11},{9,10},{10,... | collective-permute-start | bytes 442376 | tf_op jit(solution)/shard_map/ppermute | solution.py:546
  152.9 11.1 %collective-permute-start.14 = (f32[96,384]{1,0:T(8,128)S(1)}, f32[96,384]{1,0:T(8,128)S(1)}, u32[]{:S(2)}, u32[]{:S(2)}) collective-permute-start(f32[96,384]{1,0:T(8,128)S(1)} %get-tuple-element.116.refs_4_), channel_id=1, source_target_pairs={{0,2},{1,3},{2,0},{3,1},{4,6},{5,7},{6,4},{7,5},{8,10},{9,11},{10,... | collective-permute-start | bytes 442376 | tf_op jit(solution)/shard_map/ppermute | solution.py:546
  157.9 8.1 %collective-permute-start.13 = (f32[96,384]{1,0:T(8,128)S(1)}, f32[96,384]{1,0:T(8,128)S(1)}, u32[]{:S(2)}, u32[]{:S(2)}) collective-permute-start(f32[96,384]{1,0:T(8,128)S(1)} %get-tuple-element.116.refs_4_), channel_id=1, source_target_pairs={{0,1},{1,0},{2,3},{3,2},{4,5},{5,4},{6,7},{7,6},{8,9},{9,8},{10,11... | collective-permute-start | bytes 442376 | tf_op jit(solution)/shard_map/ppermute | solution.py:546
  170.5 16.6 %collective-permute-start.17 = (f32[4,56,384]{2,1,0:T(8,128)S(1)}, f32[4,56,384]{2,1,0:T(8,128)S(1)}, u32[]{:S(2)}, u32[]{:S(2)}) collective-permute-start(f32[4,56,384]{2,1,0:T(8,128)S(1)} %get-tuple-element.119), channel_id=1, source_target_pairs={{0,16},{4,12},{8,24},{12,4},{16,0},{20,28},{24,8},{28,20},{1,17},{... | collective-permute-start | bytes 1032200 | tf_op jit(solution)/shard_map/ppermute | solution.py:645
  171.5 15.6 %collective-permute-start.16 = (f32[4,48,384]{2,1,0:T(8,128)S(1)}, f32[4,48,384]{2,1,0:T(8,128)S(1)}, u32[]{:S(2)}, u32[]{:S(2)}) collective-permute-start(f32[4,48,384]{2,1,0:T(8,128)S(1)} %get-tuple-element.118.refs_12_), channel_id=1, source_target_pairs={{0,16},{4,12},{8,24},{12,4},{16,0},{20,28},{24,8},{28,20},{1,17},{... | collective-permute-start | bytes 884744 | tf_op jit(solution)/shard_map/ppermute | solution.py:645
  172.6 6.9 %collective-permute-start.18 = (f32[96,384]{1,0:T(8,128)S(1)}, f32[96,384]{1,0:T(8,128)S(1)}, u32[]{:S(2)}, u32[]{:S(2)}) collective-permute-start(f32[96,384]{1,0:T(8,128)S(1)} %get-tuple-element.120), channel_id=1, source_target_pairs={{0,1},{1,0},{2,3},{3,2},{4,5},{5,4},{6,7},{7,6},{8,9},{9,8},{10,11... | collective-permute-start | bytes 442376 | tf_op jit(solution)/shard_map/ppermute | solution.py:546
  173.3 13.8 %collective-permute-start.19 = (f32[96,384]{1,0:T(8,128)S(1)}, f32[96,384]{1,0:T(8,128)S(1)}, u32[]{:S(2)}, u32[]{:S(2)}) collective-permute-start(f32[96,384]{1,0:T(8,128)S(1)} %get-tuple-element.121), channel_id=1, source_target_pairs={{0,2},{1,3},{2,0},{3,1},{4,6},{5,7},{6,4},{7,5},{8,10},{9,11},{10,... | collective-permute-start | bytes 442376 | tf_op jit(solution)/shard_map/ppermute | solution.py:546
  176.8 10.4 %collective-permute-start.20 = (f32[96,384]{1,0:T(8,128)S(1)}, f32[96,384]{1,0:T(8,128)S(1)}, u32[]{:S(2)}, u32[]{:S(2)}) collective-permute-start(f32[96,384]{1,0:T(8,128)S(1)} %get-tuple-element.122), channel_id=1, source_target_pairs={{0,3},{1,2},{2,1},{3,0},{4,7},{5,6},{6,5},{7,4},{8,11},{9,10},{10,... | collective-permute-start | bytes 442376 | tf_op jit(solution)/shard_map/ppermute | solution.py:546
  188.9 7.2 %collective-permute-start.21 = (f32[104,384]{1,0:T(8,128)S(1)}, f32[104,384]{1,0:T(8,128)S(1)}, u32[]{:S(2)}, u32[]{:S(2)}) collective-permute-start(f32[104,384]{1,0:T(8,128)S(1)} %get-tuple-element.124), channel_id=1, source_target_pairs={{0,1},{1,0},{2,3},{3,2},{4,5},{5,4},{6,7},{7,6},{8,9},{9,8},{10,11... | collective-permute-start | bytes 479240 | tf_op jit(solution)/shard_map/ppermute | solution.py:546
  191.1 19.7 %collective-permute-start.22 = (f32[104,384]{1,0:T(8,128)S(1)}, f32[104,384]{1,0:T(8,128)S(1)}, u32[]{:S(2)}, u32[]{:S(2)}) collective-permute-start(f32[104,384]{1,0:T(8,128)S(1)} %get-tuple-element.125), channel_id=1, source_target_pairs={{0,2},{1,3},{2,0},{3,1},{4,6},{5,7},{6,4},{7,5},{8,10},{9,11},{10,... | collective-permute-start | bytes 479240 | tf_op jit(solution)/shard_map/ppermute | solution.py:546
  192.1 18.7 %collective-permute-start.23 = (f32[104,384]{1,0:T(8,128)S(1)}, f32[104,384]{1,0:T(8,128)S(1)}, u32[]{:S(2)}, u32[]{:S(2)}) collective-permute-start(f32[104,384]{1,0:T(8,128)S(1)} %get-tuple-element.126), channel_id=1, source_target_pairs={{0,3},{1,2},{2,1},{3,0},{4,7},{5,6},{6,5},{7,4},{8,11},{9,10},{10,... | collective-permute-start | bytes 479240 | tf_op jit(solution)/shard_map/ppermute | solution.py:546
  193.5 18.1 %collective-permute-start.29 = (f32[96,384]{1,0:T(8,128)S(1)}, f32[96,384]{1,0:T(8,128)S(1)}, u32[]{:S(2)}, u32[]{:S(2)}) collective-permute-start(f32[96,384]{1,0:T(8,128)S(1)} %get-tuple-element.127.refs_0_), channel_id=1, source_target_pairs={{0,3},{1,2},{2,1},{3,0},{4,7},{5,6},{6,5},{7,4},{8,11},{9,10},{10,... | collective-permute-start | bytes 442376 | tf_op jit(solution)/shard_map/ppermute | solution.py:546
  195.9 22.9 %collective-permute-start.28 = (f32[96,384]{1,0:T(8,128)S(1)}, f32[96,384]{1,0:T(8,128)S(1)}, u32[]{:S(2)}, u32[]{:S(2)}) collective-permute-start(f32[96,384]{1,0:T(8,128)S(1)} %get-tuple-element.127.refs_0_), channel_id=1, source_target_pairs={{0,2},{1,3},{2,0},{3,1},{4,6},{5,7},{6,4},{7,5},{8,10},{9,11},{10,... | collective-permute-start | bytes 442376 | tf_op jit(solution)/shard_map/ppermute | solution.py:546
  196.1 22.8 %collective-permute-start.27 = (f32[96,384]{1,0:T(8,128)S(1)}, f32[96,384]{1,0:T(8,128)S(1)}, u32[]{:S(2)}, u32[]{:S(2)}) collective-permute-start(f32[96,384]{1,0:T(8,128)S(1)} %get-tuple-element.127.refs_0_), channel_id=1, source_target_pairs={{0,1},{1,0},{2,3},{3,2},{4,5},{5,4},{6,7},{7,6},{8,9},{9,8},{10,11... | collective-permute-start | bytes 442376 | tf_op jit(solution)/shard_map/ppermute | solution.py:546
  219.8 61.0 %copy-start.12 = (s32[2]{0:T(128)S(1)}, s32[2]{0:T(128)}, u32[]{:S(2)}) copy-start(s32[2]{0:T(128)} %broadcast_select_fusion.refs_1_.me) | copy-start | bytes 28
  219.8 29.0 %collective-permute-start.37 = (f32[4,192,384]{2,1,0:T(8,128)S(1)}, f32[4,192,384]{2,1,0:T(8,128)S(1)}, u32[]{:S(2)}, u32[]{:S(2)}) collective-permute-start(f32[4,192,384]{2,1,0:T(8,128)S(1)} %combine.20.refs_4_.refs_0_), channel_id=1, source_target_pairs={{0,16},{4,12},{8,24},{12,4},{16,0},{20,28},{24,8},{28,20},{1,17},{... | collective-permute-start | bytes 3538952 | tf_op jit(solution)/shard_map/ppermute | solution.py:645
  221.8 29.0 %collective-permute-start.38 = (f32[4,192,384]{2,1,0:T(8,128)S(1)}, f32[4,192,384]{2,1,0:T(8,128)S(1)}, u32[]{:S(2)}, u32[]{:S(2)}) collective-permute-start(f32[4,192,384]{2,1,0:T(8,128)S(1)} %combine.20.refs_4_.refs_0_), channel_id=1, source_target_pairs={{0,8},{4,20},{8,0},{12,28},{16,24},{20,4},{24,16},{28,12},{1,9},{5... | collective-permute-start | bytes 3538952 | tf_op jit(solution)/shard_map/ppermute | solution.py:645
  221.9 8.8 %collective-permute-start.26 = (f32[104,384]{1,0:T(8,128)S(1)}, f32[104,384]{1,0:T(8,128)S(1)}, u32[]{:S(2)}, u32[]{:S(2)}) collective-permute-start(f32[104,384]{1,0:T(8,128)S(1)} %combine.19.refs_5_.refs_0_), channel_id=1, source_target_pairs={{0,3},{1,2},{2,1},{3,0},{4,7},{5,6},{6,5},{7,4},{8,11},{9,10},{10,... | collective-permute-start | bytes 479240 | tf_op jit(solution)/shard_map/ppermute | solution.py:546
  224.4 11.7 %collective-permute-start.25 = (f32[104,384]{1,0:T(8,128)S(1)}, f32[104,384]{1,0:T(8,128)S(1)}, u32[]{:S(2)}, u32[]{:S(2)}) collective-permute-start(f32[104,384]{1,0:T(8,128)S(1)} %combine.19.refs_5_.refs_0_), channel_id=1, source_target_pairs={{0,2},{1,3},{2,0},{3,1},{4,6},{5,7},{6,4},{7,5},{8,10},{9,11},{10,... | collective-permute-start | bytes 479240 | tf_op jit(solution)/shard_map/ppermute | solution.py:546
  224.4 11.7 %collective-permute-start.24 = (f32[104,384]{1,0:T(8,128)S(1)}, f32[104,384]{1,0:T(8,128)S(1)}, u32[]{:S(2)}, u32[]{:S(2)}) collective-permute-start(f32[104,384]{1,0:T(8,128)S(1)} %combine.19.refs_5_.refs_0_), channel_id=1, source_target_pairs={{0,1},{1,0},{2,3},{3,2},{4,5},{5,4},{6,7},{7,6},{8,9},{9,8},{10,11... | collective-permute-start | bytes 479240 | tf_op jit(solution)/shard_map/ppermute | solution.py:546
  237.0 21.8 %collective-permute-start.31 = (f32[4,104,384]{2,1,0:T(8,128)S(1)}, f32[4,104,384]{2,1,0:T(8,128)S(1)}, u32[]{:S(2)}, u32[]{:S(2)}) collective-permute-start(f32[4,104,384]{2,1,0:T(8,128)S(1)} %combine.21.refs_8_.refs_0_), channel_id=1, source_target_pairs={{0,8},{4,20},{8,0},{12,28},{16,24},{20,4},{24,16},{28,12},{1,9},{5... | collective-permute-start | bytes 1916936 | tf_op jit(solution)/shard_map/ppermute | solution.py:645
  248.8 23.4 %collective-permute-start.39 = (f32[4,192,384]{2,1,0:T(8,128)S(1)}, f32[4,192,384]{2,1,0:T(8,128)S(1)}, u32[]{:S(2)}, u32[]{:S(2)}) collective-permute-start(f32[4,192,384]{2,1,0:T(8,128)S(1)} %collective-permute-done.37.refs_1_), channel_id=1, source_target_pairs={{0,8},{4,20},{8,0},{12,28},{16,24},{20,4},{24,16},{28,12},{1,9},{5... | collective-permute-start | bytes 3538952 | tf_op jit(solution)/shard_map/ppermute | solution.py:645
  250.6 17.3 %collective-permute-start.30 = (f32[4,104,384]{2,1,0:T(8,128)S(1)}, f32[4,104,384]{2,1,0:T(8,128)S(1)}, u32[]{:S(2)}, u32[]{:S(2)}) collective-permute-start(f32[4,104,384]{2,1,0:T(8,128)S(1)} %combine.21.refs_8_.refs_0_), channel_id=1, source_target_pairs={{0,16},{4,12},{8,24},{12,4},{16,0},{20,28},{24,8},{28,20},{1,17},{... | collective-permute-start | bytes 1916936 | tf_op jit(solution)/shard_map/ppermute | solution.py:645
  250.8 22.9 %collective-permute-start.40 = (f32[4,192,384]{2,1,0:T(8,128)S(1)}, f32[4,192,384]{2,1,0:T(8,128)S(1)}, u32[]{:S(2)}, u32[]{:S(2)}) collective-permute-start(f32[4,192,384]{2,1,0:T(8,128)S(1)} %combine.20.refs_4_.refs_0_), channel_id=1, source_target_pairs={{0,4},{4,0},{8,12},{12,8},{16,20},{20,16},{24,28},{28,24},{1,5},{5... | collective-permute-start | bytes 3538952 | tf_op jit(solution)/shard_map/ppermute | solution.py:546
  250.9 29.5 %collective-permute-start.42 = (f32[4,192,384]{2,1,0:T(8,128)S(1)}, f32[4,192,384]{2,1,0:T(8,128)S(1)}, u32[]{:S(2)}, u32[]{:S(2)}) collective-permute-start(f32[4,192,384]{2,1,0:T(8,128)S(1)} %collective-permute-done.38.refs_2_), channel_id=1, source_target_pairs={{0,4},{4,0},{8,12},{12,8},{16,20},{20,16},{24,28},{28,24},{1,5},{5... | collective-permute-start | bytes 3538952 | tf_op jit(solution)/shard_map/ppermute | solution.py:546
  258.8 21.5 %collective-permute-start.41 = (f32[4,192,384]{2,1,0:T(8,128)S(1)}, f32[4,192,384]{2,1,0:T(8,128)S(1)}, u32[]{:S(2)}, u32[]{:S(2)}) collective-permute-start(f32[4,192,384]{2,1,0:T(8,128)S(1)} %collective-permute-done.37.refs_1_), channel_id=1, source_target_pairs={{0,4},{4,0},{8,12},{12,8},{16,20},{20,16},{24,28},{28,24},{1,5},{5... | collective-permute-start | bytes 3538952 | tf_op jit(solution)/shard_map/ppermute | solution.py:546
  267.9 11.1 %collective-permute-start.32 = (f32[4,104,384]{2,1,0:T(8,128)S(1)}, f32[4,104,384]{2,1,0:T(8,128)S(1)}, u32[]{:S(2)}, u32[]{:S(2)}) collective-permute-start(f32[4,104,384]{2,1,0:T(8,128)S(1)} %collective-permute-done.30.refs_1_), channel_id=1, source_target_pairs={{0,8},{4,20},{8,0},{12,28},{16,24},{20,4},{24,16},{28,12},{1,9},{5... | collective-permute-start | bytes 1916936 | tf_op jit(solution)/shard_map/ppermute | solution.py:645
  272.2 8.6 %collective-permute-start.43 = (f32[4,192,384]{2,1,0:T(8,128)S(1)}, f32[4,192,384]{2,1,0:T(8,128)S(1)}, u32[]{:S(2)}, u32[]{:S(2)}) collective-permute-start(f32[4,192,384]{2,1,0:T(8,128)S(1)} %collective-permute-done.39.refs_3_), channel_id=1, source_target_pairs={{0,4},{4,0},{8,12},{12,8},{16,20},{20,16},{24,28},{28,24},{1,5},{5... | collective-permute-start | bytes 3538952 | tf_op jit(solution)/shard_map/ppermute | solution.py:546
  273.8 12.3 %collective-permute-start.33 = (f32[4,104,384]{2,1,0:T(8,128)S(1)}, f32[4,104,384]{2,1,0:T(8,128)S(1)}, u32[]{:S(2)}, u32[]{:S(2)}) collective-permute-start(f32[4,104,384]{2,1,0:T(8,128)S(1)} %combine.21.refs_8_.refs_0_), channel_id=1, source_target_pairs={{0,4},{4,0},{8,12},{12,8},{16,20},{20,16},{24,28},{28,24},{1,5},{5... | collective-permute-start | bytes 1916936 | tf_op jit(solution)/shard_map/ppermute | solution.py:546
  279.1 7.1 %collective-permute-start.34 = (f32[4,104,384]{2,1,0:T(8,128)S(1)}, f32[4,104,384]{2,1,0:T(8,128)S(1)}, u32[]{:S(2)}, u32[]{:S(2)}) collective-permute-start(f32[4,104,384]{2,1,0:T(8,128)S(1)} %collective-permute-done.30.refs_1_), channel_id=1, source_target_pairs={{0,4},{4,0},{8,12},{12,8},{16,20},{20,16},{24,28},{28,24},{1,5},{5... | collective-permute-start | bytes 1916936 | tf_op jit(solution)/shard_map/ppermute | solution.py:546
  280.3 5.8 %collective-permute-start.35 = (f32[4,104,384]{2,1,0:T(8,128)S(1)}, f32[4,104,384]{2,1,0:T(8,128)S(1)}, u32[]{:S(2)}, u32[]{:S(2)}) collective-permute-start(f32[4,104,384]{2,1,0:T(8,128)S(1)} %collective-permute-done.31.refs_2_), channel_id=1, source_target_pairs={{0,4},{4,0},{8,12},{12,8},{16,20},{20,16},{24,28},{28,24},{1,5},{5... | collective-permute-start | bytes 1916936 | tf_op jit(solution)/shard_map/ppermute | solution.py:546
  280.3 5.8 %collective-permute-start.36 = (f32[4,104,384]{2,1,0:T(8,128)S(1)}, f32[4,104,384]{2,1,0:T(8,128)S(1)}, u32[]{:S(2)}, u32[]{:S(2)}) collective-permute-start(f32[4,104,384]{2,1,0:T(8,128)S(1)} %collective-permute-done.32.refs_3_), channel_id=1, source_target_pairs={{0,4},{4,0},{8,12},{12,8},{16,20},{20,16},{24,28},{28,24},{1,5},{5... | collective-permute-start | bytes 1916936 | tf_op jit(solution)/shard_map/ppermute | solution.py:546

commit v3 on v2

--- a/solution.py
+++ b/solution.py
@@ -252,13 +252,18 @@
     return lax.shift_right_logical(j, 3), pl.multiple_of(lax.bitwise_and(j, 7) * rows, 8)
 
 
-def emit(me, source, keep, send, first, sems):
+def moves(me, source, keep, send, first, sems):
     rows = source.shape[1] // 8
     copies = []
     for r in range(PIECES):
         block, row = spot(me[r // HALF], r % HALF, rows)
         target = (keep, send)[r // HALF].at[r % HALF, pl.ds(first, rows)]
         copies.append(pltpu.make_async_copy(source.at[block, pl.ds(row, rows)], target, sems.at[r]))
+    return copies
+
+
+def emit(me, source, keep, send, first, sems):
+    copies = moves(me, source, keep, send, first, sems)
     for item in copies:
         item.start()
     return copies
@@ -304,17 +309,25 @@
         here = slice(k * width, (k + 1) * width)
         sums[7 + k : 8 + k, :] += column[:, here]
         gw1[k] += grad[:, here]
+    last = block == pl.num_programs(0) - 1
+
+    @pl.when(last)
+    def _():
+        emit(me, gw1, keep, send, 0, sems)
+        if top:
+            emit(me, gw2, keep, send, width // 8, sems.at[pl.ds(PIECES, PIECES)])
+
     dc = dot_bt(dpre, w1[0])
     xhat = xh[0].astype(F32)
     sums[1:2, :] += jnp.sum(dc * xhat, 0, keepdims=True)
     sums[3:4, :] += jnp.sum(dc, 0, keepdims=True)
     dmid[...] = dx + norm_back(dc, xhat, rstd[0], gain[0, 1:2].astype(F32))
 
-    @pl.when(block == pl.num_programs(0) - 1)
+    @pl.when(last)
     def _():
-        copies = emit(me, gw1, keep, send, 0, sems)
+        copies = moves(me, gw1, keep, send, 0, sems)
         if top:
-            copies += emit(me, gw2, keep, send, width // 8, sems.at[pl.ds(PIECES, PIECES)])
+            copies += moves(me, gw2, keep, send, width // 8, sems.at[pl.ds(PIECES, PIECES)])
         for item in copies:
             item.wait()
 

time: 292 us -> 291 us (level)
  no operation moved by 1% of the time
where the time goes in v3:
time: 291 us
  Pallas kernels  134 us (46%)
  waiting for transfers between devices  93 us (32%)
  starting transfers between devices  52.6 us (18%)
  local copies, waits for them, and re-layouts  9.52 us (3%)
    ppermute x30, waiting for transfers between devices, exchange(): return lax.ppermute(x, axis, [(i, i ^ bits) for i in range(size)])  55.3 us
    pallas_call x2, Pallas kernels, attn_back(): pl.pallas_call(drop(attn_back_kernel, (bottom, layers), first, len(after)...  43.9 us
    ppermute x14, waiting for transfers between devices, across(): lax.ppermute(x, 'grp', [(i, i ^ bits(i)) for i in range(self.sizes['grp'])])  37.7 us
    ppermute x30, starting transfers between devices, exchange(): return lax.ppermute(x, axis, [(i, i ^ bits) for i in range(size)])  35.4 us
    pallas_call x1, Pallas kernels, forward(): pl.pallas_call(fwd_kernel, grid_spec=pltpu.PrefetchScalarGridSpec(num_sca...  33.9 us
    pallas_call x2, Pallas kernels, mlp_back(): pl.pallas_call(drop(mlp_back_kernel, (top,), 11, len(after)), grid_spec=p...  30.3 us
    ppermute x14, starting transfers between devices, across(): lax.ppermute(x, 'grp', [(i, i ^ bits(i)) for i in range(self.sizes['grp'])])  17.1 us
    pallas_call x11, Pallas kernels, combine(): pl.pallas_call(body, in_specs=[anywhere] * (len(args) + len(through) + le...  15.4 us
  transfers between devices with their start and end apart: 44, of which 17 were waited for; matrix products, arithmetic and copies ran while one was open for 0% of the time, Pallas kernels for 23%

profile of v3, /device:TPU:0, one launch (start us, length us, event | category | flops | bytes accessed | tf_op | source)
XLA Modules:
  0.0 290.6 jit_solution(17144047911365088203)
XLA Ops:
  1.2 33.9 %encoder_forward.1 = (bf16[6,197,384]{2,1,0:T(8,128)(2,1)}, bf16[2,1248,384]{2,1,0:T(8,128)(2,1)}, bf16[2,1248,1152]{2,1,0:T(8,128)(2,1)}, f32[2,6,8,208]{3,2,1,...) custom-call(s32[6]{0:T(128)} %refs_0_.7, ...), custom_call_target="tpu_custom_call" | custom-call | tf_op jit(solution)/shard_map/encoder_forward/pallas_call | solution.py:182
  35.2 17.1 %mlp_backward.2 = (f32[1248,384]{1,0:T(8,128)}, f32[16,96,384]{2,1,0:T(8,128)}, f32[16,96,384]{2,1,0:T(8,128)}, f32[16,384]{1,0:T(8,128)}) custom-call(s32[6]{0:T(128)} %refs_0_.7, s32[2]{0:T(128)} %broadcast_select_fusion.refs_1_.me, bf16[6,197,384]{2,1,0:T(8,128)(2,1)} %refs_2_.1, bf16[2,1248,384]{2,1,0:T(8,128)(2,1)} %get-tuple-element.79.refs_3_, ...), custom_call_target="tpu_custom_call" | custom-call | flops 5888802816 | bytes 14376960 | tf_op jit(solution)/shard_map/mlp_backward/pallas_call | solution.py:364
  52.8 4.4 %collective-permute-done.refs_1_.refs_3_ = f32[16,96,384]{2,1,0:T(8,128)S(1)} collective-permute-done((f32[16,96,384]{2,1,0:T(8,128)}, f32[16,96,384]{2,1,0:T(8,128)S(1)}, u32[]{:S(2)}, u32[]{:S(2)}) %collective-permute-start) | collective-permute-done | bytes 2359328 | tf_op jit(solution)/shard_map/ppermute | solution.py:559
  57.2 2.5 copy-done.1
  59.7 1.6 combine.11.refs_13_
  61.3 2.9 %collective-permute-start.1 = (f32[8,96,384]{2,1,0:T(8,128)}, f32[8,96,384]{2,1,0:T(8,128)S(1)}, u32[]{:S(2)}, u32[]{:S(2)}) collective-permute-start(f32[8,96,384]{2,1,0:T(8,128)} %combine.11.refs_13_), channel_id=1, source_target_pairs={{0,8},{4,20},{8,0},{12,28},{16,24},{20,4},{24,16},{28,12},{1,9},{5... | collective-permute-start | bytes 3538952 | tf_op jit(solution)/shard_map/ppermute | solution.py:658
  64.3 23.7 %attention_backward.2 = (f32[1248,384]{1,0:T(8,128)}, f32[16,96,384]{2,1,0:T(8,128)}, f32[16,96,384]{2,1,0:T(8,128)}, f32[16,384]{1,0:T(8,128)}) custom-call(s32[6]{0:T(128)} %refs_0_.7, s32[2]{0:T(128)} %broadcast_select_fusion.refs_1_.me, f32[1248,384]{1,0:T(8,128)} %get-tuple-element.84.refs_2_, bf16[2,1248,384]{2,1,0:T(8,128)(2,1)} %get-tuple-element.85.refs_3_, ...), custom_call_target="tpu_custom_call" | custom-call | flops 5888802816 | bytes 14376960 | tf_op jit(solution)/shard_map/attention_backward/pallas_call | solution.py:542
  88.0 1.7 copy-done.5
  89.6 1.3 combine.12
  91.0 1.6 collective-permute-start.3
  92.6 13.2 %mlp_backward.3 = (f32[1248,384]{1,0:T(8,128)}, f32[16,48,384]{2,1,0:T(8,128)}, f32[16,48,384]{2,1,0:T(8,128)}, f32[16,384]{1,0:T(8,128)}) custom-call(s32[6]{0:T(128)} %refs_0_.7, s32[2]{0:T(128)} %broadcast_select_fusion.refs_1_.me, f32[1248,384]{1,0:T(8,128)} %get-tuple-element.93.refs_2_, bf16[2,1248,384]{2,1,0:T(8,128)(2,1)} %get-tuple-element.79.refs_3_, ...), custom_call_target="tpu_custom_call" | custom-call | flops 5888802816 | bytes 14376960 | tf_op jit(solution)/shard_map/mlp_backward/pallas_call | solution.py:364
  105.8 1.7 copy-done.3
  107.5 1.7 copy-done.6
  109.1 2.9 combine.13
  113.3 1.6 collective-permute-start.6
  114.9 2.6 collective-permute-start.7
  117.7 20.2 %attention_backward.3 = (f32[6,197,384]{2,1,0:T(8,128)}, f32[16,56,384]{2,1,0:T(8,128)}, f32[16,56,384]{2,1,0:T(8,128)}) custom-call(s32[6]{0:T(128)} %refs_0_.7, s32[2]{0:T(128)} %broadcast_select_fusion.refs_1_.me, f32[1248,384]{1,0:T(8,128)} %get-tuple-element.96.refs_2_, bf16[2,1248,384]{2,1,0:T(8,128)(2,1)} %get-tuple-element.85.refs_3_, ...), custom_call_target="tpu_custom_call" | custom-call | flops 5888802816 | bytes 14376960 | tf_op jit(solution)/shard_map/attention_backward/pallas_call | solution.py:542
  138.0 1.3 copy-done.9
  139.3 1.8 combine.14
  141.2 3.1 %collective-permute-done.10.refs_1_.refs_4_.refs_5_ = f32[16,56,384]{2,1,0:T(8,128)S(1)} collective-permute-done((f32[16,56,384]{2,1,0:T(8,128)S(1)}, f32[16,56,384]{2,1,0:T(8,128)S(1)}, u32[]{:S(2)}, u32[]{:S(2)}) %collective-permute-start.10) | collective-permute-done | bytes 1376288 | tf_op jit(solution)/shard_map/ppermute | solution.py:559
  144.9 1.4 collective-permute-start.11
  146.3 0.7 collective-permute-start.12
  147.1 1.5 collective-permute-start.9
  148.6 3.6 %collective-permute-start.15 = (f32[96,384]{1,0:T(8,128)S(1)}, f32[96,384]{1,0:T(8,128)S(1)}, u32[]{:S(2)}, u32[]{:S(2)}) collective-permute-start(f32[96,384]{1,0:T(8,128)S(1)} %get-tuple-element.116.refs_4_), channel_id=1, source_target_pairs={{0,3},{1,2},{2,1},{3,0},{4,7},{5,6},{6,5},{7,4},{8,11},{9,10},{10,... | collective-permute-start | bytes 442376 | tf_op jit(solution)/shard_map/ppermute | solution.py:559
  152.1 5.0 %collective-permute-done.15.refs_7_ = f32[96,384]{1,0:T(8,128)S(1)} collective-permute-done((f32[96,384]{1,0:T(8,128)S(1)}, f32[96,384]{1,0:T(8,128)S(1)}, u32[]{:S(2)}, u32[]{:S(2)}) %collective-permute-start.15) | collective-permute-done | bytes 147488 | tf_op jit(solution)/shard_map/ppermute | solution.py:559
  157.1 5.0 %collective-permute-start.13 = (f32[96,384]{1,0:T(8,128)S(1)}, f32[96,384]{1,0:T(8,128)S(1)}, u32[]{:S(2)}, u32[]{:S(2)}) collective-permute-start(f32[96,384]{1,0:T(8,128)S(1)} %get-tuple-element.116.refs_4_), channel_id=1, source_target_pairs={{0,1},{1,0},{2,3},{3,2},{4,5},{5,4},{6,7},{7,6},{8,9},{9,8},{10,11... | collective-permute-start | bytes 442376 | tf_op jit(solution)/shard_map/ppermute | solution.py:559
  162.1 1.1 collective-permute-done.14.refs_6_
  163.2 2.0 collective-permute-done.13.refs_5_
  165.2 1.6 combine.16
  166.8 1.8 collective-permute-done.9.refs_2_
  168.6 1.2 combine.17
  169.7 1.0 collective-permute-start.17
  170.7 1.1 collective-permute-start.16
  171.8 0.7 collective-permute-start.18
  172.5 3.4 %collective-permute-start.19 = (f32[96,384]{1,0:T(8,128)S(1)}, f32[96,384]{1,0:T(8,128)S(1)}, u32[]{:S(2)}, u32[]{:S(2)}) collective-permute-start(f32[96,384]{1,0:T(8,128)S(1)} %get-tuple-element.121), channel_id=1, source_target_pairs={{0,2},{1,3},{2,0},{3,1},{4,6},{5,7},{6,4},{7,5},{8,10},{9,11},{10,... | collective-permute-start | bytes 442376 | tf_op jit(solution)/shard_map/ppermute | solution.py:559
  176.2 2.5 collective-permute-done.18.refs_9_
  178.7 7.6 %collective-permute-done.19.refs_10_ = f32[96,384]{1,0:T(8,128)S(1)} collective-permute-done((f32[96,384]{1,0:T(8,128)S(1)}, f32[96,384]{1,0:T(8,128)S(1)}, u32[]{:S(2)}, u32[]{:S(2)}) %collective-permute-start.19) | collective-permute-done | bytes 147488 | tf_op jit(solution)/shard_map/ppermute | solution.py:559
  186.3 1.7 combine.18
  188.0 2.2 collective-permute-start.21
  190.2 1.0 collective-permute-start.22
  191.3 1.4 collective-permute-start.23
  192.7 2.4 collective-permute-start.29
  195.2 2.1 collective-permute-start.27
  197.3 12.7 %collective-permute-done.22.refs_2_ = f32[104,384]{1,0:T(8,128)S(1)} collective-permute-done((f32[104,384]{1,0:T(8,128)S(1)}, f32[104,384]{1,0:T(8,128)S(1)}, u32[]{:S(2)}, u32[]{:S(2)}) %collective-permute-start.22) | collective-permute-done | bytes 159776 | tf_op jit(solution)/shard_map/ppermute | solution.py:559
  209.9 0.9 combine.19.refs_5_.refs_0_
  210.8 7.2 %collective-permute-done.28.refs_2_ = f32[96,384]{1,0:T(8,128)S(1)} collective-permute-done((f32[96,384]{1,0:T(8,128)S(1)}, f32[96,384]{1,0:T(8,128)S(1)}, u32[]{:S(2)}, u32[]{:S(2)}) %collective-permute-start.28) | collective-permute-done | bytes 147488 | tf_op jit(solution)/shard_map/ppermute | solution.py:559
  218.0 1.0 combine.20.refs_4_.refs_0_
  219.0 2.0 collective-permute-start.37
  221.2 2.4 collective-permute-start.26
  223.6 2.0 collective-permute-start.24
  225.6 4.5 %collective-permute-done.26.refs_3_ = f32[104,384]{1,0:T(8,128)S(1)} collective-permute-done((f32[104,384]{1,0:T(8,128)S(1)}, f32[104,384]{1,0:T(8,128)S(1)}, u32[]{:S(2)}, u32[]{:S(2)}) %collective-permute-start.26) | collective-permute-done | bytes 159776 | tf_op jit(solution)/shard_map/ppermute | solution.py:559
  230.0 5.3 %collective-permute-done.25.refs_2_ = f32[104,384]{1,0:T(8,128)S(1)} collective-permute-done((f32[104,384]{1,0:T(8,128)S(1)}, f32[104,384]{1,0:T(8,128)S(1)}, u32[]{:S(2)}, u32[]{:S(2)}) %collective-permute-start.25) | collective-permute-done | bytes 159776 | tf_op jit(solution)/shard_map/ppermute | solution.py:559
  235.3 0.9 combine.21.refs_8_.refs_0_
  236.2 1.7 collective-permute-start.31
  238.0 10.0 %collective-permute-done.37.refs_1_ = f32[4,192,384]{2,1,0:T(8,128)S(1)} collective-permute-done((f32[4,192,384]{2,1,0:T(8,128)S(1)}, f32[4,192,384]{2,1,0:T(8,128)S(1)}, u32[]{:S(2)}, u32[]{:S(2)}) %collective-permute-start.37) | collective-permute-done | bytes 1179680 | tf_op jit(solution)/shard_map/ppermute | solution.py:658
  248.0 1.9 collective-permute-start.39
  250.6 7.4 %collective-permute-done.31.refs_2_ = f32[4,104,384]{2,1,0:T(8,128)S(1)} collective-permute-done((f32[4,104,384]{2,1,0:T(8,128)S(1)}, f32[4,104,384]{2,1,0:T(8,128)S(1)}, u32[]{:S(2)}, u32[]{:S(2)}) %collective-permute-start.31) | collective-permute-done | bytes 639008 | tf_op jit(solution)/shard_map/ppermute | solution.py:658
  258.0 9.1 %collective-permute-done.30.refs_1_ = f32[4,104,384]{2,1,0:T(8,128)S(1)} collective-permute-done((f32[4,104,384]{2,1,0:T(8,128)S(1)}, f32[4,104,384]{2,1,0:T(8,128)S(1)}, u32[]{:S(2)}, u32[]{:S(2)}) %collective-permute-start.30) | collective-permute-done | bytes 639008 | tf_op jit(solution)/shard_map/ppermute | solution.py:658
  267.3 4.1 %collective-permute-done.39.refs_3_ = f32[4,192,384]{2,1,0:T(8,128)S(1)} collective-permute-done((f32[4,192,384]{2,1,0:T(8,128)S(1)}, f32[4,192,384]{2,1,0:T(8,128)S(1)}, u32[]{:S(2)}, u32[]{:S(2)}) %collective-permute-start.39) | collective-permute-done | bytes 1179680 | tf_op jit(solution)/shard_map/ppermute | solution.py:658
  271.4 1.6 collective-permute-start.43
  273.0 5.3 %collective-permute-done.32.refs_3_ = f32[4,104,384]{2,1,0:T(8,128)S(1)} collective-permute-done((f32[4,104,384]{2,1,0:T(8,128)S(1)}, f32[4,104,384]{2,1,0:T(8,128)S(1)}, u32[]{:S(2)}, u32[]{:S(2)}) %collective-permute-start.32) | collective-permute-done | bytes 639008 | tf_op jit(solution)/shard_map/ppermute | solution.py:658
  278.3 1.3 collective-permute-start.34
  280.1 5.3 %place.2 = (f32[2,384,1536]{2,1,0:T(8,128)}, f32[2,1536,384]{2,1,0:T(8,128)}, f32[2,384,384]{2,1,0:T(8,128)}, f32[2,384,1152]{2,1,0:T(8,128)}) custom-call(s32[2]{0:T(128)S(1)} %copy-done.12, f32[4,192,384]{2,1,0:T(8,128)S(1)} %combine.20.refs_4_.refs_0_, f32[4,192,384]{2,1,0:T(8,128)S(1)} %collective-permute-done.37.refs_1_, ...), custom_call_target="tpu_custom_call" | custom-call | tf_op jit(solution)/shard_map/place/pallas_call | solution.py:801
  285.4 5.1 %place.3 = (f32[2,384,1536]{2,1,0:T(8,128)}, f32[2,384,384]{2,1,0:T(8,128)}, f32[2,384,1152]{2,1,0:T(8,128)}, f32[197,384]{1,0:T(8,128)}, f32[2,2,384]{2,1,0:T(2...) custom-call(s32[2]{0:T(128)S(1)} %copy-done.12, ...), custom_call_target="tpu_custom_call", output_to_operand_aliasing={{0}: (9, {}), {1}: (10, {}), {2}: (11, {})} | custom-call | tf_op jit(solution)/shard_map/place/pallas_call | solution.py:801
  (69 shorter events, 5.5 us)
Async XLA Ops:
  52.3 4.9 %collective-permute-start = (f32[16,96,384]{2,1,0:T(8,128)}, f32[16,96,384]{2,1,0:T(8,128)S(1)}, u32[]{:S(2)}, u32[]{:S(2)}) collective-permute-start(f32[16,96,384]{2,1,0:T(8,128)} %get-tuple-element.92), channel_id=1, source_target_pairs={{0,4},{4,0},{8,12},{12,8},{16,20},{20,16},{24,28},{28,24},{1,5},{5... | collective-permute-start | bytes 7077896 | tf_op jit(solution)/shard_map/ppermute | solution.py:559
  57.2 4.2 %copy-start.4 = (f32[16,96,384]{2,1,0:T(8,128)}, f32[16,96,384]{2,1,0:T(8,128)S(1)}, u32[]{:S(2)}) copy-start(f32[16,96,384]{2,1,0:T(8,128)S(1)} %collective-permute-done.refs_1_.refs_3_) | copy-start | bytes 7077892
  57.2 2.5 copy-start.1
  61.3 26.6 %collective-permute-start.1 = (f32[8,96,384]{2,1,0:T(8,128)}, f32[8,96,384]{2,1,0:T(8,128)S(1)}, u32[]{:S(2)}, u32[]{:S(2)}) collective-permute-start(f32[8,96,384]{2,1,0:T(8,128)} %combine.11.refs_13_), channel_id=1, source_target_pairs={{0,8},{4,20},{8,0},{12,28},{16,24},{20,4},{24,16},{28,12},{1,9},{5... | collective-permute-start | bytes 3538952 | tf_op jit(solution)/shard_map/ppermute | solution.py:658
  64.3 23.7 %copy-start.2 = (f32[16,96,384]{2,1,0:T(8,128)S(1)}, f32[16,96,384]{2,1,0:T(8,128)}, u32[]{:S(2)}) copy-start(f32[16,96,384]{2,1,0:T(8,128)} %get-tuple-element.91.refs_0_.refs_2_) | copy-start | bytes 7077892
  88.0 1.7 copy-start.5
  90.9 14.8 %collective-permute-start.2 = (f32[16,96,384]{2,1,0:T(8,128)}, f32[16,96,384]{2,1,0:T(8,128)}, u32[]{:S(2)}, u32[]{:S(2)}) collective-permute-start(f32[16,96,384]{2,1,0:T(8,128)} %get-tuple-element.101), channel_id=1, source_target_pairs={{0,4},{4,0},{8,12},{12,8},{16,20},{20,16},{24,28},{28,24},{1,5},{5... | collective-permute-start | bytes 7077896 | tf_op jit(solution)/shard_map/ppermute | solution.py:559
  91.0 14.8 %collective-permute-start.3 = (f32[4,96,384]{2,1,0:T(8,128)}, f32[4,96,384]{2,1,0:T(8,128)S(1)}, u32[]{:S(2)}, u32[]{:S(2)}) collective-permute-start(f32[4,96,384]{2,1,0:T(8,128)} %get-tuple-element.95.refs_11_), channel_id=1, source_target_pairs={{0,16},{4,12},{8,24},{12,4},{16,0},{20,28},{24,8},{28,20},{1,17},{... | collective-permute-start | bytes 1769480 | tf_op jit(solution)/shard_map/ppermute | solution.py:658
  92.6 13.2 %copy-start = (f32[16,96,384]{2,1,0:T(8,128)S(1)}, f32[16,96,384]{2,1,0:T(8,128)}, u32[]{:S(2)}) copy-start(f32[16,96,384]{2,1,0:T(8,128)} %get-tuple-element.100.refs_0_) | copy-start | bytes 7077892
  105.8 1.7 copy-start.3
  107.5 1.7 copy-start.6
  112.0 0.7 copy-start.10
  112.7 25.3 %collective-permute-start.4 = (f32[16,48,384]{2,1,0:T(8,128)}, f32[16,48,384]{2,1,0:T(8,128)}, u32[]{:S(2)}, u32[]{:S(2)}) collective-permute-start(f32[16,48,384]{2,1,0:T(8,128)} %get-tuple-element.106), channel_id=1, source_target_pairs={{0,4},{4,0},{8,12},{12,8},{16,20},{20,16},{24,28},{28,24},{1,5},{5... | collective-permute-start | bytes 3538952 | tf_op jit(solution)/shard_map/ppermute | solution.py:559
  112.7 25.3 %collective-permute-start.5 = (f32[8,96,384]{2,1,0:T(8,128)}, f32[8,96,384]{2,1,0:T(8,128)}, u32[]{:S(2)}, u32[]{:S(2)}) collective-permute-start(f32[8,96,384]{2,1,0:T(8,128)} %get-tuple-element.103.refs_16_), channel_id=1, source_target_pairs={{0,8},{4,20},{8,0},{12,28},{16,24},{20,4},{24,16},{28,12},{1,9},{5... | collective-permute-start | bytes 3538952 | tf_op jit(solution)/shard_map/ppermute | solution.py:658
  113.3 24.6 %collective-permute-start.6 = (f32[96,384]{1,0:T(8,128)}, f32[96,384]{1,0:T(8,128)S(1)}, u32[]{:S(2)}, u32[]{:S(2)}) collective-permute-start(f32[96,384]{1,0:T(8,128)} %get-tuple-element.108), channel_id=1, source_target_pairs={{0,1},{1,0},{2,3},{3,2},{4,5},{5,4},{6,7},{7,6},{8,9},{9,8},{10,11... | collective-permute-start | bytes 442376 | tf_op jit(solution)/shard_map/ppermute | solution.py:559
  114.9 23.0 %collective-permute-start.7 = (f32[96,384]{1,0:T(8,128)}, f32[96,384]{1,0:T(8,128)S(1)}, u32[]{:S(2)}, u32[]{:S(2)}) collective-permute-start(f32[96,384]{1,0:T(8,128)} %get-tuple-element.109), channel_id=1, source_target_pairs={{0,2},{1,3},{2,0},{3,1},{4,6},{5,7},{6,4},{7,5},{8,10},{9,11},{10,... | collective-permute-start | bytes 442376 | tf_op jit(solution)/shard_map/ppermute | solution.py:559
  117.5 20.4 %collective-permute-start.8 = (f32[96,384]{1,0:T(8,128)}, f32[96,384]{1,0:T(8,128)S(1)}, u32[]{:S(2)}, u32[]{:S(2)}) collective-permute-start(f32[96,384]{1,0:T(8,128)} %get-tuple-element.110), channel_id=1, source_target_pairs={{0,3},{1,2},{2,1},{3,0},{4,7},{5,6},{6,5},{7,4},{8,11},{9,10},{10,... | collective-permute-start | bytes 442376 | tf_op jit(solution)/shard_map/ppermute | solution.py:559
  117.7 20.2 %copy-start.8 = (f32[16,48,384]{2,1,0:T(8,128)S(1)}, f32[16,48,384]{2,1,0:T(8,128)}, u32[]{:S(2)}) copy-start(f32[16,48,384]{2,1,0:T(8,128)} %get-tuple-element.105.refs_3_.refs_0_) | copy-start | bytes 3538948
  117.7 20.2 %copy-start.11 = (f32[96,384]{1,0:T(8,128)S(1)}, f32[96,384]{1,0:T(8,128)}, u32[]{:S(2)}) copy-start(f32[96,384]{1,0:T(8,128)} %copy-done.10) | copy-start | bytes 442372
  138.0 1.3 copy-start.9
  139.3 5.0 %copy-start.7 = (f32[16,56,384]{2,1,0:T(8,128)S(1)}, f32[16,56,384]{2,1,0:T(8,128)}, u32[]{:S(2)}) copy-start(f32[16,56,384]{2,1,0:T(8,128)} %get-tuple-element.113.refs_0_.refs_3_.refs_4_) | copy-start | bytes 4128772
  141.1 3.2 %collective-permute-start.10 = (f32[16,56,384]{2,1,0:T(8,128)S(1)}, f32[16,56,384]{2,1,0:T(8,128)S(1)}, u32[]{:S(2)}, u32[]{:S(2)}) collective-permute-start(f32[16,56,384]{2,1,0:T(8,128)S(1)} %get-tuple-element.114), channel_id=1, source_target_pairs={{0,4},{4,0},{8,12},{12,8},{16,20},{20,16},{24,28},{28,24},{1,5},{5... | collective-permute-start | bytes 4128776 | tf_op jit(solution)/shard_map/ppermute | solution.py:559
  144.9 23.6 %collective-permute-start.11 = (f32[8,56,384]{2,1,0:T(8,128)S(1)}, f32[8,56,384]{2,1,0:T(8,128)S(1)}, u32[]{:S(2)}, u32[]{:S(2)}) collective-permute-start(f32[8,56,384]{2,1,0:T(8,128)S(1)} %combine.15.refs_8_), channel_id=1, source_target_pairs={{0,8},{4,20},{8,0},{12,28},{16,24},{20,4},{24,16},{28,12},{1,9},{5... | collective-permute-start | bytes 2064392 | tf_op jit(solution)/shard_map/ppermute | solution.py:658
  146.3 18.9 %collective-permute-start.12 = (f32[4,96,384]{2,1,0:T(8,128)S(1)}, f32[4,96,384]{2,1,0:T(8,128)S(1)}, u32[]{:S(2)}, u32[]{:S(2)}) collective-permute-start(f32[4,96,384]{2,1,0:T(8,128)S(1)} %get-tuple-element.115.refs_2_), channel_id=1, source_target_pairs={{0,16},{4,12},{8,24},{12,4},{16,0},{20,28},{24,8},{28,20},{1,17},{... | collective-permute-start | bytes 1769480 | tf_op jit(solution)/shard_map/ppermute | solution.py:658
  147.1 21.5 %collective-permute-start.9 = (f32[8,48,384]{2,1,0:T(8,128)S(1)}, f32[8,48,384]{2,1,0:T(8,128)S(1)}, u32[]{:S(2)}, u32[]{:S(2)}) collective-permute-start(f32[8,48,384]{2,1,0:T(8,128)S(1)} %get-tuple-element.112), channel_id=1, source_target_pairs={{0,8},{4,20},{8,0},{12,28},{16,24},{20,4},{24,16},{28,12},{1,9},{5... | collective-permute-start | bytes 1769480 | tf_op jit(solution)/shard_map/ppermute | solution.py:658
  148.6 8.5 %collective-permute-start.15 = (f32[96,384]{1,0:T(8,128)S(1)}, f32[96,384]{1,0:T(8,128)S(1)}, u32[]{:S(2)}, u32[]{:S(2)}) collective-permute-start(f32[96,384]{1,0:T(8,128)S(1)} %get-tuple-element.116.refs_4_), channel_id=1, source_target_pairs={{0,3},{1,2},{2,1},{3,0},{4,7},{5,6},{6,5},{7,4},{8,11},{9,10},{10,... | collective-permute-start | bytes 442376 | tf_op jit(solution)/shard_map/ppermute | solution.py:559
  152.1 11.1 %collective-permute-start.14 = (f32[96,384]{1,0:T(8,128)S(1)}, f32[96,384]{1,0:T(8,128)S(1)}, u32[]{:S(2)}, u32[]{:S(2)}) collective-permute-start(f32[96,384]{1,0:T(8,128)S(1)} %get-tuple-element.116.refs_4_), channel_id=1, source_target_pairs={{0,2},{1,3},{2,0},{3,1},{4,6},{5,7},{6,4},{7,5},{8,10},{9,11},{10,... | collective-permute-start | bytes 442376 | tf_op jit(solution)/shard_map/ppermute | solution.py:559
  157.1 8.1 %collective-permute-start.13 = (f32[96,384]{1,0:T(8,128)S(1)}, f32[96,384]{1,0:T(8,128)S(1)}, u32[]{:S(2)}, u32[]{:S(2)}) collective-permute-start(f32[96,384]{1,0:T(8,128)S(1)} %get-tuple-element.116.refs_4_), channel_id=1, source_target_pairs={{0,1},{1,0},{2,3},{3,2},{4,5},{5,4},{6,7},{7,6},{8,9},{9,8},{10,11... | collective-permute-start | bytes 442376 | tf_op jit(solution)/shard_map/ppermute | solution.py:559
  169.7 16.6 %collective-permute-start.17 = (f32[4,56,384]{2,1,0:T(8,128)S(1)}, f32[4,56,384]{2,1,0:T(8,128)S(1)}, u32[]{:S(2)}, u32[]{:S(2)}) collective-permute-start(f32[4,56,384]{2,1,0:T(8,128)S(1)} %get-tuple-element.119), channel_id=1, source_target_pairs={{0,16},{4,12},{8,24},{12,4},{16,0},{20,28},{24,8},{28,20},{1,17},{... | collective-permute-start | bytes 1032200 | tf_op jit(solution)/shard_map/ppermute | solution.py:658
  170.7 15.6 %collective-permute-start.16 = (f32[4,48,384]{2,1,0:T(8,128)S(1)}, f32[4,48,384]{2,1,0:T(8,128)S(1)}, u32[]{:S(2)}, u32[]{:S(2)}) collective-permute-start(f32[4,48,384]{2,1,0:T(8,128)S(1)} %get-tuple-element.118.refs_12_), channel_id=1, source_target_pairs={{0,16},{4,12},{8,24},{12,4},{16,0},{20,28},{24,8},{28,20},{1,17},{... | collective-permute-start | bytes 884744 | tf_op jit(solution)/shard_map/ppermute | solution.py:658
  171.8 6.8 %collective-permute-start.18 = (f32[96,384]{1,0:T(8,128)S(1)}, f32[96,384]{1,0:T(8,128)S(1)}, u32[]{:S(2)}, u32[]{:S(2)}) collective-permute-start(f32[96,384]{1,0:T(8,128)S(1)} %get-tuple-element.120), channel_id=1, source_target_pairs={{0,1},{1,0},{2,3},{3,2},{4,5},{5,4},{6,7},{7,6},{8,9},{9,8},{10,11... | collective-permute-start | bytes 442376 | tf_op jit(solution)/shard_map/ppermute | solution.py:559
  172.5 13.8 %collective-permute-start.19 = (f32[96,384]{1,0:T(8,128)S(1)}, f32[96,384]{1,0:T(8,128)S(1)}, u32[]{:S(2)}, u32[]{:S(2)}) collective-permute-start(f32[96,384]{1,0:T(8,128)S(1)} %get-tuple-element.121), channel_id=1, source_target_pairs={{0,2},{1,3},{2,0},{3,1},{4,6},{5,7},{6,4},{7,5},{8,10},{9,11},{10,... | collective-permute-start | bytes 442376 | tf_op jit(solution)/shard_map/ppermute | solution.py:559
  176.0 10.4 %collective-permute-start.20 = (f32[96,384]{1,0:T(8,128)S(1)}, f32[96,384]{1,0:T(8,128)S(1)}, u32[]{:S(2)}, u32[]{:S(2)}) collective-permute-start(f32[96,384]{1,0:T(8,128)S(1)} %get-tuple-element.122), channel_id=1, source_target_pairs={{0,3},{1,2},{2,1},{3,0},{4,7},{5,6},{6,5},{7,4},{8,11},{9,10},{10,... | collective-permute-start | bytes 442376 | tf_op jit(solution)/shard_map/ppermute | solution.py:559
  188.0 7.2 %collective-permute-start.21 = (f32[104,384]{1,0:T(8,128)S(1)}, f32[104,384]{1,0:T(8,128)S(1)}, u32[]{:S(2)}, u32[]{:S(2)}) collective-permute-start(f32[104,384]{1,0:T(8,128)S(1)} %get-tuple-element.124), channel_id=1, source_target_pairs={{0,1},{1,0},{2,3},{3,2},{4,5},{5,4},{6,7},{7,6},{8,9},{9,8},{10,11... | collective-permute-start | bytes 479240 | tf_op jit(solution)/shard_map/ppermute | solution.py:559
  190.2 19.7 %collective-permute-start.22 = (f32[104,384]{1,0:T(8,128)S(1)}, f32[104,384]{1,0:T(8,128)S(1)}, u32[]{:S(2)}, u32[]{:S(2)}) collective-permute-start(f32[104,384]{1,0:T(8,128)S(1)} %get-tuple-element.125), channel_id=1, source_target_pairs={{0,2},{1,3},{2,0},{3,1},{4,6},{5,7},{6,4},{7,5},{8,10},{9,11},{10,... | collective-permute-start | bytes 479240 | tf_op jit(solution)/shard_map/ppermute | solution.py:559
  191.3 18.7 %collective-permute-start.23 = (f32[104,384]{1,0:T(8,128)S(1)}, f32[104,384]{1,0:T(8,128)S(1)}, u32[]{:S(2)}, u32[]{:S(2)}) collective-permute-start(f32[104,384]{1,0:T(8,128)S(1)} %get-tuple-element.126), channel_id=1, source_target_pairs={{0,3},{1,2},{2,1},{3,0},{4,7},{5,6},{6,5},{7,4},{8,11},{9,10},{10,... | collective-permute-start | bytes 479240 | tf_op jit(solution)/shard_map/ppermute | solution.py:559
  192.7 18.1 %collective-permute-start.29 = (f32[96,384]{1,0:T(8,128)S(1)}, f32[96,384]{1,0:T(8,128)S(1)}, u32[]{:S(2)}, u32[]{:S(2)}) collective-permute-start(f32[96,384]{1,0:T(8,128)S(1)} %get-tuple-element.127.refs_0_), channel_id=1, source_target_pairs={{0,3},{1,2},{2,1},{3,0},{4,7},{5,6},{6,5},{7,4},{8,11},{9,10},{10,... | collective-permute-start | bytes 442376 | tf_op jit(solution)/shard_map/ppermute | solution.py:559
  195.1 22.9 %collective-permute-start.28 = (f32[96,384]{1,0:T(8,128)S(1)}, f32[96,384]{1,0:T(8,128)S(1)}, u32[]{:S(2)}, u32[]{:S(2)}) collective-permute-start(f32[96,384]{1,0:T(8,128)S(1)} %get-tuple-element.127.refs_0_), channel_id=1, source_target_pairs={{0,2},{1,3},{2,0},{3,1},{4,6},{5,7},{6,4},{7,5},{8,10},{9,11},{10,... | collective-permute-start | bytes 442376 | tf_op jit(solution)/shard_map/ppermute | solution.py:559
  195.2 22.8 %collective-permute-start.27 = (f32[96,384]{1,0:T(8,128)S(1)}, f32[96,384]{1,0:T(8,128)S(1)}, u32[]{:S(2)}, u32[]{:S(2)}) collective-permute-start(f32[96,384]{1,0:T(8,128)S(1)} %get-tuple-element.127.refs_0_), channel_id=1, source_target_pairs={{0,1},{1,0},{2,3},{3,2},{4,5},{5,4},{6,7},{7,6},{8,9},{9,8},{10,11... | collective-permute-start | bytes 442376 | tf_op jit(solution)/shard_map/ppermute | solution.py:559
  219.0 61.1 %copy-start.12 = (s32[2]{0:T(128)S(1)}, s32[2]{0:T(128)}, u32[]{:S(2)}) copy-start(s32[2]{0:T(128)} %broadcast_select_fusion.refs_1_.me) | copy-start | bytes 28
  219.0 29.0 %collective-permute-start.37 = (f32[4,192,384]{2,1,0:T(8,128)S(1)}, f32[4,192,384]{2,1,0:T(8,128)S(1)}, u32[]{:S(2)}, u32[]{:S(2)}) collective-permute-start(f32[4,192,384]{2,1,0:T(8,128)S(1)} %combine.20.refs_4_.refs_0_), channel_id=1, source_target_pairs={{0,16},{4,12},{8,24},{12,4},{16,0},{20,28},{24,8},{28,20},{1,17},{... | collective-permute-start | bytes 3538952 | tf_op jit(solution)/shard_map/ppermute | solution.py:658
  221.0 29.1 %collective-permute-start.38 = (f32[4,192,384]{2,1,0:T(8,128)S(1)}, f32[4,192,384]{2,1,0:T(8,128)S(1)}, u32[]{:S(2)}, u32[]{:S(2)}) collective-permute-start(f32[4,192,384]{2,1,0:T(8,128)S(1)} %combine.20.refs_4_.refs_0_), channel_id=1, source_target_pairs={{0,8},{4,20},{8,0},{12,28},{16,24},{20,4},{24,16},{28,12},{1,9},{5... | collective-permute-start | bytes 3538952 | tf_op jit(solution)/shard_map/ppermute | solution.py:658
  221.2 8.8 %collective-permute-start.26 = (f32[104,384]{1,0:T(8,128)S(1)}, f32[104,384]{1,0:T(8,128)S(1)}, u32[]{:S(2)}, u32[]{:S(2)}) collective-permute-start(f32[104,384]{1,0:T(8,128)S(1)} %combine.19.refs_5_.refs_0_), channel_id=1, source_target_pairs={{0,3},{1,2},{2,1},{3,0},{4,7},{5,6},{6,5},{7,4},{8,11},{9,10},{10,... | collective-permute-start | bytes 479240 | tf_op jit(solution)/shard_map/ppermute | solution.py:559
  223.6 11.8 %collective-permute-start.25 = (f32[104,384]{1,0:T(8,128)S(1)}, f32[104,384]{1,0:T(8,128)S(1)}, u32[]{:S(2)}, u32[]{:S(2)}) collective-permute-start(f32[104,384]{1,0:T(8,128)S(1)} %combine.19.refs_5_.refs_0_), channel_id=1, source_target_pairs={{0,2},{1,3},{2,0},{3,1},{4,6},{5,7},{6,4},{7,5},{8,10},{9,11},{10,... | collective-permute-start | bytes 479240 | tf_op jit(solution)/shard_map/ppermute | solution.py:559
  223.6 11.8 %collective-permute-start.24 = (f32[104,384]{1,0:T(8,128)S(1)}, f32[104,384]{1,0:T(8,128)S(1)}, u32[]{:S(2)}, u32[]{:S(2)}) collective-permute-start(f32[104,384]{1,0:T(8,128)S(1)} %combine.19.refs_5_.refs_0_), channel_id=1, source_target_pairs={{0,1},{1,0},{2,3},{3,2},{4,5},{5,4},{6,7},{7,6},{8,9},{9,8},{10,11... | collective-permute-start | bytes 479240 | tf_op jit(solution)/shard_map/ppermute | solution.py:559
  236.2 21.8 %collective-permute-start.31 = (f32[4,104,384]{2,1,0:T(8,128)S(1)}, f32[4,104,384]{2,1,0:T(8,128)S(1)}, u32[]{:S(2)}, u32[]{:S(2)}) collective-permute-start(f32[4,104,384]{2,1,0:T(8,128)S(1)} %combine.21.refs_8_.refs_0_), channel_id=1, source_target_pairs={{0,8},{4,20},{8,0},{12,28},{16,24},{20,4},{24,16},{28,12},{1,9},{5... | collective-permute-start | bytes 1916936 | tf_op jit(solution)/shard_map/ppermute | solution.py:658
  248.0 23.5 %collective-permute-start.39 = (f32[4,192,384]{2,1,0:T(8,128)S(1)}, f32[4,192,384]{2,1,0:T(8,128)S(1)}, u32[]{:S(2)}, u32[]{:S(2)}) collective-permute-start(f32[4,192,384]{2,1,0:T(8,128)S(1)} %collective-permute-done.37.refs_1_), channel_id=1, source_target_pairs={{0,8},{4,20},{8,0},{12,28},{16,24},{20,4},{24,16},{28,12},{1,9},{5... | collective-permute-start | bytes 3538952 | tf_op jit(solution)/shard_map/ppermute | solution.py:658
  249.8 17.3 %collective-permute-start.30 = (f32[4,104,384]{2,1,0:T(8,128)S(1)}, f32[4,104,384]{2,1,0:T(8,128)S(1)}, u32[]{:S(2)}, u32[]{:S(2)}) collective-permute-start(f32[4,104,384]{2,1,0:T(8,128)S(1)} %combine.21.refs_8_.refs_0_), channel_id=1, source_target_pairs={{0,16},{4,12},{8,24},{12,4},{16,0},{20,28},{24,8},{28,20},{1,17},{... | collective-permute-start | bytes 1916936 | tf_op jit(solution)/shard_map/ppermute | solution.py:658
  250.1 22.9 %collective-permute-start.40 = (f32[4,192,384]{2,1,0:T(8,128)S(1)}, f32[4,192,384]{2,1,0:T(8,128)S(1)}, u32[]{:S(2)}, u32[]{:S(2)}) collective-permute-start(f32[4,192,384]{2,1,0:T(8,128)S(1)} %combine.20.refs_4_.refs_0_), channel_id=1, source_target_pairs={{0,4},{4,0},{8,12},{12,8},{16,20},{20,16},{24,28},{28,24},{1,5},{5... | collective-permute-start | bytes 3538952 | tf_op jit(solution)/shard_map/ppermute | solution.py:559
  250.1 29.5 %collective-permute-start.42 = (f32[4,192,384]{2,1,0:T(8,128)S(1)}, f32[4,192,384]{2,1,0:T(8,128)S(1)}, u32[]{:S(2)}, u32[]{:S(2)}) collective-permute-start(f32[4,192,384]{2,1,0:T(8,128)S(1)} %collective-permute-done.38.refs_2_), channel_id=1, source_target_pairs={{0,4},{4,0},{8,12},{12,8},{16,20},{20,16},{24,28},{28,24},{1,5},{5... | collective-permute-start | bytes 3538952 | tf_op jit(solution)/shard_map/ppermute | solution.py:559
  258.0 21.5 %collective-permute-start.41 = (f32[4,192,384]{2,1,0:T(8,128)S(1)}, f32[4,192,384]{2,1,0:T(8,128)S(1)}, u32[]{:S(2)}, u32[]{:S(2)}) collective-permute-start(f32[4,192,384]{2,1,0:T(8,128)S(1)} %collective-permute-done.37.refs_1_), channel_id=1, source_target_pairs={{0,4},{4,0},{8,12},{12,8},{16,20},{20,16},{24,28},{28,24},{1,5},{5... | collective-permute-start | bytes 3538952 | tf_op jit(solution)/shard_map/ppermute | solution.py:559
  267.1 11.1 %collective-permute-start.32 = (f32[4,104,384]{2,1,0:T(8,128)S(1)}, f32[4,104,384]{2,1,0:T(8,128)S(1)}, u32[]{:S(2)}, u32[]{:S(2)}) collective-permute-start(f32[4,104,384]{2,1,0:T(8,128)S(1)} %collective-permute-done.30.refs_1_), channel_id=1, source_target_pairs={{0,8},{4,20},{8,0},{12,28},{16,24},{20,4},{24,16},{28,12},{1,9},{5... | collective-permute-start | bytes 1916936 | tf_op jit(solution)/shard_map/ppermute | solution.py:658
  271.4 8.6 %collective-permute-start.43 = (f32[4,192,384]{2,1,0:T(8,128)S(1)}, f32[4,192,384]{2,1,0:T(8,128)S(1)}, u32[]{:S(2)}, u32[]{:S(2)}) collective-permute-start(f32[4,192,384]{2,1,0:T(8,128)S(1)} %collective-permute-done.39.refs_3_), channel_id=1, source_target_pairs={{0,4},{4,0},{8,12},{12,8},{16,20},{20,16},{24,28},{28,24},{1,5},{5... | collective-permute-start | bytes 3538952 | tf_op jit(solution)/shard_map/ppermute | solution.py:559
  273.0 12.3 %collective-permute-start.33 = (f32[4,104,384]{2,1,0:T(8,128)S(1)}, f32[4,104,384]{2,1,0:T(8,128)S(1)}, u32[]{:S(2)}, u32[]{:S(2)}) collective-permute-start(f32[4,104,384]{2,1,0:T(8,128)S(1)} %combine.21.refs_8_.refs_0_), channel_id=1, source_target_pairs={{0,4},{4,0},{8,12},{12,8},{16,20},{20,16},{24,28},{28,24},{1,5},{5... | collective-permute-start | bytes 1916936 | tf_op jit(solution)/shard_map/ppermute | solution.py:559
  278.3 7.1 %collective-permute-start.34 = (f32[4,104,384]{2,1,0:T(8,128)S(1)}, f32[4,104,384]{2,1,0:T(8,128)S(1)}, u32[]{:S(2)}, u32[]{:S(2)}) collective-permute-start(f32[4,104,384]{2,1,0:T(8,128)S(1)} %collective-permute-done.30.refs_1_), channel_id=1, source_target_pairs={{0,4},{4,0},{8,12},{12,8},{16,20},{20,16},{24,28},{28,24},{1,5},{5... | collective-permute-start | bytes 1916936 | tf_op jit(solution)/shard_map/ppermute | solution.py:559
  279.6 5.8 %collective-permute-start.35 = (f32[4,104,384]{2,1,0:T(8,128)S(1)}, f32[4,104,384]{2,1,0:T(8,128)S(1)}, u32[]{:S(2)}, u32[]{:S(2)}) collective-permute-start(f32[4,104,384]{2,1,0:T(8,128)S(1)} %collective-permute-done.31.refs_2_), channel_id=1, source_target_pairs={{0,4},{4,0},{8,12},{12,8},{16,20},{20,16},{24,28},{28,24},{1,5},{5... | collective-permute-start | bytes 1916936 | tf_op jit(solution)/shard_map/ppermute | solution.py:559
  279.6 5.8 %collective-permute-start.36 = (f32[4,104,384]{2,1,0:T(8,128)S(1)}, f32[4,104,384]{2,1,0:T(8,128)S(1)}, u32[]{:S(2)}, u32[]{:S(2)}) collective-permute-start(f32[4,104,384]{2,1,0:T(8,128)S(1)} %collective-permute-done.32.refs_3_), channel_id=1, source_target_pairs={{0,4},{4,0},{8,12},{12,8},{16,20},{20,16},{24,28},{28,24},{1,5},{5... | collective-permute-start | bytes 1916936 | tf_op jit(solution)/shard_map/ppermute | solution.py:559
